TPU v7x, 32 devices: a whole 2x2x4 slice. The times are simulated.
32 devices in a mesh: corpus: 8 (over z, y), blk: 4 (over x, core).
Axes of the slice: x: 2, y: 2, z: 4, core: 2. Of those that a mesh axis runs over, the one named last changes fastest.
Arguments:
- queries: bfloat16 [512, 32, 128], P(('corpus', 'blk')), may hold values from -0.0625 to 0.0625
- index: bfloat16 [4096, 128, 128], P('corpus'), may hold values from -6 to 6
- cand_owner: int32 [512, 64, 1], P(('corpus', 'blk')), may hold values from 0 to 7; in each aligned block of 1024 rows (0 to 1023, 1024 to 2047, ..., all dimensions but the last counted through in order) at most 256 rows name the same one
- cand_row: int32 [512, 64], P(('corpus', 'blk')), may hold values from 0 to 511
- neg_row: int32 [32, 24], P(('corpus', 'blk')), may hold values from 0 to 511
- teacher: float32 [512, 64], P(('corpus', 'blk')), may hold values from -16 to 16
Outputs:
- losses: float32 [512], P(('corpus', 'blk'))
- query_grads: float32 [512, 32, 128], P(('corpus', 'blk'))
Inputs may be any that keep to these rules, and one draw needn't show every extreme that they name: `cand_owner`: among the 1024 candidates of one device, no owner shard is named more than 256 times, and some owner shard is named exactly 256 times.
All inputs are finite; a program needn't handle non-finite values.
Results may differ from a plain program's by a relative error of at most 0.007.
Values may be sent and summed in bfloat16 or wider, within the bound.
No kernel may reach another device: no remote copies, remote signals or barrier semaphores. Data moves between devices by JAX's collectives and lax.ppermute only.
A program may use at most 256 MiB of HBM per device.

v0:
```python
import functools
import math

import jax
import jax.numpy as jnp
from jax import lax
from jax.experimental import pallas as pl
from jax.experimental.pallas import tpu as pltpu
from jax.sharding import PartitionSpec as P

inner_temp = 0.1
epsilon = 1e-06
LOG2E = 1.4426950408889634
GROUP = 4
UNITS = 8
NEG_STEP = 8
NEG_CHUNK = 96
MIB = 1024 * 1024
LAST = (((1,), (1,)), ((), ()))


def dot_last(a, b):
    return lax.dot_general(a, b, LAST, preferred_element_type=jnp.float32)


def dot(a, b):
    return jnp.dot(a, b, preferred_element_type=jnp.float32)


def split3(x):
    high = x.astype(jnp.bfloat16)
    rest = x - high.astype(jnp.float32)
    mid = rest.astype(jnp.bfloat16)
    low = (rest - mid.astype(jnp.float32)).astype(jnp.bfloat16)
    return high, mid, low


def rounded_queries(raw):
    wide = raw.astype(jnp.float32)
    radius = jnp.sqrt(jnp.sum(wide * wide, axis=-1, keepdims=True) + epsilon)
    return (wide / radius).astype(jnp.bfloat16)


def norm_kernel(index_ref, out_ref):
    count, tokens, dim = index_ref.shape
    ones = jnp.ones((8, dim), jnp.bfloat16)
    sub = lax.broadcasted_iota(jnp.int32, (8, tokens), 0)

    def body(step, carry):
        squares = jnp.zeros((8, tokens), jnp.float32)
        for k in range(8):
            tile = index_ref[step * 8 + k].astype(jnp.float32)
            tile = tile * tile
            high = tile.astype(jnp.bfloat16)
            low = (tile - high.astype(jnp.float32)).astype(jnp.bfloat16)
            squares = jnp.where(sub == k, dot_last(ones, high) + dot_last(ones, low), squares)
        out_ref[pl.ds(pl.multiple_of(step * 8, 8), 8), :] = lax.rsqrt(squares + epsilon)
        return carry

    lax.fori_loop(0, count // 8, body, 0, unroll=2)


def norms(index):
    count, tokens, dim = index.shape
    return pl.pallas_call(
        norm_kernel,
        in_specs=[pl.BlockSpec(memory_space=pltpu.VMEM)],
        out_specs=pl.BlockSpec(memory_space=pltpu.VMEM),
        out_shape=jax.ShapeDtypeStruct((count, tokens), jnp.float32),
        compiler_params=pltpu.CompilerParams(vmem_limit_bytes=8 * MIB),
        cost_estimate=pl.CostEstimate(
            flops=32 * count * tokens * dim,
            bytes_accessed=2 * count * tokens * dim,
            transcendentals=count * tokens,
        ),
        name="norms",
    )(index)


def prep_kernel(me_ref, meta_ref, rows_ref, target_ref, value_ref, place_ref, result_ref, *, shard, cands):
    count = meta_ref.shape[0]
    code = meta_ref[:, :cands]
    owner = jnp.floor((code + 0.5) * (1.0 / shard))
    row = code - owner * shard
    teacher = meta_ref[:, cands:]
    log_target = teacher - jnp.log(jnp.sum(jnp.exp(teacher), axis=-1, keepdims=True))
    target = jnp.exp(log_target)
    mine = (owner == me_ref[0].astype(jnp.float32)).astype(jnp.float32)
    before = lax.broadcasted_iota(jnp.int32, (cands, cands), 0) < lax.broadcasted_iota(
        jnp.int32, (cands, cands), 1
    )
    place = dot(mine.astype(jnp.bfloat16), before.astype(jnp.float32).astype(jnp.bfloat16))
    wide = value_ref.shape[1]
    pad = jnp.zeros((count, wide - cands), jnp.float32)
    place_ref[...] = jnp.concatenate([jnp.where(mine > 0, place, -1.0), pad - 1.0], axis=1)
    row_high = jnp.floor(row * (1.0 / 16))
    first, second, third = split3(target)
    values = [row_high, row - 16 * row_high, first, second, third]
    for v in range(8):
        value = values[v].astype(jnp.float32) if v < len(values) else jnp.zeros_like(row)
        value_ref[pl.ds(v, count, stride=8), :] = jnp.concatenate([value, pad], axis=1)
    spots = lax.broadcasted_iota(jnp.int32, (wide, wide), 0).astype(jnp.float32)

    def body(step, carry):
        for k in range(8):
            q = step * 8 + k
            hot = jnp.where(place_ref[pl.ds(q, 1), :] == spots, 1.0, 0.0).astype(jnp.bfloat16)
            at = pl.ds(pl.multiple_of(q * 8, 8), 8)
            result_ref[at, :] = dot_last(value_ref[at, :].astype(jnp.bfloat16), hot)
        return carry

    lax.fori_loop(0, count // 8, body, 0)
    result = [result_ref[pl.ds(v, count, stride=8), :] for v in range(5)]
    found = jnp.sum(mine, axis=-1, keepdims=True)
    lane = lax.broadcasted_iota(jnp.int32, (count, wide), 1)
    rows = 16 * result[0] + result[1]
    rows_ref[...] = jnp.where(lane < cands, rows, found).astype(jnp.int32)
    listed = jnp.where(lane.astype(jnp.float32) < found, result[2] + result[3] + result[4], -1.0)
    stacked = jnp.concatenate(split3(listed), axis=0)
    steps = cands // GROUP
    source = lax.broadcasted_iota(jnp.int32, (wide, wide), 0)
    block = lax.broadcasted_iota(jnp.int32, (wide, wide), 1) // (wide // GROUP)
    for t in range(steps):
        pick = jnp.where(source == block + t * GROUP, 1.0, 0.0).astype(jnp.bfloat16)
        spread = dot(stacked, pick)
        target_ref[pl.ds(t, count, stride=steps), :] = (
            spread[:count] + spread[count : 2 * count] + spread[2 * count :]
        )


def prep(me, meta, shard, cands):
    count = meta.shape[0]
    wide = 128
    return pl.pallas_call(
        functools.partial(prep_kernel, shard=shard, cands=cands),
        in_specs=[
            pl.BlockSpec(memory_space=pltpu.SMEM),
            pl.BlockSpec(memory_space=pltpu.VMEM),
        ],
        out_specs=[pl.BlockSpec(memory_space=pltpu.VMEM)] * 2,
        out_shape=[
            jax.ShapeDtypeStruct((count, wide), jnp.int32),
            jax.ShapeDtypeStruct((count * (cands // GROUP), wide), jnp.float32),
        ],
        scratch_shapes=[
            pltpu.VMEM((count * 8, wide), jnp.float32),
            pltpu.VMEM((count, wide), jnp.float32),
            pltpu.VMEM((count * 8, wide), jnp.float32),
        ],
        compiler_params=pltpu.CompilerParams(vmem_limit_bytes=12 * MIB),
        name="prep",
    )(me, meta)


def pair_kernel(source_ref, rows_ref, target_ref, queries_ref, inverse_ref, index_ref, out_ref,
                units_ref, unit_ref, acc_ref, total_ref, left_ref, right_ref, back_ref, *, cands):
    count, tokens, dim = queries_ref.shape
    wide = rows_ref.shape[1]
    per_query = cands // GROUP
    slots = count * per_query
    bits = per_query.bit_length() - 1
    total = jnp.int32(0)
    for q in range(count):
        for t in range(per_query):
            units_ref[total + t] = jnp.int32(q * per_query + t)
        total = total + lax.div(rows_ref[q, cands] + (GROUP - 1), GROUP)
    for t in range(UNITS):
        units_ref[total + t] = jnp.int32(slots)
    steps = lax.div(total + (UNITS - 1), UNITS)

    def entry(number):
        slot = units_ref[number]
        q = jnp.minimum(lax.shift_right_logical(slot, bits), count - 1)
        return slot, q, jnp.bitwise_and(slot, per_query - 1) * GROUP

    for q in range(count):
        unit_ref[q] = rounded_queries(queries_ref[q])
    acc_ref[...] = jnp.zeros_like(acc_ref)
    ones = jnp.ones((8, wide), jnp.bfloat16)

    def forward(step, carry):
        done = []
        for u in range(UNITS):
            slot, q, base = entry(step * UNITS + u)
            rows = [rows_ref[q, base + g] for g in range(GROUP)]
            tiles = jnp.concatenate([index_ref[row] for row in rows], axis=0)
            raw = dot_last(unit_ref[q], tiles)
            expos, backs = [], []
            for g in range(GROUP):
                inverse = inverse_ref[pl.ds(rows[g], 1), :]
                expo = jnp.exp2(raw[:, g * wide : (g + 1) * wide] * (inverse * (LOG2E / inner_temp)))
                expos.append(expo.astype(jnp.bfloat16))
                backs.append(
                    dot((expo * inverse).astype(jnp.bfloat16), tiles[g * wide : (g + 1) * wide]).astype(
                        jnp.bfloat16
                    )
                )
            totals = dot_last(ones, jnp.concatenate(expos, axis=0))
            done.append((slot, totals, jnp.concatenate(backs, axis=0)))
        for u, (slot, totals, back) in enumerate(done):
            total_ref[pl.ds(slot, 1), :] = totals[0:1]
            back_ref[step * UNITS + u] = back
        return carry

    lax.fori_loop(0, steps, forward, 0)

    target = target_ref[...]
    held = target >= 0.0
    totals = jnp.where(held, total_ref[0:slots, :], 1.0)
    target = jnp.where(held, target, 0.0)
    same = lax.broadcasted_iota(jnp.int32, (wide, wide), 0) // tokens == lax.broadcasted_iota(
        jnp.int32, (wide, wide), 1
    ) // tokens
    same = jnp.where(same, 1.0, 0.0).astype(jnp.bfloat16)
    parts = [dot(part, same) for part in split3(jnp.log(totals))]
    score = inner_temp * (parts[0] + parts[1] + parts[2])
    lift = jnp.where(held, jnp.exp(score), 0.0)
    recip = 1.0 / totals
    left_ref[0:slots, :] = lift * recip
    right_ref[0:slots, :] = target * recip
    left_ref[slots:, :] = jnp.zeros_like(left_ref[slots:, :])
    right_ref[slots:, :] = jnp.zeros_like(right_ref[slots:, :])

    def per_source(values):
        rows = jnp.sum(values.reshape(count, per_query, wide), axis=1)
        return jnp.sum(rows, axis=-1, keepdims=True) * (1.0 / tokens)

    lane = lax.broadcasted_iota(jnp.int32, (count, wide), 1)
    sums = jnp.where(lane < wide // 2, per_source(lift), per_source(target * score))
    diagonal = lax.broadcasted_iota(jnp.int32, (tokens, wide), 0) == lax.broadcasted_iota(
        jnp.int32, (tokens, wide), 1
    ) % tokens

    def backward(step, carry):
        done = []
        for u in range(UNITS):
            slot, q, _ = entry(step * UNITS + u)
            left = jnp.where(diagonal, left_ref[pl.ds(slot, 1), :], 0.0)
            right = jnp.where(diagonal, right_ref[pl.ds(slot, 1), :], 0.0)
            both = jnp.concatenate([left, right], axis=0)
            high = both.astype(jnp.bfloat16)
            low = (both - high.astype(jnp.float32)).astype(jnp.bfloat16)
            part = dot(jnp.concatenate([high, low], axis=0), back_ref[step * UNITS + u])
            done.append((q, part[: 2 * tokens] + part[2 * tokens :]))
        for q, part in done:
            acc_ref[q] += part
        return carry

    lax.fori_loop(0, steps, backward, 0)
    for q in range(count):
        out_ref[pl.ds(q * 2 * tokens, 2 * tokens), :] = acc_ref[q].astype(jnp.bfloat16)
    for k, part in enumerate(split3(sums)):
        out_ref[pl.ds(count * 2 * tokens + k * count, count), :] = part


def pairs(source, rows, targets, queries, inverse, index, cands, room):
    count, tokens, dim = queries.shape
    wide = rows.shape[1]
    per_query = cands // GROUP
    slots = count * per_query
    most = (room + (GROUP - 1) * count) // GROUP + UNITS
    height = count * 2 * tokens + 3 * count
    return pl.pallas_call(
        functools.partial(pair_kernel, cands=cands),
        grid_spec=pltpu.PrefetchScalarGridSpec(
            num_scalar_prefetch=1,
            grid=(1,),
            in_specs=[
                pl.BlockSpec((count, wide), lambda i, s: (s[0], 0), memory_space=pltpu.SMEM),
                pl.BlockSpec((slots, wide), lambda i, s: (s[0], 0)),
                pl.BlockSpec(memory_space=pltpu.VMEM),
                pl.BlockSpec(memory_space=pltpu.VMEM),
                pl.BlockSpec(memory_space=pltpu.VMEM),
            ],
            out_specs=pl.BlockSpec((height, dim), lambda i, s: (0, 0)),
            scratch_shapes=[
                pltpu.SMEM((slots + per_query + UNITS,), jnp.int32),
                pltpu.VMEM((count, tokens, dim), jnp.bfloat16),
                pltpu.VMEM((count, 2 * tokens, dim), jnp.float32),
                pltpu.VMEM((slots + 8, wide), jnp.float32),
                pltpu.VMEM((slots + 8, wide), jnp.float32),
                pltpu.VMEM((slots + 8, wide), jnp.float32),
                pltpu.VMEM((most, GROUP * tokens, dim), jnp.bfloat16),
            ],
        ),
        out_shape=jax.ShapeDtypeStruct((height, dim), jnp.bfloat16),
        compiler_params=pltpu.CompilerParams(vmem_limit_bytes=12 * MIB),
        cost_estimate=pl.CostEstimate(
            flops=6 * room * tokens * wide * dim,
            bytes_accessed=2 * room * wide * dim,
            transcendentals=room * tokens * wide,
        ),
        name="pairs",
    )(source, rows, targets, queries, inverse, index)


def neg_kernel(rows_ref, queries_ref, index_ref, acc_ref, sums_ref,
               unit_ref, turned_ref, expo_ref, total_ref, left_ref, back_ref, *, tokens):
    total = rows_ref.shape[0]
    chunk = expo_ref.shape[0]
    height, dim = queries_ref.shape
    wide = index_ref.shape[1]
    lanes = 128
    half = min(height, 256)
    unit_ref[...] = rounded_queries(queries_ref[...])
    back_ref[...] = jnp.zeros_like(back_ref)
    sums_ref[...] = jnp.zeros_like(sums_ref)
    same = lax.broadcasted_iota(jnp.int32, (lanes, lanes), 0) // tokens == lax.broadcasted_iota(
        jnp.int32, (lanes, lanes), 1
    ) // tokens
    same = jnp.where(same, 1.0, 0.0).astype(jnp.bfloat16)

    def block(number, carry):
        def forward(step, carry):
            first = step * NEG_STEP
            tiles = jnp.concatenate(
                [index_ref[rows_ref[number * chunk + first + g]] for g in range(NEG_STEP)], axis=0
            )
            raw = dot_last(tiles, unit_ref[...])
            broad = tiles.astype(jnp.float32)
            inverse = lax.rsqrt(jnp.sum(broad * broad, axis=-1, keepdims=True) + epsilon)
            flat = (broad * inverse).astype(jnp.bfloat16)
            expo = jnp.exp2(raw * (inverse * (LOG2E / inner_temp)))
            for g in range(NEG_STEP):
                part = slice(g * wide, (g + 1) * wide)
                turned_ref[first + g] = flat[part].T
                expo_ref[first + g] = expo[part].astype(jnp.bfloat16)
                total_ref[pl.ds(first + g, 1), :] = jnp.sum(expo[part], axis=0, keepdims=True)
            return carry

        lax.fori_loop(0, chunk // NEG_STEP, forward, 0)
        for c in range(height // lanes):
            part = slice(c * lanes, (c + 1) * lanes)
            totals = total_ref[:, part]
            pieces = [dot(piece, same) for piece in split3(jnp.log(totals))]
            lift = jnp.exp(inner_temp * (pieces[0] + pieces[1] + pieces[2]))
            left_ref[:, part] = lift / totals
            sums_ref[:, part] += jnp.broadcast_to(jnp.sum(lift, axis=0, keepdims=True), (8, lanes))
        for c in range(height // half):
            part = slice(c * half, (c + 1) * half)

            def backward(step, acc):
                for g in range(NEG_STEP):
                    k = step * NEG_STEP + g
                    acc = acc + dot(turned_ref[k], expo_ref[k, :, part]) * left_ref[pl.ds(k, 1), part]
                return acc

            back_ref[:, part] = lax.fori_loop(0, chunk // NEG_STEP, backward, back_ref[:, part])
        return carry

    lax.fori_loop(0, total // chunk, block, 0)
    for c in range(height // lanes):
        part = slice(c * lanes, (c + 1) * lanes)
        acc_ref[part, :] = back_ref[:, part].T


def negatives(rows, queries, index):
    total = rows.shape[0]
    count, tokens, dim = queries.shape
    wide = index.shape[1]
    height = count * tokens
    chunk = math.gcd(total, NEG_CHUNK)
    return pl.pallas_call(
        functools.partial(neg_kernel, tokens=tokens),
        in_specs=[
            pl.BlockSpec(memory_space=pltpu.SMEM),
            pl.BlockSpec(memory_space=pltpu.VMEM),
            pl.BlockSpec(memory_space=pltpu.VMEM),
        ],
        out_specs=[pl.BlockSpec(memory_space=pltpu.VMEM)] * 2,
        out_shape=[
            jax.ShapeDtypeStruct((height, dim), jnp.float32),
            jax.ShapeDtypeStruct((8, height), jnp.float32),
        ],
        scratch_shapes=[
            pltpu.VMEM((height, dim), jnp.bfloat16),
            pltpu.VMEM((chunk, dim, wide), jnp.bfloat16),
            pltpu.VMEM((chunk, wide, height), jnp.bfloat16),
            pltpu.VMEM((chunk, height), jnp.float32),
            pltpu.VMEM((chunk, height), jnp.float32),
            pltpu.VMEM((dim, height), jnp.float32),
        ],
        compiler_params=pltpu.CompilerParams(vmem_limit_bytes=28 * MIB),
        cost_estimate=pl.CostEstimate(
            flops=4 * total * height * wide * dim,
            bytes_accessed=2 * total * wide * dim,
            transcendentals=total * height * wide,
        ),
        name="negatives",
    )(rows, queries.reshape(height, dim), index)


def on_device(queries, index, cand_owner, cand_row, neg_row, teacher):
    count, tokens, dim = queries.shape
    cands = cand_row.shape[1]
    shard = index.shape[0]
    owners = lax.axis_size("corpus")
    room = (2 * count * cands + owners - 1) // owners
    me = lax.axis_index("corpus").astype(jnp.int32)
    group = lax.axis_size("blk")

    def from_step(value, axis, size, step):
        return lax.ppermute(value, axis, [((i + step) % size, i) for i in range(size)])

    def gathered(value, axis, size):
        return [value] + [from_step(value, axis, size, step) for step in range(1, size)]

    code = (cand_owner[..., 0] * shard + cand_row).astype(jnp.float32)
    meta = jnp.concatenate([code, teacher], axis=1)
    all_neg = jnp.concatenate(gathered(neg_row, "blk", group), axis=0).reshape(-1)
    all_meta = lax.all_gather(meta, "corpus", axis=0, tiled=True)
    all_queries = gathered(queries, "corpus", owners)
    index = pltpu.with_memory_space_constraint(index, pltpu.VMEM)
    inverse = norms(index)
    neg_acc, neg_sum = negatives(all_neg, queries, index)
    rows, targets = prep(me.reshape(1), all_meta, shard, cands)
    rows, neg_acc = lax.optimization_barrier((rows, neg_acc))
    messages = []
    for step in list(range(1, owners)) + [0]:
        source = lax.rem(me + step, owners)
        message = pairs(
            source.reshape(1), rows, targets, all_queries[step], inverse, index, cands, room
        )
        if step:
            message = lax.ppermute(
                message, "corpus", [(i, (i + step) % owners) for i in range(owners)]
            )
        messages.append(message)
    cut = count * 2 * tokens
    both = sum(m[:cut].astype(jnp.float32) for m in messages).reshape(count, 2, tokens, dim)
    scores = sum(m[cut:].astype(jnp.float32) for m in messages).reshape(3, count, dim).sum(axis=0)
    total = scores[:, 0] + neg_sum[0].reshape(count, tokens)[:, 0]
    spread = jnp.log(total)
    log_target = teacher - jnp.log(jnp.sum(jnp.exp(teacher), axis=1, keepdims=True))
    target = jnp.exp(log_target)
    losses = jnp.sum(target * (log_target + spread[:, None]), axis=1) - scores[:, dim // 2]
    pulled = (both[:, 0] + neg_acc.reshape(count, tokens, dim)) / total[:, None, None] - both[:, 1]
    widened = queries.astype(jnp.float32)
    radius = jnp.sqrt(jnp.sum(widened * widened, axis=-1, keepdims=True) + epsilon)
    unit = widened / radius
    query_grads = (pulled - unit * jnp.sum(unit * pulled, axis=-1, keepdims=True)) / radius
    return (losses, query_grads)


def solution(mesh):
    placed = (
        P(("corpus", "blk"), None, None),
        P("corpus", None, None),
        P(("corpus", "blk"), None, None),
        P(("corpus", "blk"), None),
        P(("corpus", "blk"), None),
        P(("corpus", "blk"), None),
    )
    return jax.shard_map(
        on_device,
        mesh=mesh,
        in_specs=placed,
        out_specs=(P(("corpus", "blk")), P(("corpus", "blk"), None, None)),
        check_vma=False,
    )
```

profile of v0, /device:TPU:0, one launch (start us, length us, event | category | flops | bytes accessed | tf_op | source)
XLA Modules:
  0.0 260.5 jit_solution(14740468486333987792)
XLA Ops:
  0.6 3.0 %collective-permute-start.1 = (s32[1,24]{1,0:T(1,128)}, s32[1,24]{1,0:T(1,128)S(1)}, u32[]{:S(2)}, u32[]{:S(2)}) collective-permute-start(s32[1,24]{1,0:T(1,128)} %param.10), channel_id=1, source_target_pairs={{2,0},{3,1},{0,2},{1,3},{6,4},{7,5},{4,6},{5,7},{10,8},{11,9},{8,1... | collective-permute-start | bytes 296 | tf_op jit(solution)/shard_map/ppermute | solution.py:403
  4.2 1.5 collective-permute-start.15
  5.7 1.6 collective-permute-start.13
  7.3 1.1 fusion.4
  9.0 0.7 fusion.10
  9.7 0.8 pad_maximum_fusion
  10.5 30.5 %all_gather.3.meta_ref = f32[128,128]{1,0:T(8,128)S(1)} all-gather(f32[16,128]{1,0:T(8,128)S(1)} %pad_maximum_fusion), channel_id=1, replica_groups=mesh['corpus'=8,'blk'=4] {'corpus'}, dimensions={0}, use_global_device_ids=true | all-gather | bytes 73728 | tf_op jit(solution)/shard_map/all_gather | solution.py:411
  41.0 5.8 %copy-done = bf16[512,128,128]{2,1,0:T(8,128)(2,1)S(1)} copy-done((bf16[512,128,128]{2,1,0:T(8,128)(2,1)S(1)}, bf16[512,128,128]{2,1,0:T(8,128)(2,1)}, u32[]{:S(2)}) %copy-start) | copy-done | bytes 16777240
  46.7 21.5 %norms.1.inverse_ref = f32[512,128]{1,0:T(8,128)S(1)} custom-call(bf16[512,128,128]{2,1,0:T(8,128)(2,1)S(1)} %copy-done), custom_call_target="tpu_custom_call" | custom-call | flops 268435456 | bytes 16777216 | tf_op jit(solution)/shard_map/norms/pallas_call | solution.py:65
  68.2 5.0 %prep.1 = (s32[128,128]{1,0:T(8,128)S(1)}, f32[2048,128]{1,0:T(8,128)S(1)}) custom-call(s32[1]{0:T(128)} %bitcast.1.me_ref, f32[128,128]{1,0:T(8,128)S(1)} %all_gather.3.meta_ref), custom_call_target="tpu_custom_call" | custom-call | tf_op jit(solution)/shard_map/prep/pallas_call | solution.py:134
  73.3 3.7 %collective-permute-start.9 = (bf16[16,32,128]{2,1,0:T(8,128)(2,1)S(1)}, bf16[16,32,128]{2,1,0:T(8,128)(2,1)S(1)}, u32[]{:S(2)}, u32[]{:S(2)}) collective-permute-start(bf16[16,32,128]{2,1,0:T(8,128)(2,1)S(1)} %copy-done.4), channel_id=1, source_target_pairs={{16,0},{20,4},{24,8},{28,12},{0,16},{4,20},{8,24},{12,28},{17,1},{... | collective-permute-start | bytes 393224 | tf_op jit(solution)/shard_map/ppermute | solution.py:403
  77.1 0.6 collective-permute-start.3
  77.8 5.8 %copy-done.1 = bf16[512,128,128]{2,1,0:T(8,128)(2,1)S(1)} copy-done((bf16[512,128,128]{2,1,0:T(8,128)(2,1)S(1)}, bf16[512,128,128]{2,1,0:T(8,128)(2,1)}, u32[]{:S(2)}) %copy-start.1) | copy-done | bytes 16777240
  83.6 15.1 %negatives.1 = (f32[512,128]{1,0:T(8,128)S(1)}, f32[8,512]{1,0:T(8,128)S(1)}) custom-call(s32[96]{0:T(128)S(1)} %reshape.71.rows_ref, bf16[512,128]{1,0:T(8,128)(2,1)S(1)} %bitcast.46, bf16[512,128,128]{2,1,0:T(8,128)(2,1)S(1)} %copy-done.1), custom_call_target="tpu_custom_call" | custom-call | flops 3221225472 | bytes 3145728 | tf_op jit(solution)/shard_map/negatives/pallas_call | solution.py:363
  98.7 1.0 collective-permute-start.5
  99.7 11.0 %pairs.14 = bf16[1072,128]{1,0:T(8,128)(2,1)S(1)} custom-call(s32[1]{0:T(128)} %bitcast.10.source_ref, s32[128,128]{1,0:T(8,128)S(1)} %get-tuple-element.10.rows_ref, f32[2048,128]{1,0:T(8,128)S(1)} %get-tuple-element.11.target_ref, bf16[16,32,128]{2,1,0:T(8,128)(2,1)S(1)} %collective-permute-done.15.queries_ref, f32[512,128]{1,0:T(8,128)S(1)} %norms.1.inverse_ref, ...), custom_call_target="tpu_custom_call" | custom-call | flops 805306368 | bytes 8388608 | tf_op jit(solution)/shard_map/pairs/pallas_call | solution.py:263
  110.7 9.7 %collective-permute-start.7 = (bf16[16,32,128]{2,1,0:T(8,128)(2,1)S(1)}, bf16[16,32,128]{2,1,0:T(8,128)(2,1)S(1)}, u32[]{:S(2)}, u32[]{:S(2)}) collective-permute-start(bf16[16,32,128]{2,1,0:T(8,128)(2,1)S(1)} %copy-done.4), channel_id=1, source_target_pairs={{12,0},{16,4},{20,8},{24,12},{28,16},{0,20},{4,24},{8,28},{13,1},{... | collective-permute-start | bytes 393224 | tf_op jit(solution)/shard_map/ppermute | solution.py:403
  120.4 12.9 %pairs.8 = bf16[1072,128]{1,0:T(8,128)(2,1)S(1)} custom-call(s32[1]{0:T(128)} %bitcast.source_ref, s32[128,128]{1,0:T(8,128)S(1)} %get-tuple-element.10.rows_ref, f32[2048,128]{1,0:T(8,128)S(1)} %get-tuple-element.11.target_ref, bf16[16,32,128]{2,1,0:T(8,128)(2,1)S(1)} %collective-permute-done.3.queries_ref, f32[512,128]{1,0:T(8,128)S(1)} %norms.1.inverse_ref, ...), custom_call_target="tpu_custom_call" | custom-call | flops 805306368 | bytes 8388608 | tf_op jit(solution)/shard_map/pairs/pallas_call | solution.py:263
  133.4 11.0 %pairs.9 = bf16[1072,128]{1,0:T(8,128)(2,1)S(1)} custom-call(s32[1]{0:T(128)} %bitcast.5.source_ref, s32[128,128]{1,0:T(8,128)S(1)} %get-tuple-element.10.rows_ref, f32[2048,128]{1,0:T(8,128)S(1)} %get-tuple-element.11.target_ref, bf16[16,32,128]{2,1,0:T(8,128)(2,1)S(1)} %collective-permute-done.5.queries_ref, f32[512,128]{1,0:T(8,128)S(1)} %norms.1.inverse_ref, ...), custom_call_target="tpu_custom_call" | custom-call | flops 805306368 | bytes 8388608 | tf_op jit(solution)/shard_map/pairs/pallas_call | solution.py:263
  144.4 12.9 %pairs.10 = bf16[1072,128]{1,0:T(8,128)(2,1)S(1)} custom-call(s32[1]{0:T(128)} %bitcast.6.source_ref, s32[128,128]{1,0:T(8,128)S(1)} %get-tuple-element.10.rows_ref, f32[2048,128]{1,0:T(8,128)S(1)} %get-tuple-element.11.target_ref, bf16[16,32,128]{2,1,0:T(8,128)(2,1)S(1)} %collective-permute-done.7.queries_ref, f32[512,128]{1,0:T(8,128)S(1)} %norms.1.inverse_ref, ...), custom_call_target="tpu_custom_call" | custom-call | flops 805306368 | bytes 8388608 | tf_op jit(solution)/shard_map/pairs/pallas_call | solution.py:263
  157.3 8.3 %collective-permute-start.8 = (bf16[1072,128]{1,0:T(8,128)(2,1)S(1)}, bf16[1072,128]{1,0:T(8,128)(2,1)}, u32[]{:S(2)}, u32[]{:S(2)}) collective-permute-start(bf16[1072,128]{1,0:T(8,128)(2,1)S(1)} %pairs.10), channel_id=1, source_target_pairs={{0,12},{4,16},{8,20},{12,24},{16,28},{20,0},{24,4},{28,8},{1,13},{... | collective-permute-start | bytes 823304 | tf_op jit(solution)/shard_map/ppermute | solution.py:425
  165.7 13.1 %pairs.11 = bf16[1072,128]{1,0:T(8,128)(2,1)S(1)} custom-call(s32[1]{0:T(128)} %bitcast.7.source_ref, s32[128,128]{1,0:T(8,128)S(1)} %get-tuple-element.10.rows_ref, f32[2048,128]{1,0:T(8,128)S(1)} %get-tuple-element.11.target_ref, bf16[16,32,128]{2,1,0:T(8,128)(2,1)S(1)} %collective-permute-done.9.queries_ref, f32[512,128]{1,0:T(8,128)S(1)} %norms.1.inverse_ref, ...), custom_call_target="tpu_custom_call" | custom-call | flops 805306368 | bytes 8388608 | tf_op jit(solution)/shard_map/pairs/pallas_call | solution.py:263
  178.8 9.7 %collective-permute-start.10 = (bf16[1072,128]{1,0:T(8,128)(2,1)S(1)}, bf16[1072,128]{1,0:T(8,128)(2,1)}, u32[]{:S(2)}, u32[]{:S(2)}) collective-permute-start(bf16[1072,128]{1,0:T(8,128)(2,1)S(1)} %pairs.11), channel_id=1, source_target_pairs={{0,16},{4,20},{8,24},{12,28},{16,0},{20,4},{24,8},{28,12},{1,17},{... | collective-permute-start | bytes 823304 | tf_op jit(solution)/shard_map/ppermute | solution.py:425
  188.5 11.0 %pairs.12 = bf16[1072,128]{1,0:T(8,128)(2,1)S(1)} custom-call(s32[1]{0:T(128)} %bitcast.8.source_ref, s32[128,128]{1,0:T(8,128)S(1)} %get-tuple-element.10.rows_ref, f32[2048,128]{1,0:T(8,128)S(1)} %get-tuple-element.11.target_ref, bf16[16,32,128]{2,1,0:T(8,128)(2,1)S(1)} %collective-permute-done.11.queries_ref, f32[512,128]{1,0:T(8,128)S(1)} %norms.1.inverse_ref, ...), custom_call_target="tpu_custom_call" | custom-call | flops 805306368 | bytes 8388608 | tf_op jit(solution)/shard_map/pairs/pallas_call | solution.py:263
  199.5 15.0 %collective-permute-start.12 = (bf16[1072,128]{1,0:T(8,128)(2,1)S(1)}, bf16[1072,128]{1,0:T(8,128)(2,1)}, u32[]{:S(2)}, u32[]{:S(2)}) collective-permute-start(bf16[1072,128]{1,0:T(8,128)(2,1)S(1)} %pairs.12), channel_id=1, source_target_pairs={{0,20},{4,24},{8,28},{12,0},{16,4},{20,8},{24,12},{28,16},{1,21},{... | collective-permute-start | bytes 823304 | tf_op jit(solution)/shard_map/ppermute | solution.py:425
  214.5 12.9 %pairs.13 = bf16[1072,128]{1,0:T(8,128)(2,1)S(1)} custom-call(s32[1]{0:T(128)} %bitcast.9.source_ref, s32[128,128]{1,0:T(8,128)S(1)} %get-tuple-element.10.rows_ref, f32[2048,128]{1,0:T(8,128)S(1)} %get-tuple-element.11.target_ref, bf16[16,32,128]{2,1,0:T(8,128)(2,1)S(1)} %collective-permute-done.13.queries_ref, f32[512,128]{1,0:T(8,128)S(1)} %norms.1.inverse_ref, ...), custom_call_target="tpu_custom_call" | custom-call | flops 805306368 | bytes 8388608 | tf_op jit(solution)/shard_map/pairs/pallas_call | solution.py:263
  227.5 7.3 %collective-permute-start.16 = (bf16[1072,128]{1,0:T(8,128)(2,1)S(1)}, bf16[1072,128]{1,0:T(8,128)(2,1)}, u32[]{:S(2)}, u32[]{:S(2)}) collective-permute-start(bf16[1072,128]{1,0:T(8,128)(2,1)S(1)} %pairs.14), channel_id=1, source_target_pairs={{0,28},{4,0},{8,4},{12,8},{16,12},{20,16},{24,20},{28,24},{1,29},{... | collective-permute-start | bytes 823304 | tf_op jit(solution)/shard_map/ppermute | solution.py:425
  235.0 5.8 %copy-done.3 = bf16[512,128,128]{2,1,0:T(8,128)(2,1)S(1)} copy-done((bf16[512,128,128]{2,1,0:T(8,128)(2,1)S(1)}, bf16[512,128,128]{2,1,0:T(8,128)(2,1)}, u32[]{:S(2)}) %copy-start.3) | copy-done | bytes 16777240
  240.7 12.9 %pairs.15 = bf16[1072,128]{1,0:T(8,128)(2,1)S(1)} custom-call(s32[1]{0:T(128)} %bitcast.11.source_ref, s32[128,128]{1,0:T(8,128)S(1)} %get-tuple-element.10.rows_ref, f32[2048,128]{1,0:T(8,128)S(1)} %get-tuple-element.11.target_ref, bf16[16,32,128]{2,1,0:T(8,128)(2,1)S(1)} %copy-done.4, f32[512,128]{1,0:T(8,128)S(1)} %norms.1.inverse_ref, ...), custom_call_target="tpu_custom_call" | custom-call | flops 805306368 | bytes 8388608 | tf_op jit(solution)/shard_map/pairs/pallas_call | solution.py:263
  253.7 0.8 convert_add_fusion.1
  255.4 1.7 convert_add_fusion
  257.1 3.3 %fusion.3 = f32[16,32,128]{2,1,0:T(8,128)} fusion(bf16[16,32,128]{2,1,0:T(8,128)(2,1)S(1)} %copy-done.4, f32[16,32]{1,0:T(8,128)S(1)} %copy-done.6, f32[16,2,32,128]{3,2,1,0:T(8,128)S(1)} %bitcast.48, f32[16]{0:T(128)S(1)} %get-tuple-element.14, f32[16,32,128]{2,1,0:T(8,128)S(1)} %bitcast.47), kind=kOutput, calls=%fused_computation.3 | output fusion | flops 918143 | bytes 2114560 | tf_op jit(solution)/shard_map/mul | solution.py:441
  (47 shorter events, 2.6 us)
Async XLA Ops:
  0.6 77.1 %copy-start.7 = (s32[1,24]{1,0:T(1,128)S(1)}, s32[1,24]{1,0:T(1,128)}, u32[]{:S(2)}) copy-start(s32[1,24]{1,0:T(1,128)} %param.10) | copy-start | bytes 292
  0.6 72.6 %copy-start.4 = (bf16[16,32,128]{2,1,0:T(8,128)(2,1)S(1)}, bf16[16,32,128]{2,1,0:T(8,128)(2,1)}, u32[]{:S(2)}) copy-start(bf16[16,32,128]{2,1,0:T(8,128)(2,1)} %queries_ref.1) | copy-start | bytes 393220
  0.6 72.6 %collective-permute-start.1 = (s32[1,24]{1,0:T(1,128)}, s32[1,24]{1,0:T(1,128)S(1)}, u32[]{:S(2)}, u32[]{:S(2)}) collective-permute-start(s32[1,24]{1,0:T(1,128)} %param.10), channel_id=1, source_target_pairs={{2,0},{3,1},{0,2},{1,3},{6,4},{7,5},{4,6},{5,7},{10,8},{11,9},{8,1... | collective-permute-start | bytes 296 | tf_op jit(solution)/shard_map/ppermute | solution.py:403
  3.7 69.7 %collective-permute-start = (s32[1,24]{1,0:T(1,128)}, s32[1,24]{1,0:T(1,128)S(1)}, u32[]{:S(2)}, u32[]{:S(2)}) collective-permute-start(s32[1,24]{1,0:T(1,128)} %param.10), channel_id=1, source_target_pairs={{1,0},{2,1},{3,2},{0,3},{5,4},{6,5},{7,6},{4,7},{9,8},{10,9},{11,1... | collective-permute-start | bytes 296 | tf_op jit(solution)/shard_map/ppermute | solution.py:403
  3.7 73.4 %collective-permute-start.2 = (s32[1,24]{1,0:T(1,128)}, s32[1,24]{1,0:T(1,128)S(1)}, u32[]{:S(2)}, u32[]{:S(2)}) collective-permute-start(s32[1,24]{1,0:T(1,128)} %param.10), channel_id=1, source_target_pairs={{3,0},{0,1},{1,2},{2,3},{7,4},{4,5},{5,6},{6,7},{11,8},{8,9},{9,10... | collective-permute-start | bytes 296 | tf_op jit(solution)/shard_map/ppermute | solution.py:403
  4.2 94.6 %collective-permute-start.15 = (bf16[16,32,128]{2,1,0:T(8,128)(2,1)}, bf16[16,32,128]{2,1,0:T(8,128)(2,1)S(1)}, u32[]{:S(2)}, u32[]{:S(2)}) collective-permute-start(bf16[16,32,128]{2,1,0:T(8,128)(2,1)} %queries_ref.1), channel_id=1, source_target_pairs={{28,0},{0,4},{4,8},{8,12},{12,16},{16,20},{20,24},{24,28},{29,1},{... | collective-permute-start | bytes 393224 | tf_op jit(solution)/shard_map/ppermute | solution.py:403
  5.7 193.8 %collective-permute-start.13 = (bf16[16,32,128]{2,1,0:T(8,128)(2,1)}, bf16[16,32,128]{2,1,0:T(8,128)(2,1)S(1)}, u32[]{:S(2)}, u32[]{:S(2)}) collective-permute-start(bf16[16,32,128]{2,1,0:T(8,128)(2,1)} %queries_ref.1), channel_id=1, source_target_pairs={{24,0},{28,4},{0,8},{4,12},{8,16},{12,20},{16,24},{20,28},{25,1},{... | collective-permute-start | bytes 393224 | tf_op jit(solution)/shard_map/ppermute | solution.py:403
  41.0 5.8 %copy-start = (bf16[512,128,128]{2,1,0:T(8,128)(2,1)S(1)}, bf16[512,128,128]{2,1,0:T(8,128)(2,1)}, u32[]{:S(2)}) copy-start(bf16[512,128,128]{2,1,0:T(8,128)(2,1)} %index_ref.19) | copy-start | bytes 50331652
  73.3 105.5 %collective-permute-start.11 = (bf16[16,32,128]{2,1,0:T(8,128)(2,1)S(1)}, bf16[16,32,128]{2,1,0:T(8,128)(2,1)S(1)}, u32[]{:S(2)}, u32[]{:S(2)}) collective-permute-start(bf16[16,32,128]{2,1,0:T(8,128)(2,1)S(1)} %copy-done.4), channel_id=1, source_target_pairs={{20,0},{24,4},{28,8},{0,12},{4,16},{8,20},{12,24},{16,28},{21,1},{... | collective-permute-start | bytes 393224 | tf_op jit(solution)/shard_map/ppermute | solution.py:403
  73.3 84.0 %collective-permute-start.9 = (bf16[16,32,128]{2,1,0:T(8,128)(2,1)S(1)}, bf16[16,32,128]{2,1,0:T(8,128)(2,1)S(1)}, u32[]{:S(2)}, u32[]{:S(2)}) collective-permute-start(bf16[16,32,128]{2,1,0:T(8,128)(2,1)S(1)} %copy-done.4), channel_id=1, source_target_pairs={{16,0},{20,4},{24,8},{28,12},{0,16},{4,20},{8,24},{12,28},{17,1},{... | collective-permute-start | bytes 393224 | tf_op jit(solution)/shard_map/ppermute | solution.py:403
  77.1 33.6 %collective-permute-start.3 = (bf16[16,32,128]{2,1,0:T(8,128)(2,1)S(1)}, bf16[16,32,128]{2,1,0:T(8,128)(2,1)S(1)}, u32[]{:S(2)}, u32[]{:S(2)}) collective-permute-start(bf16[16,32,128]{2,1,0:T(8,128)(2,1)S(1)} %copy-done.4), channel_id=1, source_target_pairs={{4,0},{8,4},{12,8},{16,12},{20,16},{24,20},{28,24},{0,28},{5,1},{9... | collective-permute-start | bytes 393224 | tf_op jit(solution)/shard_map/ppermute | solution.py:403
  77.8 5.8 %copy-start.1 = (bf16[512,128,128]{2,1,0:T(8,128)(2,1)S(1)}, bf16[512,128,128]{2,1,0:T(8,128)(2,1)}, u32[]{:S(2)}) copy-start(bf16[512,128,128]{2,1,0:T(8,128)(2,1)} %index_ref.19) | copy-start | bytes 50331652
  83.6 16.1 %copy-start.2 = (bf16[512,128,128]{2,1,0:T(8,128)(2,1)S(1)}, bf16[512,128,128]{2,1,0:T(8,128)(2,1)}, u32[]{:S(2)}) copy-start(bf16[512,128,128]{2,1,0:T(8,128)(2,1)} %index_ref.19) | copy-start | bytes 50331652
  98.7 34.5 %collective-permute-start.5 = (bf16[16,32,128]{2,1,0:T(8,128)(2,1)S(1)}, bf16[16,32,128]{2,1,0:T(8,128)(2,1)S(1)}, u32[]{:S(2)}, u32[]{:S(2)}) collective-permute-start(bf16[16,32,128]{2,1,0:T(8,128)(2,1)S(1)} %copy-done.4), channel_id=1, source_target_pairs={{8,0},{12,4},{16,8},{20,12},{24,16},{28,20},{0,24},{4,28},{9,1},{1... | collective-permute-start | bytes 393224 | tf_op jit(solution)/shard_map/ppermute | solution.py:403
  110.7 33.7 %collective-permute-start.7 = (bf16[16,32,128]{2,1,0:T(8,128)(2,1)S(1)}, bf16[16,32,128]{2,1,0:T(8,128)(2,1)S(1)}, u32[]{:S(2)}, u32[]{:S(2)}) collective-permute-start(bf16[16,32,128]{2,1,0:T(8,128)(2,1)S(1)} %copy-done.4), channel_id=1, source_target_pairs={{12,0},{16,4},{20,8},{24,12},{28,16},{0,20},{4,24},{8,28},{13,1},{... | collective-permute-start | bytes 393224 | tf_op jit(solution)/shard_map/ppermute | solution.py:403
  133.3 94.1 %collective-permute-start.4 = (bf16[1072,128]{1,0:T(8,128)(2,1)S(1)}, bf16[1072,128]{1,0:T(8,128)(2,1)}, u32[]{:S(2)}, u32[]{:S(2)}) collective-permute-start(bf16[1072,128]{1,0:T(8,128)(2,1)S(1)} %pairs.8), channel_id=1, source_target_pairs={{0,4},{4,8},{8,12},{12,16},{16,20},{20,24},{24,28},{28,0},{1,5},{5... | collective-permute-start | bytes 823304 | tf_op jit(solution)/shard_map/ppermute | solution.py:425
  144.3 83.1 %collective-permute-start.6 = (bf16[1072,128]{1,0:T(8,128)(2,1)S(1)}, bf16[1072,128]{1,0:T(8,128)(2,1)}, u32[]{:S(2)}, u32[]{:S(2)}) collective-permute-start(bf16[1072,128]{1,0:T(8,128)(2,1)S(1)} %pairs.9), channel_id=1, source_target_pairs={{0,8},{4,12},{8,16},{12,20},{16,24},{20,28},{24,0},{28,4},{1,9},{5... | collective-permute-start | bytes 823304 | tf_op jit(solution)/shard_map/ppermute | solution.py:425
  157.3 96.3 %collective-permute-start.8 = (bf16[1072,128]{1,0:T(8,128)(2,1)S(1)}, bf16[1072,128]{1,0:T(8,128)(2,1)}, u32[]{:S(2)}, u32[]{:S(2)}) collective-permute-start(bf16[1072,128]{1,0:T(8,128)(2,1)S(1)} %pairs.10), channel_id=1, source_target_pairs={{0,12},{4,16},{8,20},{12,24},{16,28},{20,0},{24,4},{28,8},{1,13},{... | collective-permute-start | bytes 823304 | tf_op jit(solution)/shard_map/ppermute | solution.py:425
  178.8 74.9 %collective-permute-start.10 = (bf16[1072,128]{1,0:T(8,128)(2,1)S(1)}, bf16[1072,128]{1,0:T(8,128)(2,1)}, u32[]{:S(2)}, u32[]{:S(2)}) collective-permute-start(bf16[1072,128]{1,0:T(8,128)(2,1)S(1)} %pairs.11), channel_id=1, source_target_pairs={{0,16},{4,20},{8,24},{12,28},{16,0},{20,4},{24,8},{28,12},{1,17},{... | collective-permute-start | bytes 823304 | tf_op jit(solution)/shard_map/ppermute | solution.py:425
  188.5 46.2 %copy-start.5 = (f32[16,64]{1,0:T(8,128)S(1)}, f32[16,64]{1,0:T(8,128)}, u32[]{:S(2)}) copy-start(f32[16,64]{1,0:T(8,128)} %param.11) | copy-start | bytes 12292
  199.5 54.2 %collective-permute-start.12 = (bf16[1072,128]{1,0:T(8,128)(2,1)S(1)}, bf16[1072,128]{1,0:T(8,128)(2,1)}, u32[]{:S(2)}, u32[]{:S(2)}) collective-permute-start(bf16[1072,128]{1,0:T(8,128)(2,1)S(1)} %pairs.12), channel_id=1, source_target_pairs={{0,20},{4,24},{8,28},{12,0},{16,4},{20,8},{24,12},{28,16},{1,21},{... | collective-permute-start | bytes 823304 | tf_op jit(solution)/shard_map/ppermute | solution.py:425
  227.4 29.8 %copy-start.6 = (f32[16,32]{1,0:T(8,128)S(1)}, f32[16,32]{1,0:T(8,128)}, u32[]{:S(2)}) copy-start(f32[16,32]{1,0:T(8,128)} %add_sqrt_fusion) | copy-start | bytes 6148
  227.4 26.3 %collective-permute-start.14 = (bf16[1072,128]{1,0:T(8,128)(2,1)S(1)}, bf16[1072,128]{1,0:T(8,128)(2,1)}, u32[]{:S(2)}, u32[]{:S(2)}) collective-permute-start(bf16[1072,128]{1,0:T(8,128)(2,1)S(1)} %pairs.13), channel_id=1, source_target_pairs={{0,24},{4,28},{8,0},{12,4},{16,8},{20,12},{24,16},{28,20},{1,25},{... | collective-permute-start | bytes 823304 | tf_op jit(solution)/shard_map/ppermute | solution.py:425
  227.5 26.2 %collective-permute-start.16 = (bf16[1072,128]{1,0:T(8,128)(2,1)S(1)}, bf16[1072,128]{1,0:T(8,128)(2,1)}, u32[]{:S(2)}, u32[]{:S(2)}) collective-permute-start(bf16[1072,128]{1,0:T(8,128)(2,1)S(1)} %pairs.14), channel_id=1, source_target_pairs={{0,28},{4,0},{8,4},{12,8},{16,12},{20,16},{24,20},{28,24},{1,29},{... | collective-permute-start | bytes 823304 | tf_op jit(solution)/shard_map/ppermute | solution.py:425
  235.0 5.8 %copy-start.3 = (bf16[512,128,128]{2,1,0:T(8,128)(2,1)S(1)}, bf16[512,128,128]{2,1,0:T(8,128)(2,1)}, u32[]{:S(2)}) copy-start(bf16[512,128,128]{2,1,0:T(8,128)(2,1)} %index_ref.19) | copy-start | bytes 50331652
where the time goes:
time: 261 us; the launch traced here: 260 us
  Pallas kernels  139 us (53%)
  starting transfers between devices  62.2 us (24%)
  blocking collectives  30.5 us (12%)
  local copies, waits for them, and re-layouts  17.5 us (7%)
  other arithmetic  10.1 us (4%)
    pallas_call x8, Pallas kernels, pairs(): pl.pallas_call(functools.partial(pair_kernel, cands=cands), grid_spec=plt...  97.6 us
    ppermute x7, starting transfers between devices, on_device(): lax.ppermute(message, 'corpus', [(i, (i + step) % owners) for i in range(...  40.5 us
    all_gather x1, blocking collectives, on_device(): all_meta = lax.all_gather(meta, 'corpus', axis=0, tiled=True)  30.5 us
    ppermute x10, starting transfers between devices, from_step(): lax.ppermute(value, axis, [((i + step) % size, i) for i in range(size)])  21.7 us
    pallas_call x1, Pallas kernels, norms(): pl.pallas_call(norm_kernel, in_specs=[pl.BlockSpec(memory_space=pltpu.VME...  21.5 us
    unnamed x16, local copies, waits for them, and re-layouts  17.3 us
    pallas_call x1, Pallas kernels, negatives(): pl.pallas_call(functools.partial(neg_kernel, tokens=tokens), in_specs=[pl...  15.1 us
  transfers between devices with their start and end apart: 17, of which 0 were waited for; matrix products, arithmetic and copies ran while one was open for 1% of the time, Pallas kernels for 53%

commit v1 on v0

--- a/solution.py
+++ b/solution.py
@@ -41,15 +41,17 @@
     return (wide / radius).astype(jnp.bfloat16)
 
 
-def norm_kernel(index_ref, out_ref):
-    count, tokens, dim = index_ref.shape
+def norm_kernel(part_ref, index_ref, out_ref):
+    count, tokens = out_ref.shape
+    dim = index_ref.shape[2]
+    base = part_ref[0] * count
     ones = jnp.ones((8, dim), jnp.bfloat16)
     sub = lax.broadcasted_iota(jnp.int32, (8, tokens), 0)
 
     def body(step, carry):
         squares = jnp.zeros((8, tokens), jnp.float32)
         for k in range(8):
-            tile = index_ref[step * 8 + k].astype(jnp.float32)
+            tile = index_ref[base + step * 8 + k].astype(jnp.float32)
             tile = tile * tile
             high = tile.astype(jnp.bfloat16)
             low = (tile - high.astype(jnp.float32)).astype(jnp.bfloat16)
@@ -60,11 +62,12 @@
     lax.fori_loop(0, count // 8, body, 0, unroll=2)
 
 
-def norms(index):
-    count, tokens, dim = index.shape
+def norms(part, index, parts):
+    tokens, dim = index.shape[1:]
+    count = index.shape[0] // parts
     return pl.pallas_call(
         norm_kernel,
-        in_specs=[pl.BlockSpec(memory_space=pltpu.VMEM)],
+        in_specs=[pl.BlockSpec(memory_space=pltpu.SMEM), pl.BlockSpec(memory_space=pltpu.VMEM)],
         out_specs=pl.BlockSpec(memory_space=pltpu.VMEM),
         out_shape=jax.ShapeDtypeStruct((count, tokens), jnp.float32),
         compiler_params=pltpu.CompilerParams(vmem_limit_bytes=8 * MIB),
@@ -74,7 +77,7 @@
             transcendentals=count * tokens,
         ),
         name="norms",
-    )(index)
+    )(part, index)
 
 
 def prep_kernel(me_ref, meta_ref, rows_ref, target_ref, value_ref, place_ref, result_ref, *, shard, cands):
@@ -153,7 +156,7 @@
 
 
 def pair_kernel(source_ref, rows_ref, target_ref, queries_ref, inverse_ref, index_ref, out_ref,
-                units_ref, unit_ref, acc_ref, total_ref, left_ref, right_ref, back_ref, *, cands):
+                units_ref, unit_ref, acc_ref, total_ref, left_ref, right_ref, back_ref, raw_ref, *, cands):
     count, tokens, dim = queries_ref.shape
     wide = rows_ref.shape[1]
     per_query = cands // GROUP
@@ -164,7 +167,7 @@
         for t in range(per_query):
             units_ref[total + t] = jnp.int32(q * per_query + t)
         total = total + lax.div(rows_ref[q, cands] + (GROUP - 1), GROUP)
-    for t in range(UNITS):
+    for t in range(2 * UNITS):
         units_ref[total + t] = jnp.int32(slots)
     steps = lax.div(total + (UNITS - 1), UNITS)
 
@@ -178,30 +181,48 @@
     acc_ref[...] = jnp.zeros_like(acc_ref)
     ones = jnp.ones((8, wide), jnp.bfloat16)
 
+    def tiles_of(number):
+        _, q, base = entry(number)
+        rows = [rows_ref[q, base + g] for g in range(GROUP)]
+        return q, rows, [index_ref[row] for row in rows]
+
+    def multiply(step):
+        found = []
+        for u in range(UNITS):
+            q, _, tiles = tiles_of(step * UNITS + u)
+            found.append(dot_last(unit_ref[q], jnp.concatenate(tiles, axis=0)))
+        return found
+
     def forward(step, carry):
+        expos, weights = [], []
+        for u in range(UNITS):
+            _, q, base = entry(step * UNITS + u)
+            for g in range(GROUP):
+                row = rows_ref[q, base + g] - source_ref[1]
+                row = row + jnp.where(row < 0, index_ref.shape[0], 0)
+                inverse = inverse_ref[pl.ds(row, 1), :]
+                raw = raw_ref[u, :, g * wide : (g + 1) * wide]
+                expo = jnp.exp2(raw * (inverse * (LOG2E / inner_temp)))
+                expos.append(expo.astype(jnp.bfloat16))
+                weights.append((expo * inverse).astype(jnp.bfloat16))
+        following = multiply(step + 1)
         done = []
         for u in range(UNITS):
-            slot, q, base = entry(step * UNITS + u)
-            rows = [rows_ref[q, base + g] for g in range(GROUP)]
-            tiles = jnp.concatenate([index_ref[row] for row in rows], axis=0)
-            raw = dot_last(unit_ref[q], tiles)
-            expos, backs = [], []
-            for g in range(GROUP):
-                inverse = inverse_ref[pl.ds(rows[g], 1), :]
-                expo = jnp.exp2(raw[:, g * wide : (g + 1) * wide] * (inverse * (LOG2E / inner_temp)))
-                expos.append(expo.astype(jnp.bfloat16))
-                backs.append(
-                    dot((expo * inverse).astype(jnp.bfloat16), tiles[g * wide : (g + 1) * wide]).astype(
-                        jnp.bfloat16
-                    )
-                )
-            totals = dot_last(ones, jnp.concatenate(expos, axis=0))
+            slot = units_ref[step * UNITS + u]
+            part = slice(u * GROUP, (u + 1) * GROUP)
+            _, _, tiles = tiles_of(step * UNITS + u)
+            backs = [dot(w, tile).astype(jnp.bfloat16) for w, tile in zip(weights[part], tiles)]
+            totals = dot_last(ones, jnp.concatenate(expos[part], axis=0))
             done.append((slot, totals, jnp.concatenate(backs, axis=0)))
+        for u in range(UNITS):
+            raw_ref[u] = following[u]
         for u, (slot, totals, back) in enumerate(done):
             total_ref[pl.ds(slot, 1), :] = totals[0:1]
             back_ref[step * UNITS + u] = back
         return carry
 
+    for u, raw in enumerate(multiply(0)):
+        raw_ref[u] = raw
     lax.fori_loop(0, steps, forward, 0)
 
     target = target_ref[...]
@@ -274,13 +295,14 @@
             ],
             out_specs=pl.BlockSpec((height, dim), lambda i, s: (0, 0)),
             scratch_shapes=[
-                pltpu.SMEM((slots + per_query + UNITS,), jnp.int32),
+                pltpu.SMEM((slots + per_query + 2 * UNITS,), jnp.int32),
                 pltpu.VMEM((count, tokens, dim), jnp.bfloat16),
                 pltpu.VMEM((count, 2 * tokens, dim), jnp.float32),
                 pltpu.VMEM((slots + 8, wide), jnp.float32),
                 pltpu.VMEM((slots + 8, wide), jnp.float32),
                 pltpu.VMEM((slots + 8, wide), jnp.float32),
                 pltpu.VMEM((most, GROUP * tokens, dim), jnp.bfloat16),
+                pltpu.VMEM((UNITS, tokens, GROUP * wide), jnp.float32),
             ],
         ),
         out_shape=jax.ShapeDtypeStruct((height, dim), jnp.bfloat16),
@@ -409,9 +431,13 @@
     meta = jnp.concatenate([code, teacher], axis=1)
     all_neg = jnp.concatenate(gathered(neg_row, "blk", group), axis=0).reshape(-1)
     all_meta = lax.all_gather(meta, "corpus", axis=0, tiled=True)
-    all_queries = gathered(queries, "corpus", owners)
+    all_meta, sent = lax.optimization_barrier((all_meta, queries))
+    all_queries = gathered(sent, "corpus", owners)
     index = pltpu.with_memory_space_constraint(index, pltpu.VMEM)
-    inverse = norms(index)
+    part = lax.axis_index("blk").astype(jnp.int32)
+    pieces = gathered(norms(part.reshape(1), index, group), "blk", group)
+    inverse = jnp.concatenate(pieces, axis=0)
+    turn = part * pieces[0].shape[0]
     neg_acc, neg_sum = negatives(all_neg, queries, index)
     rows, targets = prep(me.reshape(1), all_meta, shard, cands)
     rows, neg_acc = lax.optimization_barrier((rows, neg_acc))
@@ -419,7 +445,7 @@
     for step in list(range(1, owners)) + [0]:
         source = lax.rem(me + step, owners)
         message = pairs(
-            source.reshape(1), rows, targets, all_queries[step], inverse, index, cands, room
+            jnp.stack([source, turn]), rows, targets, all_queries[step], inverse, index, cands, room
         )
         if step:
             message = lax.ppermute(

time: 261 us -> 200 us (0.77)
  the two profiles are of different devices: /device:TPU:0 before, /device:TPU:20 now
where the time goes in v1:
time: 200 us; the launch traced here: 198 us
  Pallas kernels  123 us (62%)
  blocking collectives  28.8 us (14%)
  local copies, waits for them, and re-layouts  23.3 us (12%)
  starting transfers between devices  12.3 us (6%)
  other arithmetic  9.8 us (5%)
    pallas_call x8, Pallas kernels, pairs(): pl.pallas_call(functools.partial(pair_kernel, cands=cands), grid_spec=plt...  97.7 us
    all_gather x1, blocking collectives, on_device(): all_meta = lax.all_gather(meta, 'corpus', axis=0, tiled=True)  28.8 us
    unnamed x18, local copies, waits for them, and re-layouts  23.1 us
    pallas_call x1, Pallas kernels, negatives(): pl.pallas_call(functools.partial(neg_kernel, tokens=tokens), in_specs=[pl...  15.1 us
    ppermute x13, starting transfers between devices, from_step(): lax.ppermute(value, axis, [((i + step) % size, i) for i in range(size)])  11.7 us
    pallas_call x1, Pallas kernels, norms(): pl.pallas_call(norm_kernel, in_specs=[pl.BlockSpec(memory_space=pltpu.SME...  5.37 us
    pallas_call x1, Pallas kernels, prep(): pl.pallas_call(functools.partial(prep_kernel, shard=shard, cands=cands),...  4.98 us
    mul x1, other arithmetic, on_device(): unit * jnp.sum(unit * pulled, axis=-1, keepdims=True)  4.12 us
  transfers between devices with their start and end apart: 20, of which 0 were waited for; matrix products, arithmetic and copies ran while one was open for 1% of the time, Pallas kernels for 62%

profile of v1, /device:TPU:20, one launch (start us, length us, event | category | flops | bytes accessed | tf_op | source)
XLA Modules:
  0.0 198.4 jit_solution(15904466067237943939)
XLA Ops:
  0.6 1.6 collective-permute-start.1
  2.2 0.5 collective-permute-start.2
  2.7 5.8 %copy-done = bf16[512,128,128]{2,1,0:T(8,128)(2,1)S(1)} copy-done((bf16[512,128,128]{2,1,0:T(8,128)(2,1)S(1)}, bf16[512,128,128]{2,1,0:T(8,128)(2,1)}, u32[]{:S(2)}) %copy-start) | copy-done | bytes 16777240
  8.5 5.4 %norms.1 = f32[128,128]{1,0:T(8,128)S(1)} custom-call(s32[1]{0:T(128)} %bitcast.6.part_ref, bf16[512,128,128]{2,1,0:T(8,128)(2,1)S(1)} %copy-done), custom_call_target="tpu_custom_call" | custom-call | flops 67108864 | bytes 4194304 | tf_op jit(solution)/shard_map/norms/pallas_call | solution.py:68
  13.9 0.8 collective-permute-start.6
  14.7 0.8 collective-permute-start.5
  16.4 0.6 add_sqrt_fusion
  17.0 28.8 %all_gather.3.meta_ref = f32[128,128]{1,0:T(8,128)S(1)} all-gather(f32[16,128]{1,0:T(8,128)S(1)} %pad_maximum_fusion.1), channel_id=1, replica_groups=mesh['corpus'=8,'blk'=4] {'corpus'}, dimensions={0}, use_global_device_ids=true | all-gather | bytes 73728 | tf_op jit(solution)/shard_map/all_gather | solution.py:433
  45.8 5.0 %prep.1 = (s32[128,128]{1,0:T(8,128)S(1)}, f32[2048,128]{1,0:T(8,128)S(1)}) custom-call(s32[1]{0:T(128)} %bitcast.2.me_ref, f32[128,128]{1,0:T(8,128)S(1)} %all_gather.3.meta_ref), custom_call_target="tpu_custom_call" | custom-call | tf_op jit(solution)/shard_map/prep/pallas_call | solution.py:137
  50.9 0.6 collective-permute-start.18
  51.5 3.3 %collective-permute-start.16 = (bf16[16,32,128]{2,1,0:T(8,128)(2,1)S(1)}, bf16[16,32,128]{2,1,0:T(8,128)(2,1)S(1)}, u32[]{:S(2)}, u32[]{:S(2)}) collective-permute-start(bf16[16,32,128]{2,1,0:T(8,128)(2,1)S(1)} %copy-done.4), channel_id=1, source_target_pairs={{24,0},{28,4},{0,8},{4,12},{8,16},{12,20},{16,24},{20,28},{25,1},{... | collective-permute-start | bytes 393224 | tf_op jit(solution)/shard_map/ppermute | solution.py:425
  54.8 5.8 %copy-done.1 = bf16[512,128,128]{2,1,0:T(8,128)(2,1)S(1)} copy-done((bf16[512,128,128]{2,1,0:T(8,128)(2,1)S(1)}, bf16[512,128,128]{2,1,0:T(8,128)(2,1)}, u32[]{:S(2)}) %copy-start.1) | copy-done | bytes 16777240
  60.6 15.1 %negatives.1 = (f32[512,128]{1,0:T(8,128)S(1)}, f32[8,512]{1,0:T(8,128)S(1)}) custom-call(s32[96]{0:T(128)S(1)} %reshape.49.rows_ref, bf16[512,128]{1,0:T(8,128)(2,1)S(1)} %bitcast.48, bf16[512,128,128]{2,1,0:T(8,128)(2,1)S(1)} %copy-done.1), custom_call_target="tpu_custom_call" | custom-call | flops 3221225472 | bytes 3145728 | tf_op jit(solution)/shard_map/negatives/pallas_call | solution.py:385
  75.7 0.2 collective-permute-start.14
  75.9 3.8 %collective-permute-start.12 = (bf16[16,32,128]{2,1,0:T(8,128)(2,1)S(1)}, bf16[16,32,128]{2,1,0:T(8,128)(2,1)S(1)}, u32[]{:S(2)}, u32[]{:S(2)}) collective-permute-start(bf16[16,32,128]{2,1,0:T(8,128)(2,1)S(1)} %copy-done.4), channel_id=1, source_target_pairs={{16,0},{20,4},{24,8},{28,12},{0,16},{4,20},{8,24},{12,28},{17,1},{... | collective-permute-start | bytes 393224 | tf_op jit(solution)/shard_map/ppermute | solution.py:425
  79.8 5.8 %copy-done.2 = bf16[512,128,128]{2,1,0:T(8,128)(2,1)S(1)} copy-done((bf16[512,128,128]{2,1,0:T(8,128)(2,1)S(1)}, bf16[512,128,128]{2,1,0:T(8,128)(2,1)}, u32[]{:S(2)}) %copy-start.2) | copy-done | bytes 16777240
  85.6 12.2 %pairs.14 = bf16[1072,128]{1,0:T(8,128)(2,1)S(1)} custom-call(s32[2]{0:T(128)S(1)} %pad_add_fusion.7.source_ref, s32[128,128]{1,0:T(8,128)S(1)} %get-tuple-element.13.rows_ref, f32[2048,128]{1,0:T(8,128)S(1)} %get-tuple-element.14.target_ref, bf16[16,32,128]{2,1,0:T(8,128)(2,1)S(1)} %collective-permute-done.18.queries_ref, ...), custom_call_target="tpu_custom_call" | custom-call | flops 805306368 | bytes 8388608 | tf_op jit(solution)/shard_map/pairs/pallas_call | solution.py:284
  97.9 12.2 %pairs.8 = bf16[1072,128]{1,0:T(8,128)(2,1)S(1)} custom-call(s32[2]{0:T(128)S(1)} %pad_add_fusion.1.source_ref, s32[128,128]{1,0:T(8,128)S(1)} %get-tuple-element.13.rows_ref, f32[2048,128]{1,0:T(8,128)S(1)} %get-tuple-element.14.target_ref, bf16[16,32,128]{2,1,0:T(8,128)(2,1)S(1)} %collective-permute-done.3.queries_ref, ...), custom_call_target="tpu_custom_call" | custom-call | flops 805306368 | bytes 8388608 | tf_op jit(solution)/shard_map/pairs/pallas_call | solution.py:284
  110.2 12.2 %pairs.9 = bf16[1072,128]{1,0:T(8,128)(2,1)S(1)} custom-call(s32[2]{0:T(128)S(1)} %pad_add_fusion.2.source_ref, s32[128,128]{1,0:T(8,128)S(1)} %get-tuple-element.13.rows_ref, f32[2048,128]{1,0:T(8,128)S(1)} %get-tuple-element.14.target_ref, bf16[16,32,128]{2,1,0:T(8,128)(2,1)S(1)} %collective-permute-done.8.queries_ref, ...), custom_call_target="tpu_custom_call" | custom-call | flops 805306368 | bytes 8388608 | tf_op jit(solution)/shard_map/pairs/pallas_call | solution.py:284
  122.5 12.2 %pairs.10 = bf16[1072,128]{1,0:T(8,128)(2,1)S(1)} custom-call(s32[2]{0:T(128)S(1)} %pad_add_fusion.3.source_ref, s32[128,128]{1,0:T(8,128)S(1)} %get-tuple-element.13.rows_ref, f32[2048,128]{1,0:T(8,128)S(1)} %get-tuple-element.14.target_ref, bf16[16,32,128]{2,1,0:T(8,128)(2,1)S(1)} %collective-permute-done.10.queries_ref, ...), custom_call_target="tpu_custom_call" | custom-call | flops 805306368 | bytes 8388608 | tf_op jit(solution)/shard_map/pairs/pallas_call | solution.py:284
  134.7 0.2 collective-permute-start.11
  134.9 12.2 %pairs.11 = bf16[1072,128]{1,0:T(8,128)(2,1)S(1)} custom-call(s32[2]{0:T(128)S(1)} %pad_add_fusion.4.source_ref, s32[128,128]{1,0:T(8,128)S(1)} %get-tuple-element.13.rows_ref, f32[2048,128]{1,0:T(8,128)S(1)} %get-tuple-element.14.target_ref, bf16[16,32,128]{2,1,0:T(8,128)(2,1)S(1)} %collective-permute-done.12.queries_ref, ...), custom_call_target="tpu_custom_call" | custom-call | flops 805306368 | bytes 8388608 | tf_op jit(solution)/shard_map/pairs/pallas_call | solution.py:284
  147.3 12.2 %pairs.12 = bf16[1072,128]{1,0:T(8,128)(2,1)S(1)} custom-call(s32[2]{0:T(128)S(1)} %pad_add_fusion.5.source_ref, s32[128,128]{1,0:T(8,128)S(1)} %get-tuple-element.13.rows_ref, f32[2048,128]{1,0:T(8,128)S(1)} %get-tuple-element.14.target_ref, bf16[16,32,128]{2,1,0:T(8,128)(2,1)S(1)} %collective-permute-done.14.queries_ref, ...), custom_call_target="tpu_custom_call" | custom-call | flops 805306368 | bytes 8388608 | tf_op jit(solution)/shard_map/pairs/pallas_call | solution.py:284
  159.6 12.2 %pairs.13 = bf16[1072,128]{1,0:T(8,128)(2,1)S(1)} custom-call(s32[2]{0:T(128)S(1)} %pad_add_fusion.6.source_ref, s32[128,128]{1,0:T(8,128)S(1)} %get-tuple-element.13.rows_ref, f32[2048,128]{1,0:T(8,128)S(1)} %get-tuple-element.14.target_ref, bf16[16,32,128]{2,1,0:T(8,128)(2,1)S(1)} %collective-permute-done.16.queries_ref, ...), custom_call_target="tpu_custom_call" | custom-call | flops 805306368 | bytes 8388608 | tf_op jit(solution)/shard_map/pairs/pallas_call | solution.py:284
  172.1 5.8 %copy-done.3 = bf16[512,128,128]{2,1,0:T(8,128)(2,1)S(1)} copy-done((bf16[512,128,128]{2,1,0:T(8,128)(2,1)S(1)}, bf16[512,128,128]{2,1,0:T(8,128)(2,1)}, u32[]{:S(2)}) %copy-start.3) | copy-done | bytes 16777240
  177.9 12.2 %pairs.15 = bf16[1072,128]{1,0:T(8,128)(2,1)S(1)} custom-call(s32[2]{0:T(128)S(1)} %pad_add_fusion.8.source_ref, s32[128,128]{1,0:T(8,128)S(1)} %get-tuple-element.13.rows_ref, f32[2048,128]{1,0:T(8,128)S(1)} %get-tuple-element.14.target_ref, bf16[16,32,128]{2,1,0:T(8,128)(2,1)S(1)} %copy-done.4, f32[512,128]{1,0:T(8,128)S(1)} %pad_maximum_fusion.inverse_ref, ...), custom_call_target="tpu_custom_call" | custom-call | flops 805306368 | bytes 8388608 | tf_op jit(solution)/shard_map/pairs/pallas_call | solution.py:284
  190.2 0.8 convert_add_fusion.1
  191.0 0.2 fusion.11
  191.2 0.9 multiply_reduce_fusion.1
  192.1 0.5 sub.19
  192.6 1.7 convert_add_fusion
  194.3 4.1 %fusion.3 = f32[16,32,128]{2,1,0:T(8,128)} fusion(bf16[16,32,128]{2,1,0:T(8,128)(2,1)S(1)} %copy-done.4, f32[16,32]{1,0:T(8,128)} %add_sqrt_fusion, f32[16,2,32,128]{3,2,1,0:T(8,128)S(1)} %bitcast.50, f32[16]{0:T(128)S(1)} %get-tuple-element.18, f32[16,32,128]{2,1,0:T(8,128)S(1)} %bitcast.49), kind=kOutput, calls=%fused_computation.3 | output fusion | flops 918143 | bytes 2114560 | tf_op jit(solution)/shard_map/mul | solution.py:467
  (64 shorter events, 1.8 us)
Async XLA Ops:
  0.6 54.1 %copy-start.8 = (s32[1,24]{1,0:T(1,128)S(1)}, s32[1,24]{1,0:T(1,128)}, u32[]{:S(2)}) copy-start(s32[1,24]{1,0:T(1,128)} %param.10) | copy-start | bytes 292
  0.6 50.2 %collective-permute-start.1 = (s32[1,24]{1,0:T(1,128)}, s32[1,24]{1,0:T(1,128)S(1)}, u32[]{:S(2)}, u32[]{:S(2)}) collective-permute-start(s32[1,24]{1,0:T(1,128)} %param.10), channel_id=1, source_target_pairs={{2,0},{3,1},{0,2},{1,3},{6,4},{7,5},{4,6},{5,7},{10,8},{11,9},{8,1... | collective-permute-start | bytes 296 | tf_op jit(solution)/shard_map/ppermute | solution.py:425
  2.2 48.7 %collective-permute-start = (s32[1,24]{1,0:T(1,128)}, s32[1,24]{1,0:T(1,128)S(1)}, u32[]{:S(2)}, u32[]{:S(2)}) collective-permute-start(s32[1,24]{1,0:T(1,128)} %param.10), channel_id=1, source_target_pairs={{1,0},{2,1},{3,2},{0,3},{5,4},{6,5},{7,6},{4,7},{9,8},{10,9},{11,1... | collective-permute-start | bytes 296 | tf_op jit(solution)/shard_map/ppermute | solution.py:425
  2.2 49.3 %collective-permute-start.2 = (s32[1,24]{1,0:T(1,128)}, s32[1,24]{1,0:T(1,128)S(1)}, u32[]{:S(2)}, u32[]{:S(2)}) collective-permute-start(s32[1,24]{1,0:T(1,128)} %param.10), channel_id=1, source_target_pairs={{3,0},{0,1},{1,2},{2,3},{7,4},{4,5},{5,6},{6,7},{11,8},{8,9},{9,10... | collective-permute-start | bytes 296 | tf_op jit(solution)/shard_map/ppermute | solution.py:425
  2.7 5.8 %copy-start = (bf16[512,128,128]{2,1,0:T(8,128)(2,1)S(1)}, bf16[512,128,128]{2,1,0:T(8,128)(2,1)}, u32[]{:S(2)}) copy-start(bf16[512,128,128]{2,1,0:T(8,128)(2,1)} %index_ref.19) | copy-start | bytes 50331652
  8.5 7.6 %copy-start.5 = (f32[16,64]{1,0:T(8,128)S(1)}, f32[16,64]{1,0:T(8,128)}, u32[]{:S(2)}) copy-start(f32[16,64]{1,0:T(8,128)} %param.11) | copy-start | bytes 12292
  8.5 7.7 %copy-start.6 = (s32[16,64]{1,0:T(8,128)S(1)}, s32[16,64]{1,0:T(8,128)}, u32[]{:S(2)}) copy-start(s32[16,64]{1,0:T(8,128)} %param.9) | copy-start | bytes 12292
  8.5 7.7 %copy-start.7 = (s32[16,64,1]{1,2,0:T(1,128)S(1)}, s32[16,64,1]{1,2,0:T(1,128)}, u32[]{:S(2)}) copy-start(s32[16,64,1]{1,2,0:T(1,128)} %param.8) | copy-start | bytes 12292
  8.5 7.8 %copy-start.4 = (bf16[16,32,128]{2,1,0:T(8,128)(2,1)S(1)}, bf16[16,32,128]{2,1,0:T(8,128)(2,1)}, u32[]{:S(2)}) copy-start(bf16[16,32,128]{2,1,0:T(8,128)(2,1)} %queries_ref) | copy-start | bytes 393220
  13.9 61.8 %collective-permute-start.6 = (f32[128,128]{1,0:T(8,128)S(1)}, f32[128,128]{1,0:T(8,128)S(1)}, u32[]{:S(2)}, u32[]{:S(2)}) collective-permute-start(f32[128,128]{1,0:T(8,128)S(1)} %norms.1), channel_id=1, source_target_pairs={{3,0},{0,1},{1,2},{2,3},{7,4},{4,5},{5,6},{6,7},{11,8},{8,9},{9,10... | collective-permute-start | bytes 196616 | tf_op jit(solution)/shard_map/ppermute | solution.py:425
  14.7 61.2 %collective-permute-start.5 = (f32[128,128]{1,0:T(8,128)S(1)}, f32[128,128]{1,0:T(8,128)S(1)}, u32[]{:S(2)}, u32[]{:S(2)}) collective-permute-start(f32[128,128]{1,0:T(8,128)S(1)} %norms.1), channel_id=1, source_target_pairs={{2,0},{3,1},{0,2},{1,3},{6,4},{7,5},{4,6},{5,7},{10,8},{11,9},{8,1... | collective-permute-start | bytes 196616 | tf_op jit(solution)/shard_map/ppermute | solution.py:425
  50.8 28.9 %collective-permute-start.4 = (f32[128,128]{1,0:T(8,128)S(1)}, f32[128,128]{1,0:T(8,128)S(1)}, u32[]{:S(2)}, u32[]{:S(2)}) collective-permute-start(f32[128,128]{1,0:T(8,128)S(1)} %norms.1), channel_id=1, source_target_pairs={{1,0},{2,1},{3,2},{0,3},{5,4},{6,5},{7,6},{4,7},{9,8},{10,9},{11,1... | collective-permute-start | bytes 196616 | tf_op jit(solution)/shard_map/ppermute | solution.py:425
  50.9 28.8 %collective-permute-start.18 = (bf16[16,32,128]{2,1,0:T(8,128)(2,1)S(1)}, bf16[16,32,128]{2,1,0:T(8,128)(2,1)S(1)}, u32[]{:S(2)}, u32[]{:S(2)}) collective-permute-start(bf16[16,32,128]{2,1,0:T(8,128)(2,1)S(1)} %copy-done.4), channel_id=1, source_target_pairs={{28,0},{0,4},{4,8},{8,12},{12,16},{16,20},{20,24},{24,28},{29,1},{... | collective-permute-start | bytes 393224 | tf_op jit(solution)/shard_map/ppermute | solution.py:425
  51.5 108.0 %collective-permute-start.16 = (bf16[16,32,128]{2,1,0:T(8,128)(2,1)S(1)}, bf16[16,32,128]{2,1,0:T(8,128)(2,1)S(1)}, u32[]{:S(2)}, u32[]{:S(2)}) collective-permute-start(bf16[16,32,128]{2,1,0:T(8,128)(2,1)S(1)} %copy-done.4), channel_id=1, source_target_pairs={{24,0},{28,4},{0,8},{4,12},{8,16},{12,20},{16,24},{20,28},{25,1},{... | collective-permute-start | bytes 393224 | tf_op jit(solution)/shard_map/ppermute | solution.py:425
  54.8 5.8 %copy-start.1 = (bf16[512,128,128]{2,1,0:T(8,128)(2,1)S(1)}, bf16[512,128,128]{2,1,0:T(8,128)(2,1)}, u32[]{:S(2)}) copy-start(bf16[512,128,128]{2,1,0:T(8,128)(2,1)} %index_ref.19) | copy-start | bytes 50331652
  75.7 71.5 %collective-permute-start.14 = (bf16[16,32,128]{2,1,0:T(8,128)(2,1)S(1)}, bf16[16,32,128]{2,1,0:T(8,128)(2,1)S(1)}, u32[]{:S(2)}, u32[]{:S(2)}) collective-permute-start(bf16[16,32,128]{2,1,0:T(8,128)(2,1)S(1)} %copy-done.4), channel_id=1, source_target_pairs={{20,0},{24,4},{28,8},{0,12},{4,16},{8,20},{12,24},{16,28},{21,1},{... | collective-permute-start | bytes 393224 | tf_op jit(solution)/shard_map/ppermute | solution.py:425
  75.9 58.8 %collective-permute-start.12 = (bf16[16,32,128]{2,1,0:T(8,128)(2,1)S(1)}, bf16[16,32,128]{2,1,0:T(8,128)(2,1)S(1)}, u32[]{:S(2)}, u32[]{:S(2)}) collective-permute-start(bf16[16,32,128]{2,1,0:T(8,128)(2,1)S(1)} %copy-done.4), channel_id=1, source_target_pairs={{16,0},{20,4},{24,8},{28,12},{0,16},{4,20},{8,24},{12,28},{17,1},{... | collective-permute-start | bytes 393224 | tf_op jit(solution)/shard_map/ppermute | solution.py:425
  79.7 18.1 %collective-permute-start.3 = (bf16[16,32,128]{2,1,0:T(8,128)(2,1)S(1)}, bf16[16,32,128]{2,1,0:T(8,128)(2,1)S(1)}, u32[]{:S(2)}, u32[]{:S(2)}) collective-permute-start(bf16[16,32,128]{2,1,0:T(8,128)(2,1)S(1)} %copy-done.4), channel_id=1, source_target_pairs={{4,0},{8,4},{12,8},{16,12},{20,16},{24,20},{28,24},{0,28},{5,1},{9... | collective-permute-start | bytes 393224 | tf_op jit(solution)/shard_map/ppermute | solution.py:425
  79.7 30.4 %collective-permute-start.8 = (bf16[16,32,128]{2,1,0:T(8,128)(2,1)S(1)}, bf16[16,32,128]{2,1,0:T(8,128)(2,1)S(1)}, u32[]{:S(2)}, u32[]{:S(2)}) collective-permute-start(bf16[16,32,128]{2,1,0:T(8,128)(2,1)S(1)} %copy-done.4), channel_id=1, source_target_pairs={{8,0},{12,4},{16,8},{20,12},{24,16},{28,20},{0,24},{4,28},{9,1},{1... | collective-permute-start | bytes 393224 | tf_op jit(solution)/shard_map/ppermute | solution.py:425
  79.8 5.8 %copy-start.2 = (bf16[512,128,128]{2,1,0:T(8,128)(2,1)S(1)}, bf16[512,128,128]{2,1,0:T(8,128)(2,1)}, u32[]{:S(2)}) copy-start(bf16[512,128,128]{2,1,0:T(8,128)(2,1)} %index_ref.19) | copy-start | bytes 50331652
  97.8 24.6 %collective-permute-start.10 = (bf16[16,32,128]{2,1,0:T(8,128)(2,1)S(1)}, bf16[16,32,128]{2,1,0:T(8,128)(2,1)S(1)}, u32[]{:S(2)}, u32[]{:S(2)}) collective-permute-start(bf16[16,32,128]{2,1,0:T(8,128)(2,1)S(1)} %copy-done.4), channel_id=1, source_target_pairs={{12,0},{16,4},{20,8},{24,12},{28,16},{0,20},{4,24},{8,28},{13,1},{... | collective-permute-start | bytes 393224 | tf_op jit(solution)/shard_map/ppermute | solution.py:425
  110.1 61.7 %collective-permute-start.7 = (bf16[1072,128]{1,0:T(8,128)(2,1)S(1)}, bf16[1072,128]{1,0:T(8,128)(2,1)}, u32[]{:S(2)}, u32[]{:S(2)}) collective-permute-start(bf16[1072,128]{1,0:T(8,128)(2,1)S(1)} %pairs.8), channel_id=1, source_target_pairs={{0,4},{4,8},{8,12},{12,16},{16,20},{20,24},{24,28},{28,0},{1,5},{5... | collective-permute-start | bytes 823304 | tf_op jit(solution)/shard_map/ppermute | solution.py:451
  122.4 49.5 %collective-permute-start.9 = (bf16[1072,128]{1,0:T(8,128)(2,1)S(1)}, bf16[1072,128]{1,0:T(8,128)(2,1)}, u32[]{:S(2)}, u32[]{:S(2)}) collective-permute-start(bf16[1072,128]{1,0:T(8,128)(2,1)S(1)} %pairs.9), channel_id=1, source_target_pairs={{0,8},{4,12},{8,16},{12,20},{16,24},{20,28},{24,0},{28,4},{1,9},{5... | collective-permute-start | bytes 823304 | tf_op jit(solution)/shard_map/ppermute | solution.py:451
  134.7 55.4 %collective-permute-start.11 = (bf16[1072,128]{1,0:T(8,128)(2,1)S(1)}, bf16[1072,128]{1,0:T(8,128)(2,1)}, u32[]{:S(2)}, u32[]{:S(2)}) collective-permute-start(bf16[1072,128]{1,0:T(8,128)(2,1)S(1)} %pairs.10), channel_id=1, source_target_pairs={{0,12},{4,16},{8,20},{12,24},{16,28},{20,0},{24,4},{28,8},{1,13},{... | collective-permute-start | bytes 823304 | tf_op jit(solution)/shard_map/ppermute | solution.py:451
  147.2 42.9 %collective-permute-start.13 = (bf16[1072,128]{1,0:T(8,128)(2,1)S(1)}, bf16[1072,128]{1,0:T(8,128)(2,1)}, u32[]{:S(2)}, u32[]{:S(2)}) collective-permute-start(bf16[1072,128]{1,0:T(8,128)(2,1)S(1)} %pairs.11), channel_id=1, source_target_pairs={{0,16},{4,20},{8,24},{12,28},{16,0},{20,4},{24,8},{28,12},{1,17},{... | collective-permute-start | bytes 823304 | tf_op jit(solution)/shard_map/ppermute | solution.py:451
  159.5 30.6 %collective-permute-start.15 = (bf16[1072,128]{1,0:T(8,128)(2,1)S(1)}, bf16[1072,128]{1,0:T(8,128)(2,1)}, u32[]{:S(2)}, u32[]{:S(2)}) collective-permute-start(bf16[1072,128]{1,0:T(8,128)(2,1)S(1)} %pairs.12), channel_id=1, source_target_pairs={{0,20},{4,24},{8,28},{12,0},{16,4},{20,8},{24,12},{28,16},{1,21},{... | collective-permute-start | bytes 823304 | tf_op jit(solution)/shard_map/ppermute | solution.py:451
  171.8 18.4 %collective-permute-start.17 = (bf16[1072,128]{1,0:T(8,128)(2,1)S(1)}, bf16[1072,128]{1,0:T(8,128)(2,1)}, u32[]{:S(2)}, u32[]{:S(2)}) collective-permute-start(bf16[1072,128]{1,0:T(8,128)(2,1)S(1)} %pairs.13), channel_id=1, source_target_pairs={{0,24},{4,28},{8,0},{12,4},{16,8},{20,12},{24,16},{28,20},{1,25},{... | collective-permute-start | bytes 823304 | tf_op jit(solution)/shard_map/ppermute | solution.py:451
  171.9 18.3 %collective-permute-start.19 = (bf16[1072,128]{1,0:T(8,128)(2,1)S(1)}, bf16[1072,128]{1,0:T(8,128)(2,1)}, u32[]{:S(2)}, u32[]{:S(2)}) collective-permute-start(bf16[1072,128]{1,0:T(8,128)(2,1)S(1)} %pairs.14), channel_id=1, source_target_pairs={{0,28},{4,0},{8,4},{12,8},{16,12},{20,16},{24,20},{28,24},{1,29},{... | collective-permute-start | bytes 823304 | tf_op jit(solution)/shard_map/ppermute | solution.py:451
  172.1 5.8 %copy-start.3 = (bf16[512,128,128]{2,1,0:T(8,128)(2,1)S(1)}, bf16[512,128,128]{2,1,0:T(8,128)(2,1)}, u32[]{:S(2)}) copy-start(bf16[512,128,128]{2,1,0:T(8,128)(2,1)} %index_ref.19) | copy-start | bytes 50331652

commit v2 on v1

--- a/solution.py
+++ b/solution.py
@@ -13,9 +13,12 @@
 LOG2E = 1.4426950408889634
 GROUP = 4
 UNITS = 8
+LOADS = 8
+LOAD_STEP = 16
 NEG_STEP = 8
-NEG_CHUNK = 96
-MIB = 1024 * 1024
+NEG_CHUNK = 24
+SOURCES = 2
+VMEM_LIMIT = 12 * 1024 * 1024
 LAST = (((1,), (1,)), ((), ()))
 
 
@@ -41,46 +44,39 @@
     return (wide / radius).astype(jnp.bfloat16)
 
 
-def norm_kernel(part_ref, index_ref, out_ref):
-    count, tokens = out_ref.shape
-    dim = index_ref.shape[2]
-    base = part_ref[0] * count
-    ones = jnp.ones((8, dim), jnp.bfloat16)
-    sub = lax.broadcasted_iota(jnp.int32, (8, tokens), 0)
-
-    def body(step, carry):
-        squares = jnp.zeros((8, tokens), jnp.float32)
-        for k in range(8):
-            tile = index_ref[base + step * 8 + k].astype(jnp.float32)
-            tile = tile * tile
-            high = tile.astype(jnp.bfloat16)
-            low = (tile - high.astype(jnp.float32)).astype(jnp.bfloat16)
-            squares = jnp.where(sub == k, dot_last(ones, high) + dot_last(ones, low), squares)
-        out_ref[pl.ds(pl.multiple_of(step * 8, 8), 8), :] = lax.rsqrt(squares + epsilon)
-        return carry
-
-    lax.fori_loop(0, count // 8, body, 0, unroll=2)
-
-
-def norms(part, index, parts):
-    tokens, dim = index.shape[1:]
-    count = index.shape[0] // parts
-    return pl.pallas_call(
-        norm_kernel,
-        in_specs=[pl.BlockSpec(memory_space=pltpu.SMEM), pl.BlockSpec(memory_space=pltpu.VMEM)],
-        out_specs=pl.BlockSpec(memory_space=pltpu.VMEM),
-        out_shape=jax.ShapeDtypeStruct((count, tokens), jnp.float32),
-        compiler_params=pltpu.CompilerParams(vmem_limit_bytes=8 * MIB),
-        cost_estimate=pl.CostEstimate(
-            flops=32 * count * tokens * dim,
-            bytes_accessed=2 * count * tokens * dim,
-            transcendentals=count * tokens,
-        ),
-        name="norms",
-    )(part, index)
-
-
-def prep_kernel(me_ref, meta_ref, rows_ref, target_ref, value_ref, place_ref, result_ref, *, shard, cands):
+def load_shard(index_ref, tiles_ref, turned_ref, inverse_ref, sems):
+    count = index_ref.shape[0]
+    chunk = count // LOADS
+
+    def copy(part):
+        at = pl.ds(part * chunk, chunk)
+        return pltpu.make_async_copy(index_ref.at[at], tiles_ref.at[at], sems.at[part])
+
+    for part in range(LOADS):
+        copy(part).start()
+
+    for part in range(LOADS):
+        copy(part).wait()
+
+        def body(step, carry):
+            first = part * chunk + step * LOAD_STEP
+            squares = []
+            turned = []
+            for k in range(LOAD_STEP):
+                tile = tiles_ref[first + k].T
+                turned.append(tile)
+                wide = tile.astype(jnp.float32)
+                squares.append(jnp.sum(wide * wide, axis=0, keepdims=True))
+            for k in range(LOAD_STEP):
+                turned_ref[first + k] = turned[k]
+            at = pl.ds(pl.multiple_of(first, LOAD_STEP), LOAD_STEP)
+            inverse_ref[at, :] = lax.rsqrt(jnp.concatenate(squares, axis=0) + epsilon)
+            return carry
+
+        lax.fori_loop(0, chunk // LOAD_STEP, body, 0)
+
+
+def prep_kernel(me_ref, meta_ref, index_ref, turned_ref, rows_ref, target_ref, value_ref, place_ref, result_ref, *, shard, cands):
     count = meta_ref.shape[0]
     code = meta_ref[:, :cands]
     owner = jnp.floor((code + 0.5) * (1.0 / shard))
@@ -131,7 +127,7 @@
         )
 
 
-def prep(me, meta, shard, cands):
+def prep(me, meta, index, turned, shard, cands):
     count = meta.shape[0]
     wide = 128
     return pl.pallas_call(
@@ -139,6 +135,8 @@
         in_specs=[
             pl.BlockSpec(memory_space=pltpu.SMEM),
             pl.BlockSpec(memory_space=pltpu.VMEM),
+            pl.BlockSpec(memory_space=pltpu.VMEM),
+            pl.BlockSpec(memory_space=pltpu.VMEM),
         ],
         out_specs=[pl.BlockSpec(memory_space=pltpu.VMEM)] * 2,
         out_shape=[
@@ -150,14 +148,16 @@
             pltpu.VMEM((count, wide), jnp.float32),
             pltpu.VMEM((count * 8, wide), jnp.float32),
         ],
-        compiler_params=pltpu.CompilerParams(vmem_limit_bytes=12 * MIB),
+        compiler_params=pltpu.CompilerParams(vmem_limit_bytes=VMEM_LIMIT),
+        cost_estimate=pl.CostEstimate(flops=count * wide, bytes_accessed=count * wide, transcendentals=0),
         name="prep",
-    )(me, meta)
-
-
-def pair_kernel(source_ref, rows_ref, target_ref, queries_ref, inverse_ref, index_ref, out_ref,
-                units_ref, unit_ref, acc_ref, total_ref, left_ref, right_ref, back_ref, raw_ref, *, cands):
-    count, tokens, dim = queries_ref.shape
+    )(me, meta, index, turned)
+
+
+def pair_kernel(source_ref, rows_ref, target_ref, queries_ref, inverse_ref, index_ref, turned_ref, *refs, cands, sources):
+    out_refs = refs[:sources]
+    (units_ref, unit_ref, acc_ref, total_ref, left_ref, right_ref, back_ref, raw_ref) = refs[sources:]
+    count, tokens, dim = unit_ref.shape
     wide = rows_ref.shape[1]
     per_query = cands // GROUP
     slots = count * per_query
@@ -177,20 +177,19 @@
         return slot, q, jnp.bitwise_and(slot, per_query - 1) * GROUP
 
     for q in range(count):
-        unit_ref[q] = rounded_queries(queries_ref[q])
+        unit_ref[q] = rounded_queries(queries_ref[0, q])
     acc_ref[...] = jnp.zeros_like(acc_ref)
     ones = jnp.ones((8, wide), jnp.bfloat16)
 
-    def tiles_of(number):
+    def tiles_of(number, ref):
         _, q, base = entry(number)
-        rows = [rows_ref[q, base + g] for g in range(GROUP)]
-        return q, rows, [index_ref[row] for row in rows]
+        return q, [ref[rows_ref[q, base + g]] for g in range(GROUP)]
 
     def multiply(step):
         found = []
         for u in range(UNITS):
-            q, _, tiles = tiles_of(step * UNITS + u)
-            found.append(dot_last(unit_ref[q], jnp.concatenate(tiles, axis=0)))
+            q, tiles = tiles_of(step * UNITS + u, turned_ref)
+            found.append(dot(unit_ref[q], jnp.concatenate(tiles, axis=1)))
         return found
 
     def forward(step, carry):
@@ -198,9 +197,7 @@
         for u in range(UNITS):
             _, q, base = entry(step * UNITS + u)
             for g in range(GROUP):
-                row = rows_ref[q, base + g] - source_ref[1]
-                row = row + jnp.where(row < 0, index_ref.shape[0], 0)
-                inverse = inverse_ref[pl.ds(row, 1), :]
+                inverse = inverse_ref[pl.ds(rows_ref[q, base + g], 1), :]
                 raw = raw_ref[u, :, g * wide : (g + 1) * wide]
                 expo = jnp.exp2(raw * (inverse * (LOG2E / inner_temp)))
                 expos.append(expo.astype(jnp.bfloat16))
@@ -210,7 +207,7 @@
         for u in range(UNITS):
             slot = units_ref[step * UNITS + u]
             part = slice(u * GROUP, (u + 1) * GROUP)
-            _, _, tiles = tiles_of(step * UNITS + u)
+            _, tiles = tiles_of(step * UNITS + u, index_ref)
             backs = [dot(w, tile).astype(jnp.bfloat16) for w, tile in zip(weights[part], tiles)]
             totals = dot_last(ones, jnp.concatenate(expos[part], axis=0))
             done.append((slot, totals, jnp.concatenate(backs, axis=0)))
@@ -268,32 +265,36 @@
         return carry
 
     lax.fori_loop(0, steps, backward, 0)
-    for q in range(count):
-        out_ref[pl.ds(q * 2 * tokens, 2 * tokens), :] = acc_ref[q].astype(jnp.bfloat16)
-    for k, part in enumerate(split3(sums)):
-        out_ref[pl.ds(count * 2 * tokens + k * count, count), :] = part
-
-
-def pairs(source, rows, targets, queries, inverse, index, cands, room):
-    count, tokens, dim = queries.shape
+    for k, out_ref in enumerate(out_refs):
+        @pl.when(pl.program_id(0) == k)
+        def _():
+            for q in range(count):
+                out_ref[pl.ds(q * 2 * tokens, 2 * tokens), :] = acc_ref[q].astype(jnp.bfloat16)
+            for j, part in enumerate(split3(sums)):
+                out_ref[pl.ds(count * 2 * tokens + j * count, count), :] = part
+
+
+def pairs(sources, rows, targets, queries, inverse, index, turned, cands, room):
+    count, tokens, dim = queries.shape[1:]
     wide = rows.shape[1]
     per_query = cands // GROUP
     slots = count * per_query
     most = (room + (GROUP - 1) * count) // GROUP + UNITS
     height = count * 2 * tokens + 3 * count
     return pl.pallas_call(
-        functools.partial(pair_kernel, cands=cands),
+        functools.partial(pair_kernel, cands=cands, sources=len(sources)),
         grid_spec=pltpu.PrefetchScalarGridSpec(
             num_scalar_prefetch=1,
-            grid=(1,),
+            grid=(len(sources),),
             in_specs=[
-                pl.BlockSpec((count, wide), lambda i, s: (s[0], 0), memory_space=pltpu.SMEM),
-                pl.BlockSpec((slots, wide), lambda i, s: (s[0], 0)),
+                pl.BlockSpec((count, wide), lambda i, s: (s[i], 0), memory_space=pltpu.SMEM),
+                pl.BlockSpec((slots, wide), lambda i, s: (s[i], 0)),
+                pl.BlockSpec((1, count, tokens, dim), lambda i, s: (s[i], 0, 0, 0)),
                 pl.BlockSpec(memory_space=pltpu.VMEM),
                 pl.BlockSpec(memory_space=pltpu.VMEM),
                 pl.BlockSpec(memory_space=pltpu.VMEM),
             ],
-            out_specs=pl.BlockSpec((height, dim), lambda i, s: (0, 0)),
+            out_specs=[pl.BlockSpec((height, dim), lambda i, s: (0, 0))] * len(sources),
             scratch_shapes=[
                 pltpu.SMEM((slots + per_query + 2 * UNITS,), jnp.int32),
                 pltpu.VMEM((count, tokens, dim), jnp.bfloat16),
@@ -305,26 +306,29 @@
                 pltpu.VMEM((UNITS, tokens, GROUP * wide), jnp.float32),
             ],
         ),
-        out_shape=jax.ShapeDtypeStruct((height, dim), jnp.bfloat16),
-        compiler_params=pltpu.CompilerParams(vmem_limit_bytes=12 * MIB),
+        out_shape=[jax.ShapeDtypeStruct((height, dim), jnp.bfloat16)] * len(sources),
+        compiler_params=pltpu.CompilerParams(vmem_limit_bytes=VMEM_LIMIT),
         cost_estimate=pl.CostEstimate(
-            flops=6 * room * tokens * wide * dim,
-            bytes_accessed=2 * room * wide * dim,
-            transcendentals=room * tokens * wide,
+            flops=6 * len(sources) * room * tokens * wide * dim,
+            bytes_accessed=2 * len(sources) * room * wide * dim,
+            transcendentals=len(sources) * room * tokens * wide,
         ),
         name="pairs",
-    )(source, rows, targets, queries, inverse, index)
-
-
-def neg_kernel(rows_ref, queries_ref, index_ref, acc_ref, sums_ref,
-               unit_ref, turned_ref, expo_ref, total_ref, left_ref, back_ref, *, tokens):
+    )(jnp.stack(sources), rows, targets, queries, inverse, index, turned)
+
+
+def neg_kernel(rows_ref, queries_ref, shard_ref, index_ref, turned_ref, inverse_ref, acc_ref, sums_ref,
+               sems, unit_ref, expo_ref, total_ref, left_ref, back_ref, *, tokens):
     total = rows_ref.shape[0]
     chunk = expo_ref.shape[0]
     height, dim = queries_ref.shape
     wide = index_ref.shape[1]
     lanes = 128
     half = min(height, 256)
-    unit_ref[...] = rounded_queries(queries_ref[...])
+    for c in range(height // lanes):
+        part = slice(c * lanes, (c + 1) * lanes)
+        unit_ref[:, part] = rounded_queries(queries_ref[part]).T
+    load_shard(shard_ref, index_ref, turned_ref, inverse_ref, sems)
     back_ref[...] = jnp.zeros_like(back_ref)
     sums_ref[...] = jnp.zeros_like(sums_ref)
     same = lax.broadcasted_iota(jnp.int32, (lanes, lanes), 0) // tokens == lax.broadcasted_iota(
@@ -338,15 +342,13 @@
             tiles = jnp.concatenate(
                 [index_ref[rows_ref[number * chunk + first + g]] for g in range(NEG_STEP)], axis=0
             )
-            raw = dot_last(tiles, unit_ref[...])
+            raw = dot(tiles, unit_ref[...])
             broad = tiles.astype(jnp.float32)
             inverse = lax.rsqrt(jnp.sum(broad * broad, axis=-1, keepdims=True) + epsilon)
-            flat = (broad * inverse).astype(jnp.bfloat16)
             expo = jnp.exp2(raw * (inverse * (LOG2E / inner_temp)))
             for g in range(NEG_STEP):
                 part = slice(g * wide, (g + 1) * wide)
-                turned_ref[first + g] = flat[part].T
-                expo_ref[first + g] = expo[part].astype(jnp.bfloat16)
+                expo_ref[first + g] = (expo[part] * inverse[part]).astype(jnp.bfloat16)
                 total_ref[pl.ds(first + g, 1), :] = jnp.sum(expo[part], axis=0, keepdims=True)
             return carry
 
@@ -364,7 +366,8 @@
             def backward(step, acc):
                 for g in range(NEG_STEP):
                     k = step * NEG_STEP + g
-                    acc = acc + dot(turned_ref[k], expo_ref[k, :, part]) * left_ref[pl.ds(k, 1), part]
+                    tile = turned_ref[rows_ref[number * chunk + k]]
+                    acc = acc + dot(tile, expo_ref[k, :, part]) * left_ref[pl.ds(k, 1), part]
                 return acc
 
             back_ref[:, part] = lax.fori_loop(0, chunk // NEG_STEP, backward, back_ref[:, part])
@@ -387,29 +390,77 @@
         in_specs=[
             pl.BlockSpec(memory_space=pltpu.SMEM),
             pl.BlockSpec(memory_space=pltpu.VMEM),
-            pl.BlockSpec(memory_space=pltpu.VMEM),
-        ],
-        out_specs=[pl.BlockSpec(memory_space=pltpu.VMEM)] * 2,
+            pl.BlockSpec(memory_space=pltpu.HBM),
+        ],
+        out_specs=[pl.BlockSpec(memory_space=pltpu.VMEM)] * 5,
         out_shape=[
+            pltpu.VMEM(index.shape, jnp.bfloat16),
+            pltpu.VMEM((index.shape[0], dim, wide), jnp.bfloat16),
+            pltpu.VMEM((index.shape[0], wide), jnp.float32),
             jax.ShapeDtypeStruct((height, dim), jnp.float32),
             jax.ShapeDtypeStruct((8, height), jnp.float32),
         ],
         scratch_shapes=[
-            pltpu.VMEM((height, dim), jnp.bfloat16),
-            pltpu.VMEM((chunk, dim, wide), jnp.bfloat16),
+            pltpu.SemaphoreType.DMA((LOADS,)),
+            pltpu.VMEM((dim, height), jnp.bfloat16),
             pltpu.VMEM((chunk, wide, height), jnp.bfloat16),
             pltpu.VMEM((chunk, height), jnp.float32),
             pltpu.VMEM((chunk, height), jnp.float32),
             pltpu.VMEM((dim, height), jnp.float32),
         ],
-        compiler_params=pltpu.CompilerParams(vmem_limit_bytes=28 * MIB),
+        compiler_params=pltpu.CompilerParams(vmem_limit_bytes=VMEM_LIMIT),
         cost_estimate=pl.CostEstimate(
             flops=4 * total * height * wide * dim,
             bytes_accessed=2 * total * wide * dim,
             transcendentals=total * height * wide,
         ),
         name="negatives",
-    )(rows, queries.reshape(height, dim), index)
+    )(rows, queries.reshape(height, dim), pltpu.with_memory_space_constraint(index, pltpu.HBM))
+
+
+def finish_kernel(queries_ref, teacher_ref, back_ref, sums_ref, *refs, owners):
+    messages, (loss_ref, grad_ref) = refs[:owners], refs[owners:]
+    count, tokens, dim = grad_ref.shape
+    cut = count * 2 * tokens
+    scores = jnp.zeros((count, dim), jnp.float32)
+    for message in messages:
+        for k in range(3):
+            scores = scores + message[cut + k * count : cut + (k + 1) * count, :].astype(jnp.float32)
+    totals = []
+    for q in range(count):
+        total = scores[q : q + 1, 0:1] + sums_ref[0:1, q * tokens : q * tokens + 1]
+        totals.append(total)
+        pulled = back_ref[q * tokens : (q + 1) * tokens, :]
+        right = jnp.zeros((tokens, dim), jnp.float32)
+        for message in messages:
+            pulled = pulled + message[q * 2 * tokens : (q * 2 + 1) * tokens, :].astype(jnp.float32)
+            right = right + message[(q * 2 + 1) * tokens : (q + 1) * 2 * tokens, :].astype(jnp.float32)
+        pulled = pulled / total - right
+        wide = queries_ref[q].astype(jnp.float32)
+        radius = jnp.sqrt(jnp.sum(wide * wide, axis=-1, keepdims=True) + epsilon)
+        unit = wide / radius
+        grad_ref[q] = (pulled - unit * jnp.sum(unit * pulled, axis=-1, keepdims=True)) / radius
+    spread = jnp.log(jnp.concatenate(totals, axis=0))
+    teacher = teacher_ref[...]
+    log_target = teacher - jnp.log(jnp.sum(jnp.exp(teacher), axis=-1, keepdims=True))
+    gain = jnp.sum(jnp.exp(log_target) * (log_target + spread), axis=-1, keepdims=True)
+    loss_ref[...] = gain - scores[:, dim // 2 : dim // 2 + 1] + jnp.zeros_like(loss_ref)
+
+
+def finish(queries, teacher, back, sums, messages):
+    count, tokens, dim = queries.shape
+    owners = len(messages)
+    return pl.pallas_call(
+        functools.partial(finish_kernel, owners=owners),
+        in_specs=[pl.BlockSpec(memory_space=pltpu.VMEM)] * (4 + owners),
+        out_specs=[pl.BlockSpec(memory_space=pltpu.VMEM)] * 2,
+        out_shape=[
+            jax.ShapeDtypeStruct((count, dim), jnp.float32),
+            jax.ShapeDtypeStruct((count, tokens, dim), jnp.float32),
+        ],
+        compiler_params=pltpu.CompilerParams(vmem_limit_bytes=VMEM_LIMIT),
+        name="finish",
+    )(queries, teacher, back, sums, *messages)
 
 
 def on_device(queries, index, cand_owner, cand_row, neg_row, teacher):
@@ -430,42 +481,30 @@
     code = (cand_owner[..., 0] * shard + cand_row).astype(jnp.float32)
     meta = jnp.concatenate([code, teacher], axis=1)
     all_neg = jnp.concatenate(gathered(neg_row, "blk", group), axis=0).reshape(-1)
-    all_meta = lax.all_gather(meta, "corpus", axis=0, tiled=True)
-    all_meta, sent = lax.optimization_barrier((all_meta, queries))
-    all_queries = gathered(sent, "corpus", owners)
-    index = pltpu.with_memory_space_constraint(index, pltpu.VMEM)
-    part = lax.axis_index("blk").astype(jnp.int32)
-    pieces = gathered(norms(part.reshape(1), index, group), "blk", group)
-    inverse = jnp.concatenate(pieces, axis=0)
-    turn = part * pieces[0].shape[0]
-    neg_acc, neg_sum = negatives(all_neg, queries, index)
-    rows, targets = prep(me.reshape(1), all_meta, shard, cands)
-    rows, neg_acc = lax.optimization_barrier((rows, neg_acc))
+    def told(value):
+        copies = jnp.broadcast_to(value[None], (owners,) + value.shape)
+        return lax.all_to_all(copies, "corpus", split_axis=0, concat_axis=0, tiled=True)
+
+    all_meta = told(meta).reshape(owners * count, -1)
+    all_queries = told(queries)
+    index, turned, inverse, neg_acc, neg_sum = negatives(all_neg, queries, index)
+    rows, targets = prep(me.reshape(1), all_meta, index, turned, shard, cands)
     messages = []
-    for step in list(range(1, owners)) + [0]:
-        source = lax.rem(me + step, owners)
-        message = pairs(
-            jnp.stack([source, turn]), rows, targets, all_queries[step], inverse, index, cands, room
+    order = list(range(1, owners)) + [0]
+    for first in range(0, owners, SOURCES):
+        steps = order[first : first + SOURCES]
+        sources = [lax.rem(me + step, owners) for step in steps]
+        found = pairs(
+            sources, rows, targets, all_queries, inverse, index, turned, cands, room
         )
-        if step:
-            message = lax.ppermute(
-                message, "corpus", [(i, (i + step) % owners) for i in range(owners)]
-            )
-        messages.append(message)
-    cut = count * 2 * tokens
-    both = sum(m[:cut].astype(jnp.float32) for m in messages).reshape(count, 2, tokens, dim)
-    scores = sum(m[cut:].astype(jnp.float32) for m in messages).reshape(3, count, dim).sum(axis=0)
-    total = scores[:, 0] + neg_sum[0].reshape(count, tokens)[:, 0]
-    spread = jnp.log(total)
-    log_target = teacher - jnp.log(jnp.sum(jnp.exp(teacher), axis=1, keepdims=True))
-    target = jnp.exp(log_target)
-    losses = jnp.sum(target * (log_target + spread[:, None]), axis=1) - scores[:, dim // 2]
-    pulled = (both[:, 0] + neg_acc.reshape(count, tokens, dim)) / total[:, None, None] - both[:, 1]
-    widened = queries.astype(jnp.float32)
-    radius = jnp.sqrt(jnp.sum(widened * widened, axis=-1, keepdims=True) + epsilon)
-    unit = widened / radius
-    query_grads = (pulled - unit * jnp.sum(unit * pulled, axis=-1, keepdims=True)) / radius
-    return (losses, query_grads)
+        for step, message in zip(steps, found):
+            if step:
+                message = lax.ppermute(
+                    message, "corpus", [(i, (i + step) % owners) for i in range(owners)]
+                )
+            messages.append(message)
+    losses, query_grads = finish(queries, teacher, neg_acc, neg_sum, messages)
+    return (losses[:, 0], query_grads)
 
 
 def solution(mesh):

time: 200 us -> 176 us (0.88)
  Pallas kernels: 123 us -> 66.6 us
  starting transfers between devices: 12.3 us -> 53.7 us
  blocking collectives: 28.8 us -> 9.28 us
  waiting for transfers between devices: 0.05 us -> 13.9 us
  other arithmetic: 9.8 us -> 2.45 us
  local copies, waits for them, and re-layouts: 23.3 us -> 26.7 us
    pallas_call x9 -> x5, Pallas kernels: 103 us -> 37.1 us  [the longest x4 35 us: pairs(): pl.pallas_call(functools.partial(pair_kernel, cands=cands, sources=len(so...]
    ppermute x7, starting transfers between devices: 0.61 us -> 43.7 us  [on_device(): lax.ppermute(message, 'corpus', [(i, (i + step) % owners) for i in range(...]
    all_gather x1 -> x0, blocking collectives: 28.8 us -> none  [on_device(): all_meta = lax.all_gather(meta, 'corpus', axis=0, tiled=True)]
    ppermute x7, waiting for transfers between devices: 0.02 us -> 12.7 us  [on_device(): lax.ppermute(message, 'corpus', [(i, (i + step) % owners) for i in range(...]
    pallas_call x1, Pallas kernels: 15.1 us -> 24.5 us  [negatives(): pl.pallas_call(functools.partial(neg_kernel, tokens=tokens), in_specs=[pl...]
    all_to_all x0 -> x1, blocking collectives: none -> 9.28 us  [told(): lax.all_to_all(copies, 'corpus', split_axis=0, concat_axis=0, tiled=True)]
    ppermute x13 -> x3, starting transfers between devices: 11.7 us -> 2.96 us  [from_step(): lax.ppermute(value, axis, [((i + step) % size, i) for i in range(size)])]
    all_to_all x0 -> x1, starting transfers between devices: none -> 7.01 us  [told(): lax.all_to_all(copies, 'corpus', split_axis=0, concat_axis=0, tiled=True)]
  transfers between devices with their start and end apart: 20 -> 11, of which waited for: 0 -> 3; matrix products, arithmetic and copies ran while one was open for 1% -> 1% of each run, Pallas kernels for 62% -> 32%
where the time goes in v2:
time: 176 us; the launch traced here: 173 us
  Pallas kernels  66.6 us (38%)
  starting transfers between devices  53.7 us (31%)
  local copies, waits for them, and re-layouts  26.7 us (15%)
  waiting for transfers between devices  13.9 us (8%)
  blocking collectives  9.28 us (5%)
  other arithmetic  2.45 us (1%)
    ppermute x7, starting transfers between devices, on_device(): lax.ppermute(message, 'corpus', [(i, (i + step) % owners) for i in range(...  43.7 us
    pallas_call x4, Pallas kernels, pairs(): pl.pallas_call(functools.partial(pair_kernel, cands=cands, sources=len(so...  35 us
    pallas_call x1, Pallas kernels, negatives(): pl.pallas_call(functools.partial(neg_kernel, tokens=tokens), in_specs=[pl...  24.5 us
    unnamed x14, local copies, waits for them, and re-layouts  23.9 us
    ppermute x7, waiting for transfers between devices, on_device(): lax.ppermute(message, 'corpus', [(i, (i + step) % owners) for i in range(...  12.7 us
    all_to_all x1, blocking collectives, told(): lax.all_to_all(copies, 'corpus', split_axis=0, concat_axis=0, tiled=True)  9.28 us
    all_to_all x1, starting transfers between devices, told(): lax.all_to_all(copies, 'corpus', split_axis=0, concat_axis=0, tiled=True)  7.01 us
    pallas_call x1, Pallas kernels, prep(): pl.pallas_call(functools.partial(prep_kernel, shard=shard, cands=cands),...  4.98 us
  transfers between devices with their start and end apart: 11, of which 3 were waited for; matrix products, arithmetic and copies ran while one was open for 1% of the time, Pallas kernels for 32%

profile of v2, /device:TPU:20, one launch (start us, length us, event | category | flops | bytes accessed | tf_op | source)
XLA Modules:
  0.0 173.3 jit_solution(3424879928526755392)
XLA Ops:
  0.6 0.7 fusion
  1.4 0.8 pad_maximum_fusion
  2.1 9.3 %all_to_all.10 = f32[8,16,128]{2,1,0:T(8,128)S(1)} all-to-all(f32[8,16,128]{2,1,0:T(8,128)S(1)} %broadcast_in_dim.4), channel_id=1, replica_groups=mesh['corpus'=8,'blk'=4] {'corpus'}, dimensions={0} | all-to-all | bytes 131072 | tf_op jit(solution)/shard_map/all_to_all | solution.py:486
  11.4 2.1 %broadcast_in_dim.5 = bf16[8,16,32,128]{3,2,1,0:T(8,128)(2,1)} broadcast(bf16[16,32,128]{2,1,0:T(8,128)(2,1)} %queries_ref.1), dimensions={1,2,3} | broadcast | bytes 1179648 | tf_op jit(solution)/shard_map/broadcast_in_dim | solution.py:485
  13.5 7.0 %all-to-all-start.1 = ((bf16[8,16,32,128]{3,2,1,0:T(8,128)(2,1)}), bf16[8,16,32,128]{3,2,1,0:T(8,128)(2,1)S(1)}, u32[]{:S(2)}, u32[]{:S(2)}) async-start(bf16[8,16,32,128]{3,2,1,0:T(8,128)(2,1)} %broadcast_in_dim.5), calls=%async_computation.1 | async-start | bytes 2097152 | tf_op jit(solution)/shard_map/all_to_all | solution.py:486
  20.5 1.5 collective-permute-start.1
  22.0 1.4 collective-permute-start
  23.5 0.1 pad_add_fusion.1.source_ref
  23.5 0.1 pad_add_fusion.2.source_ref
  23.8 0.4 collective-permute-done.1
  24.2 0.7 collective-permute-done
  24.9 0.7 pad_add_fusion
  25.6 0.1 reshape.20.rows_ref
  25.7 0.9 copy-done.4
  26.6 24.5 %negatives.1 = (bf16[512,128,128]{2,1,0:T(8,128)(2,1)S(1)}, bf16[512,128,128]{2,1,0:T(8,128)(2,1)S(1)}, f32[512,128]{1,0:T(8,128)S(1)}, f32[512,128]{1,0:T(8,128)S(1)}, f32[8,512]{1,0:T(8,128)S(1)}) custom-call(s32[96]{0:T(128)S(1)} %reshape.20.rows_ref, bf16[512,128]{1,0:T(8,128)(2,1)S(1)} %bitcast.16, bf16[512,128,128]{2,1,0:T(8,128)(2,1)} %shard_ref.1), custom_call_target="tpu_custom_call" | custom-call | flops 3221225472 | bytes 3145728 | tf_op jit(solution)/shard_map/negatives/pallas_call | solution.py:388
  51.1 5.0 %prep.1 = (s32[128,128]{1,0:T(8,128)S(1)}, f32[2048,128]{1,0:T(8,128)S(1)}) custom-call(s32[1]{0:T(128)} %bitcast.3.me_ref, f32[128,128]{1,0:T(8,128)S(1)} %bitcast.17, bf16[512,128,128]{2,1,0:T(8,128)(2,1)S(1)} %get-tuple-element.21.index_ref, bf16[512,128,128]{2,1,0:T(8,128)(2,1)S(1)} %get-tuple-element.22.turned_ref), custom_call_target="tpu_custom_call" | custom-call | flops 16384 | bytes 16384 | tf_op jit(solution)/shard_map/prep/pallas_call | solution.py:133
  56.1 5.7 %copy-done = bf16[512,128,128]{2,1,0:T(8,128)(2,1)} copy-done((bf16[512,128,128]{2,1,0:T(8,128)(2,1)}, bf16[512,128,128]{2,1,0:T(8,128)(2,1)S(1)}, u32[]{:S(2)}) %copy-start) | copy-done | bytes 16777240
  61.8 5.7 %copy-done.2 = bf16[512,128,128]{2,1,0:T(8,128)(2,1)} copy-done((bf16[512,128,128]{2,1,0:T(8,128)(2,1)}, bf16[512,128,128]{2,1,0:T(8,128)(2,1)S(1)}, u32[]{:S(2)}) %copy-start.2) | copy-done | bytes 16777240
  67.5 5.8 %copy-done.1 = bf16[512,128,128]{2,1,0:T(8,128)(2,1)S(1)} copy-done((bf16[512,128,128]{2,1,0:T(8,128)(2,1)S(1)}, bf16[512,128,128]{2,1,0:T(8,128)(2,1)}, u32[]{:S(2)}) %copy-start.1) | copy-done | bytes 16777240
  73.3 5.8 %copy-done.3 = bf16[512,128,128]{2,1,0:T(8,128)(2,1)S(1)} copy-done((bf16[512,128,128]{2,1,0:T(8,128)(2,1)S(1)}, bf16[512,128,128]{2,1,0:T(8,128)(2,1)}, u32[]{:S(2)}) %copy-start.3) | copy-done | bytes 16777240
  79.1 8.8 %pairs.4 = (bf16[1072,128]{1,0:T(8,128)(2,1)S(1)}, bf16[1072,128]{1,0:T(8,128)(2,1)S(1)}) custom-call(s32[2]{0:T(128)S(1)} %pad_add_fusion.1.source_ref, s32[128,128]{1,0:T(8,128)S(1)} %get-tuple-element.23.rows_ref, f32[2048,128]{1,0:T(8,128)S(1)} %get-tuple-element.24.target_ref, bf16[8,16,32,128]{3,2,1,0:T(8,128)(2,1)S(1)} %all-to-all-done.1.queries_ref, ...), custom_call_target="tpu_custom_call" | custom-call | flops 1610612736 | bytes 16777216 | tf_op jit(solution)/shard_map/pairs/pallas_call | solution.py:284
  87.9 5.2 %collective-permute-start.3 = (bf16[1072,128]{1,0:T(8,128)(2,1)S(1)}, bf16[1072,128]{1,0:T(8,128)(2,1)S(1)}, u32[]{:S(2)}, u32[]{:S(2)}) collective-permute-start(bf16[1072,128]{1,0:T(8,128)(2,1)S(1)} %get-tuple-element.26), channel_id=1, source_target_pairs={{0,4},{4,8},{8,12},{12,16},{16,20},{20,24},{24,28},{28,0},{1,5},{5... | collective-permute-start | bytes 823304 | tf_op jit(solution)/shard_map/ppermute | solution.py:502
  93.1 8.8 %pairs.5 = (bf16[1072,128]{1,0:T(8,128)(2,1)S(1)}, bf16[1072,128]{1,0:T(8,128)(2,1)S(1)}) custom-call(s32[2]{0:T(128)S(1)} %pad_add_fusion.2.source_ref, s32[128,128]{1,0:T(8,128)S(1)} %get-tuple-element.23.rows_ref, f32[2048,128]{1,0:T(8,128)S(1)} %get-tuple-element.24.target_ref, bf16[8,16,32,128]{3,2,1,0:T(8,128)(2,1)S(1)} %all-to-all-done.1.queries_ref, ...), custom_call_target="tpu_custom_call" | custom-call | flops 1610612736 | bytes 16777216 | tf_op jit(solution)/shard_map/pairs/pallas_call | solution.py:284
  101.9 7.1 %collective-permute-start.5 = (bf16[1072,128]{1,0:T(8,128)(2,1)S(1)}, bf16[1072,128]{1,0:T(8,128)(2,1)S(1)}, u32[]{:S(2)}, u32[]{:S(2)}) collective-permute-start(bf16[1072,128]{1,0:T(8,128)(2,1)S(1)} %get-tuple-element.28), channel_id=1, source_target_pairs={{0,12},{4,16},{8,20},{12,24},{16,28},{20,0},{24,4},{28,8},{1,13},{... | collective-permute-start | bytes 823304 | tf_op jit(solution)/shard_map/ppermute | solution.py:502
  108.9 11.2 %collective-permute-start.6 = (bf16[1072,128]{1,0:T(8,128)(2,1)S(1)}, bf16[1072,128]{1,0:T(8,128)(2,1)S(1)}, u32[]{:S(2)}, u32[]{:S(2)}) collective-permute-start(bf16[1072,128]{1,0:T(8,128)(2,1)S(1)} %get-tuple-element.29), channel_id=1, source_target_pairs={{0,16},{4,20},{8,24},{12,28},{16,0},{20,4},{24,8},{28,12},{1,17},{... | collective-permute-start | bytes 823304 | tf_op jit(solution)/shard_map/ppermute | solution.py:502
  120.1 8.8 %pairs.6 = (bf16[1072,128]{1,0:T(8,128)(2,1)S(1)}, bf16[1072,128]{1,0:T(8,128)(2,1)S(1)}) custom-call(s32[2]{0:T(128)S(1)} %pad_add_fusion.3.source_ref, s32[128,128]{1,0:T(8,128)S(1)} %get-tuple-element.23.rows_ref, f32[2048,128]{1,0:T(8,128)S(1)} %get-tuple-element.24.target_ref, bf16[8,16,32,128]{3,2,1,0:T(8,128)(2,1)S(1)} %all-to-all-done.1.queries_ref, ...), custom_call_target="tpu_custom_call" | custom-call | flops 1610612736 | bytes 16777216 | tf_op jit(solution)/shard_map/pairs/pallas_call | solution.py:284
  128.9 10.3 %collective-permute-start.7 = (bf16[1072,128]{1,0:T(8,128)(2,1)S(1)}, bf16[1072,128]{1,0:T(8,128)(2,1)S(1)}, u32[]{:S(2)}, u32[]{:S(2)}) collective-permute-start(bf16[1072,128]{1,0:T(8,128)(2,1)S(1)} %get-tuple-element.30), channel_id=1, source_target_pairs={{0,20},{4,24},{8,28},{12,0},{16,4},{20,8},{24,12},{28,16},{1,21},{... | collective-permute-start | bytes 823304 | tf_op jit(solution)/shard_map/ppermute | solution.py:502
  139.2 8.8 %pairs.7 = (bf16[1072,128]{1,0:T(8,128)(2,1)S(1)}, bf16[1072,128]{1,0:T(8,128)(2,1)S(1)}) custom-call(s32[2]{0:T(128)S(1)} %pad_add_fusion.4.source_ref, s32[128,128]{1,0:T(8,128)S(1)} %get-tuple-element.23.rows_ref, f32[2048,128]{1,0:T(8,128)S(1)} %get-tuple-element.24.target_ref, bf16[8,16,32,128]{3,2,1,0:T(8,128)(2,1)S(1)} %all-to-all-done.1.queries_ref, ...), custom_call_target="tpu_custom_call" | custom-call | flops 1610612736 | bytes 16777216 | tf_op jit(solution)/shard_map/pairs/pallas_call | solution.py:284
  148.1 9.8 %collective-permute-start.9 = (bf16[1072,128]{1,0:T(8,128)(2,1)S(1)}, bf16[1072,128]{1,0:T(8,128)(2,1)S(1)}, u32[]{:S(2)}, u32[]{:S(2)}) collective-permute-start(bf16[1072,128]{1,0:T(8,128)(2,1)S(1)} %get-tuple-element.32), channel_id=1, source_target_pairs={{0,28},{4,0},{8,4},{12,8},{16,12},{20,16},{24,20},{28,24},{1,29},{... | collective-permute-start | bytes 823304 | tf_op jit(solution)/shard_map/ppermute | solution.py:502
  157.9 12.7 %collective-permute-done.9.refs_6_ = bf16[1072,128]{1,0:T(8,128)(2,1)S(1)} collective-permute-done((bf16[1072,128]{1,0:T(8,128)(2,1)S(1)}, bf16[1072,128]{1,0:T(8,128)(2,1)S(1)}, u32[]{:S(2)}, u32[]{:S(2)}) %collective-permute-start.9) | collective-permute-done | bytes 274464 | tf_op jit(solution)/shard_map/ppermute | solution.py:502
  170.7 2.0 %finish.1 = (f32[16,128]{1,0:T(8,128)S(1)}, f32[16,32,128]{2,1,0:T(8,128)}) custom-call(bf16[16,32,128]{2,1,0:T(8,128)(2,1)S(1)} %copy-done.5, f32[16,64]{1,0:T(8,128)S(1)} %copy-done.6, f32[512,128]{1,0:T(8,128)S(1)} %get-tuple-element.19.back_ref, f32[8,512]{1,0:T(8,128)S(1)} %get-tuple-element.20.sums_ref, ...), custom_call_target="tpu_custom_call" | custom-call | tf_op jit(solution)/shard_map/finish/pallas_call | solution.py:453
  172.7 0.6 slice_reduce_fusion
  (23 shorter events, 0.3 us)
Async XLA Ops:
  13.5 54.0 %all-to-all-start.1 = ((bf16[8,16,32,128]{3,2,1,0:T(8,128)(2,1)}), bf16[8,16,32,128]{3,2,1,0:T(8,128)(2,1)S(1)}, u32[]{:S(2)}, u32[]{:S(2)}) async-start(bf16[8,16,32,128]{3,2,1,0:T(8,128)(2,1)} %broadcast_in_dim.5), calls=%async_computation.1 | async-start | bytes 2097152 | tf_op jit(solution)/shard_map/all_to_all | solution.py:486
  20.5 3.3 %collective-permute-start.2 = (s32[1,24]{1,0:T(1,128)}, s32[1,24]{1,0:T(1,128)S(1)}, u32[]{:S(2)}, u32[]{:S(2)}) collective-permute-start(s32[1,24]{1,0:T(1,128)} %param.10), channel_id=1, source_target_pairs={{3,0},{0,1},{1,2},{2,3},{7,4},{4,5},{5,6},{6,7},{11,8},{8,9},{9,10... | collective-permute-start | bytes 296 | tf_op jit(solution)/shard_map/ppermute | solution.py:476
  20.5 3.7 %collective-permute-start.1 = (s32[1,24]{1,0:T(1,128)}, s32[1,24]{1,0:T(1,128)S(1)}, u32[]{:S(2)}, u32[]{:S(2)}) collective-permute-start(s32[1,24]{1,0:T(1,128)} %param.10), channel_id=1, source_target_pairs={{2,0},{3,1},{0,2},{1,3},{6,4},{7,5},{4,6},{5,7},{10,8},{11,9},{8,1... | collective-permute-start | bytes 296 | tf_op jit(solution)/shard_map/ppermute | solution.py:476
  22.0 2.9 %collective-permute-start = (s32[1,24]{1,0:T(1,128)}, s32[1,24]{1,0:T(1,128)S(1)}, u32[]{:S(2)}, u32[]{:S(2)}) collective-permute-start(s32[1,24]{1,0:T(1,128)} %param.10), channel_id=1, source_target_pairs={{1,0},{2,1},{3,2},{0,3},{5,4},{6,5},{7,6},{4,7},{9,8},{10,9},{11,1... | collective-permute-start | bytes 296 | tf_op jit(solution)/shard_map/ppermute | solution.py:476
  25.7 0.9 copy-start.4
  56.1 5.7 %copy-start = (bf16[512,128,128]{2,1,0:T(8,128)(2,1)}, bf16[512,128,128]{2,1,0:T(8,128)(2,1)S(1)}, u32[]{:S(2)}) copy-start(bf16[512,128,128]{2,1,0:T(8,128)(2,1)S(1)} %get-tuple-element.21.index_ref) | copy-start | bytes 50331652
  61.8 5.7 %copy-start.2 = (bf16[512,128,128]{2,1,0:T(8,128)(2,1)}, bf16[512,128,128]{2,1,0:T(8,128)(2,1)S(1)}, u32[]{:S(2)}) copy-start(bf16[512,128,128]{2,1,0:T(8,128)(2,1)S(1)} %get-tuple-element.22.turned_ref) | copy-start | bytes 50331652
  67.5 5.8 %copy-start.1 = (bf16[512,128,128]{2,1,0:T(8,128)(2,1)S(1)}, bf16[512,128,128]{2,1,0:T(8,128)(2,1)}, u32[]{:S(2)}) copy-start(bf16[512,128,128]{2,1,0:T(8,128)(2,1)} %copy-done) | copy-start | bytes 50331652
  73.3 5.8 %copy-start.3 = (bf16[512,128,128]{2,1,0:T(8,128)(2,1)S(1)}, bf16[512,128,128]{2,1,0:T(8,128)(2,1)}, u32[]{:S(2)}) copy-start(bf16[512,128,128]{2,1,0:T(8,128)(2,1)} %copy-done.2) | copy-start | bytes 50331652
  87.9 60.2 %collective-permute-start.3 = (bf16[1072,128]{1,0:T(8,128)(2,1)S(1)}, bf16[1072,128]{1,0:T(8,128)(2,1)S(1)}, u32[]{:S(2)}, u32[]{:S(2)}) collective-permute-start(bf16[1072,128]{1,0:T(8,128)(2,1)S(1)} %get-tuple-element.26), channel_id=1, source_target_pairs={{0,4},{4,8},{8,12},{12,16},{16,20},{20,24},{24,28},{28,0},{1,5},{5... | collective-permute-start | bytes 823304 | tf_op jit(solution)/shard_map/ppermute | solution.py:502
  93.1 55.0 %collective-permute-start.4 = (bf16[1072,128]{1,0:T(8,128)(2,1)S(1)}, bf16[1072,128]{1,0:T(8,128)(2,1)S(1)}, u32[]{:S(2)}, u32[]{:S(2)}) collective-permute-start(bf16[1072,128]{1,0:T(8,128)(2,1)S(1)} %get-tuple-element.27), channel_id=1, source_target_pairs={{0,8},{4,12},{8,16},{12,20},{16,24},{20,28},{24,0},{28,4},{1,9},{5... | collective-permute-start | bytes 823304 | tf_op jit(solution)/shard_map/ppermute | solution.py:502
  101.9 56.1 %collective-permute-start.5 = (bf16[1072,128]{1,0:T(8,128)(2,1)S(1)}, bf16[1072,128]{1,0:T(8,128)(2,1)S(1)}, u32[]{:S(2)}, u32[]{:S(2)}) collective-permute-start(bf16[1072,128]{1,0:T(8,128)(2,1)S(1)} %get-tuple-element.28), channel_id=1, source_target_pairs={{0,12},{4,16},{8,20},{12,24},{16,28},{20,0},{24,4},{28,8},{1,13},{... | collective-permute-start | bytes 823304 | tf_op jit(solution)/shard_map/ppermute | solution.py:502
  108.9 49.0 %collective-permute-start.6 = (bf16[1072,128]{1,0:T(8,128)(2,1)S(1)}, bf16[1072,128]{1,0:T(8,128)(2,1)S(1)}, u32[]{:S(2)}, u32[]{:S(2)}) collective-permute-start(bf16[1072,128]{1,0:T(8,128)(2,1)S(1)} %get-tuple-element.29), channel_id=1, source_target_pairs={{0,16},{4,20},{8,24},{12,28},{16,0},{20,4},{24,8},{28,12},{1,17},{... | collective-permute-start | bytes 823304 | tf_op jit(solution)/shard_map/ppermute | solution.py:502
  128.9 41.7 %copy-start.5 = (bf16[16,32,128]{2,1,0:T(8,128)(2,1)S(1)}, bf16[16,32,128]{2,1,0:T(8,128)(2,1)}, u32[]{:S(2)}) copy-start(bf16[16,32,128]{2,1,0:T(8,128)(2,1)} %queries_ref.1) | copy-start | bytes 393220
  128.9 41.7 %copy-start.6 = (f32[16,64]{1,0:T(8,128)S(1)}, f32[16,64]{1,0:T(8,128)}, u32[]{:S(2)}) copy-start(f32[16,64]{1,0:T(8,128)} %teacher_ref.1) | copy-start | bytes 12292
  128.9 29.0 %collective-permute-start.7 = (bf16[1072,128]{1,0:T(8,128)(2,1)S(1)}, bf16[1072,128]{1,0:T(8,128)(2,1)S(1)}, u32[]{:S(2)}, u32[]{:S(2)}) collective-permute-start(bf16[1072,128]{1,0:T(8,128)(2,1)S(1)} %get-tuple-element.30), channel_id=1, source_target_pairs={{0,20},{4,24},{8,28},{12,0},{16,4},{20,8},{24,12},{28,16},{1,21},{... | collective-permute-start | bytes 823304 | tf_op jit(solution)/shard_map/ppermute | solution.py:502
  148.0 9.9 %collective-permute-start.8 = (bf16[1072,128]{1,0:T(8,128)(2,1)S(1)}, bf16[1072,128]{1,0:T(8,128)(2,1)S(1)}, u32[]{:S(2)}, u32[]{:S(2)}) collective-permute-start(bf16[1072,128]{1,0:T(8,128)(2,1)S(1)} %get-tuple-element.31), channel_id=1, source_target_pairs={{0,24},{4,28},{8,0},{12,4},{16,8},{20,12},{24,16},{28,20},{1,25},{... | collective-permute-start | bytes 823304 | tf_op jit(solution)/shard_map/ppermute | solution.py:502
  148.1 22.6 %collective-permute-start.9 = (bf16[1072,128]{1,0:T(8,128)(2,1)S(1)}, bf16[1072,128]{1,0:T(8,128)(2,1)S(1)}, u32[]{:S(2)}, u32[]{:S(2)}) collective-permute-start(bf16[1072,128]{1,0:T(8,128)(2,1)S(1)} %get-tuple-element.32), channel_id=1, source_target_pairs={{0,28},{4,0},{8,4},{12,8},{16,12},{20,16},{24,20},{28,24},{1,29},{... | collective-permute-start | bytes 823304 | tf_op jit(solution)/shard_map/ppermute | solution.py:502

commit v3 on v2

--- a/solution.py
+++ b/solution.py
@@ -76,7 +76,7 @@
         lax.fori_loop(0, chunk // LOAD_STEP, body, 0)
 
 
-def prep_kernel(me_ref, meta_ref, index_ref, turned_ref, rows_ref, target_ref, value_ref, place_ref, result_ref, *, shard, cands):
+def prep_kernel(me_ref, meta_ref, rows_ref, target_ref, value_ref, place_ref, result_ref, *, shard, cands):
     count = meta_ref.shape[0]
     code = meta_ref[:, :cands]
     owner = jnp.floor((code + 0.5) * (1.0 / shard))
@@ -127,7 +127,7 @@
         )
 
 
-def prep(me, meta, index, turned, shard, cands):
+def prep(me, meta, shard, cands):
     count = meta.shape[0]
     wide = 128
     return pl.pallas_call(
@@ -135,8 +135,6 @@
         in_specs=[
             pl.BlockSpec(memory_space=pltpu.SMEM),
             pl.BlockSpec(memory_space=pltpu.VMEM),
-            pl.BlockSpec(memory_space=pltpu.VMEM),
-            pl.BlockSpec(memory_space=pltpu.VMEM),
         ],
         out_specs=[pl.BlockSpec(memory_space=pltpu.VMEM)] * 2,
         out_shape=[
@@ -151,7 +149,7 @@
         compiler_params=pltpu.CompilerParams(vmem_limit_bytes=VMEM_LIMIT),
         cost_estimate=pl.CostEstimate(flops=count * wide, bytes_accessed=count * wide, transcendentals=0),
         name="prep",
-    )(me, meta, index, turned)
+    )(me, meta)
 
 
 def pair_kernel(source_ref, rows_ref, target_ref, queries_ref, inverse_ref, index_ref, turned_ref, *refs, cands, sources):
@@ -203,19 +201,27 @@
                 expos.append(expo.astype(jnp.bfloat16))
                 weights.append((expo * inverse).astype(jnp.bfloat16))
         following = multiply(step + 1)
-        done = []
+        backs = []
         for u in range(UNITS):
-            slot = units_ref[step * UNITS + u]
-            part = slice(u * GROUP, (u + 1) * GROUP)
             _, tiles = tiles_of(step * UNITS + u, index_ref)
-            backs = [dot(w, tile).astype(jnp.bfloat16) for w, tile in zip(weights[part], tiles)]
-            totals = dot_last(ones, jnp.concatenate(expos[part], axis=0))
-            done.append((slot, totals, jnp.concatenate(backs, axis=0)))
+            for g in range(0, GROUP, 2):
+                k = u * GROUP + g
+                part = dot(
+                    jnp.concatenate(weights[k : k + 2], axis=0),
+                    jnp.concatenate(tiles[g : g + 2], axis=1),
+                )
+                backs += [part[:tokens, :dim], part[tokens:, dim:]]
+        totals = []
+        for u in range(0, UNITS, 2):
+            part = dot_last(ones, jnp.concatenate(expos[u * GROUP : (u + 2) * GROUP], axis=0))
+            totals += [part[0:1, :wide], part[0:1, wide:]]
+        for u in range(UNITS):
+            back_ref[step * UNITS + u] = jnp.concatenate(
+                backs[u * GROUP : (u + 1) * GROUP], axis=0
+            ).astype(jnp.bfloat16)
+            total_ref[pl.ds(units_ref[step * UNITS + u], 1), :] = totals[u]
         for u in range(UNITS):
             raw_ref[u] = following[u]
-        for u, (slot, totals, back) in enumerate(done):
-            total_ref[pl.ds(slot, 1), :] = totals[0:1]
-            back_ref[step * UNITS + u] = back
         return carry
 
     for u, raw in enumerate(multiply(0)):
@@ -250,17 +256,27 @@
     ) % tokens
 
     def backward(step, carry):
-        done = []
+        owners, sides = [], []
         for u in range(UNITS):
             slot, q, _ = entry(step * UNITS + u)
             left = jnp.where(diagonal, left_ref[pl.ds(slot, 1), :], 0.0)
             right = jnp.where(diagonal, right_ref[pl.ds(slot, 1), :], 0.0)
             both = jnp.concatenate([left, right], axis=0)
             high = both.astype(jnp.bfloat16)
-            low = (both - high.astype(jnp.float32)).astype(jnp.bfloat16)
-            part = dot(jnp.concatenate([high, low], axis=0), back_ref[step * UNITS + u])
-            done.append((q, part[: 2 * tokens] + part[2 * tokens :]))
-        for q, part in done:
+            sides += [high, (both - high.astype(jnp.float32)).astype(jnp.bfloat16)]
+            owners.append(q)
+        parts = []
+        for u in range(0, UNITS, 2):
+            pulled = dot(
+                jnp.concatenate(sides[2 * u : 2 * u + 4], axis=0),
+                jnp.concatenate([back_ref[step * UNITS + u], back_ref[step * UNITS + u + 1]], axis=1),
+            )
+            height = 2 * tokens
+            parts += [
+                pulled[:height, :dim] + pulled[height : 2 * height, :dim],
+                pulled[2 * height : 3 * height, dim:] + pulled[3 * height :, dim:],
+            ]
+        for q, part in zip(owners, parts):
             acc_ref[q] += part
         return carry
 
@@ -487,12 +503,14 @@
 
     all_meta = told(meta).reshape(owners * count, -1)
     all_queries = told(queries)
+    rows, targets = prep(me.reshape(1), all_meta, shard, cands)
+    rows, all_neg = lax.optimization_barrier((rows, all_neg))
     index, turned, inverse, neg_acc, neg_sum = negatives(all_neg, queries, index)
-    rows, targets = prep(me.reshape(1), all_meta, index, turned, shard, cands)
     messages = []
     order = list(range(1, owners)) + [0]
-    for first in range(0, owners, SOURCES):
-        steps = order[first : first + SOURCES]
+    groups = [order[first : first + SOURCES] for first in range(0, owners, SOURCES)]
+    groups = groups[:-1] + [groups[-1][:-1], groups[-1][-1:]]
+    for steps in groups:
         sources = [lax.rem(me + step, owners) for step in steps]
         found = pairs(
             sources, rows, targets, all_queries, inverse, index, turned, cands, room

time: 176 us -> 171 us (0.972); the launches traced: 173 us -> 172 us
  starting transfers between devices: 53.7 us -> 11.8 us
  Pallas kernels: 66.6 us -> 106 us
  local copies, waits for them, and re-layouts: 26.7 us -> 38.9 us
  waiting for transfers between devices: 13.9 us -> 2.39 us
    ppermute x7, starting transfers between devices: 43.7 us -> 2.81 us  [on_device(): lax.ppermute(message, 'corpus', [(i, (i + step) % owners) for i in range(...]
    pallas_call x4 -> x5, Pallas kernels: 35 us -> 73.9 us  [pairs(): pl.pallas_call(functools.partial(pair_kernel, cands=cands, sources=len(so...]
    ppermute x7, waiting for transfers between devices: 12.7 us -> 0.02 us  [on_device(): lax.ppermute(message, 'corpus', [(i, (i + step) % owners) for i in range(...]
    unnamed x14 -> x22, local copies, waits for them, and re-layouts: 23.9 us -> 36.1 us
  transfers between devices with their start and end apart: 11 -> 11, of which waited for: 3 -> 2; matrix products, arithmetic and copies ran while one was open for 1% -> 1% of each run, Pallas kernels for 32% -> 55%
where the time goes in v3:
time: 171 us; the launch traced here: 172 us
  Pallas kernels  106 us (62%)
  local copies, waits for them, and re-layouts  38.9 us (23%)
  starting transfers between devices  11.8 us (7%)
  blocking collectives  9.28 us (5%)
  waiting for transfers between devices  2.39 us (1%)
  other arithmetic  2.38 us (1%)
    pallas_call x5, Pallas kernels, pairs(): pl.pallas_call(functools.partial(pair_kernel, cands=cands, sources=len(so...  73.9 us
    unnamed x22, local copies, waits for them, and re-layouts  36.1 us
    pallas_call x1, Pallas kernels, negatives(): pl.pallas_call(functools.partial(neg_kernel, tokens=tokens), in_specs=[pl...  24.5 us
    all_to_all x1, blocking collectives, told(): lax.all_to_all(copies, 'corpus', split_axis=0, concat_axis=0, tiled=True)  9.28 us
    all_to_all x1, starting transfers between devices, told(): lax.all_to_all(copies, 'corpus', split_axis=0, concat_axis=0, tiled=True)  7.01 us
    pallas_call x1, Pallas kernels, prep(): pl.pallas_call(functools.partial(prep_kernel, shard=shard, cands=cands),...  4.98 us
  transfers between devices with their start and end apart: 11, of which 2 were waited for; matrix products, arithmetic and copies ran while one was open for 1% of the time, Pallas kernels for 55%

profile of v3, /device:TPU:20, one launch (start us, length us, event | category | flops | bytes accessed | tf_op | source)
XLA Modules:
  0.0 172.1 jit_solution(13294212428363105076)
XLA Ops:
  0.6 0.7 fusion
  1.4 0.8 pad_maximum_fusion
  2.1 9.3 %all_to_all.10 = f32[8,16,128]{2,1,0:T(8,128)S(1)} all-to-all(f32[8,16,128]{2,1,0:T(8,128)S(1)} %broadcast_in_dim.4), channel_id=1, replica_groups=mesh['corpus'=8,'blk'=4] {'corpus'}, dimensions={0} | all-to-all | bytes 131072 | tf_op jit(solution)/shard_map/all_to_all | solution.py:502
  11.4 2.1 %broadcast_in_dim.5 = bf16[8,16,32,128]{3,2,1,0:T(8,128)(2,1)} broadcast(bf16[16,32,128]{2,1,0:T(8,128)(2,1)} %queries_ref.1), dimensions={1,2,3} | broadcast | bytes 1179648 | tf_op jit(solution)/shard_map/broadcast_in_dim | solution.py:501
  13.5 7.0 %all-to-all-start.1 = ((bf16[8,16,32,128]{3,2,1,0:T(8,128)(2,1)}), bf16[8,16,32,128]{3,2,1,0:T(8,128)(2,1)S(1)}, u32[]{:S(2)}, u32[]{:S(2)}) async-start(bf16[8,16,32,128]{3,2,1,0:T(8,128)(2,1)} %broadcast_in_dim.5), calls=%async_computation.1 | async-start | bytes 2097152 | tf_op jit(solution)/shard_map/all_to_all | solution.py:502
  20.5 1.5 collective-permute-start.1
  22.0 0.5 collective-permute-start.2
  22.5 0.1 pad_add_fusion.1.source_ref
  22.6 0.1 pad_add_fusion.2.source_ref
  22.7 0.1 pad_add_fusion.3.source_ref
  22.7 1.4 collective-permute-done.1
  24.2 0.9 collective-permute-done.2
  25.1 0.7 pad_add_fusion
  25.8 0.1 reshape.22.rows_ref
  25.9 5.0 %prep.1 = (s32[128,128]{1,0:T(8,128)S(1)}, f32[2048,128]{1,0:T(8,128)S(1)}) custom-call(s32[1]{0:T(128)} %bitcast.me_ref, f32[128,128]{1,0:T(8,128)S(1)} %bitcast.17), custom_call_target="tpu_custom_call" | custom-call | flops 16384 | bytes 16384 | tf_op jit(solution)/shard_map/prep/pallas_call | solution.py:133
  30.9 0.9 copy-done.6
  31.7 24.5 %negatives.1 = (bf16[512,128,128]{2,1,0:T(8,128)(2,1)S(1)}, bf16[512,128,128]{2,1,0:T(8,128)(2,1)S(1)}, f32[512,128]{1,0:T(8,128)S(1)}, f32[512,128]{1,0:T(8,128)S(1)}, f32[8,512]{1,0:T(8,128)S(1)}) custom-call(s32[96]{0:T(128)S(1)} %reshape.22.rows_ref, bf16[512,128]{1,0:T(8,128)(2,1)S(1)} %bitcast.16, bf16[512,128,128]{2,1,0:T(8,128)(2,1)} %shard_ref.1), custom_call_target="tpu_custom_call" | custom-call | flops 3221225472 | bytes 3145728 | tf_op jit(solution)/shard_map/negatives/pallas_call | solution.py:404
  56.3 5.7 %copy-done = bf16[512,128,128]{2,1,0:T(8,128)(2,1)} copy-done((bf16[512,128,128]{2,1,0:T(8,128)(2,1)}, bf16[512,128,128]{2,1,0:T(8,128)(2,1)S(1)}, u32[]{:S(2)}) %copy-start) | copy-done | bytes 16777240
  62.0 5.7 %copy-done.3 = bf16[512,128,128]{2,1,0:T(8,128)(2,1)} copy-done((bf16[512,128,128]{2,1,0:T(8,128)(2,1)}, bf16[512,128,128]{2,1,0:T(8,128)(2,1)S(1)}, u32[]{:S(2)}) %copy-start.3) | copy-done | bytes 16777240
  67.7 0.7 copy-done.8
  68.4 5.8 %copy-done.1 = bf16[512,128,128]{2,1,0:T(8,128)(2,1)S(1)} copy-done((bf16[512,128,128]{2,1,0:T(8,128)(2,1)S(1)}, bf16[512,128,128]{2,1,0:T(8,128)(2,1)}, u32[]{:S(2)}) %copy-start.1) | copy-done | bytes 16777240
  74.2 5.8 %copy-done.4 = bf16[512,128,128]{2,1,0:T(8,128)(2,1)S(1)} copy-done((bf16[512,128,128]{2,1,0:T(8,128)(2,1)S(1)}, bf16[512,128,128]{2,1,0:T(8,128)(2,1)}, u32[]{:S(2)}) %copy-start.4) | copy-done | bytes 16777240
  80.0 9.0 %pairs.8 = bf16[1072,128]{1,0:T(8,128)(2,1)S(1)} custom-call(s32[1]{0:T(128)} %bitcast.11.source_ref, s32[128,128]{1,0:T(8,128)S(1)} %get-tuple-element.23.rows_ref, f32[2048,128]{1,0:T(8,128)S(1)} %get-tuple-element.24.target_ref, bf16[8,16,32,128]{3,2,1,0:T(8,128)(2,1)S(1)} %all-to-all-done.1.queries_ref, f32[512,128]{1,0:T(8,128)S(1)} %get-tuple-element.25.inverse_ref, ...), custom_call_target="tpu_custom_call" | custom-call | flops 805306368 | bytes 8388608 | tf_op jit(solution)/shard_map/pairs/pallas_call | solution.py:300
  89.1 18.5 %pairs.7 = (bf16[1072,128]{1,0:T(8,128)(2,1)S(1)}, bf16[1072,128]{1,0:T(8,128)(2,1)}) custom-call(s32[2]{0:T(128)S(1)} %pad_add_fusion.3.source_ref, s32[128,128]{1,0:T(8,128)S(1)} %get-tuple-element.23.rows_ref, f32[2048,128]{1,0:T(8,128)S(1)} %get-tuple-element.24.target_ref, bf16[8,16,32,128]{3,2,1,0:T(8,128)(2,1)S(1)} %all-to-all-done.1.queries_ref, ...), custom_call_target="tpu_custom_call" | custom-call | flops 1610612736 | bytes 16777216 | tf_op jit(solution)/shard_map/pairs/pallas_call | solution.py:300
  107.6 18.6 %pairs.6 = (bf16[1072,128]{1,0:T(8,128)(2,1)}, bf16[1072,128]{1,0:T(8,128)(2,1)}) custom-call(s32[2]{0:T(128)S(1)} %pad_add_fusion.2.source_ref, s32[128,128]{1,0:T(8,128)S(1)} %get-tuple-element.23.rows_ref, f32[2048,128]{1,0:T(8,128)S(1)} %get-tuple-element.24.target_ref, bf16[8,16,32,128]{3,2,1,0:T(8,128)(2,1)S(1)} %all-to-all-done.1.queries_ref, ...), custom_call_target="tpu_custom_call" | custom-call | flops 1610612736 | bytes 16777216 | tf_op jit(solution)/shard_map/pairs/pallas_call | solution.py:300
  126.3 18.7 %pairs.5 = (bf16[1072,128]{1,0:T(8,128)(2,1)}, bf16[1072,128]{1,0:T(8,128)(2,1)}) custom-call(s32[2]{0:T(128)S(1)} %pad_add_fusion.1.source_ref, s32[128,128]{1,0:T(8,128)S(1)} %get-tuple-element.23.rows_ref, f32[2048,128]{1,0:T(8,128)S(1)} %get-tuple-element.24.target_ref, bf16[8,16,32,128]{3,2,1,0:T(8,128)(2,1)S(1)} %all-to-all-done.1.queries_ref, ...), custom_call_target="tpu_custom_call" | custom-call | flops 1610612736 | bytes 16777216 | tf_op jit(solution)/shard_map/pairs/pallas_call | solution.py:300
  144.9 2.7 %collective-permute-start.3 = (bf16[1072,128]{1,0:T(8,128)(2,1)}, bf16[1072,128]{1,0:T(8,128)(2,1)}, u32[]{:S(2)}, u32[]{:S(2)}) collective-permute-start(bf16[1072,128]{1,0:T(8,128)(2,1)} %get-tuple-element.28), channel_id=1, source_target_pairs={{0,4},{4,8},{8,12},{12,16},{16,20},{20,24},{24,28},{28,0},{1,5},{5... | collective-permute-start | bytes 823304 | tf_op jit(solution)/shard_map/ppermute | solution.py:520
  147.7 5.8 %copy-done.2 = bf16[512,128,128]{2,1,0:T(8,128)(2,1)S(1)} copy-done((bf16[512,128,128]{2,1,0:T(8,128)(2,1)S(1)}, bf16[512,128,128]{2,1,0:T(8,128)(2,1)}, u32[]{:S(2)}) %copy-start.2) | copy-done | bytes 16777240
  153.4 5.8 %copy-done.5 = bf16[512,128,128]{2,1,0:T(8,128)(2,1)S(1)} copy-done((bf16[512,128,128]{2,1,0:T(8,128)(2,1)S(1)}, bf16[512,128,128]{2,1,0:T(8,128)(2,1)}, u32[]{:S(2)}) %copy-start.5) | copy-done | bytes 16777240
  159.2 9.0 %pairs.9.refs_7_ = bf16[1072,128]{1,0:T(8,128)(2,1)S(1)} custom-call(s32[1]{0:T(128)} %bitcast.12.source_ref, s32[128,128]{1,0:T(8,128)S(1)} %get-tuple-element.23.rows_ref, f32[2048,128]{1,0:T(8,128)S(1)} %get-tuple-element.24.target_ref, bf16[8,16,32,128]{3,2,1,0:T(8,128)(2,1)S(1)} %all-to-all-done.1.queries_ref, ...), custom_call_target="tpu_custom_call" | custom-call | flops 805306368 | bytes 8388608 | tf_op jit(solution)/shard_map/pairs/pallas_call | solution.py:300
  168.3 3.1 %finish.1 = (f32[16,128]{1,0:T(8,128)S(1)}, f32[16,32,128]{2,1,0:T(8,128)}) custom-call(bf16[16,32,128]{2,1,0:T(8,128)(2,1)S(1)} %copy-done.7, f32[16,64]{1,0:T(8,128)S(1)} %copy-done.10, f32[512,128]{1,0:T(8,128)S(1)} %copy-done.9, f32[8,512]{1,0:T(8,128)S(1)} %get-tuple-element.22.sums_ref, bf16[1072,128]{1,0:T(8,128)(2,1)} %collective-permute-done.3.refs_0_, ...), custom_call_target="tpu_custom_call" | custom-call | tf_op jit(solution)/shard_map/finish/pallas_call | solution.py:469
  171.5 0.6 slice_reduce_fusion
  (31 shorter events, 0.1 us)
Async XLA Ops:
  13.5 54.9 %all-to-all-start.1 = ((bf16[8,16,32,128]{3,2,1,0:T(8,128)(2,1)}), bf16[8,16,32,128]{3,2,1,0:T(8,128)(2,1)S(1)}, u32[]{:S(2)}, u32[]{:S(2)}) async-start(bf16[8,16,32,128]{3,2,1,0:T(8,128)(2,1)} %broadcast_in_dim.5), calls=%async_computation.1 | async-start | bytes 2097152 | tf_op jit(solution)/shard_map/all_to_all | solution.py:502
  20.5 3.7 %collective-permute-start.1 = (s32[1,24]{1,0:T(1,128)}, s32[1,24]{1,0:T(1,128)S(1)}, u32[]{:S(2)}, u32[]{:S(2)}) collective-permute-start(s32[1,24]{1,0:T(1,128)} %param.10), channel_id=1, source_target_pairs={{2,0},{3,1},{0,2},{1,3},{6,4},{7,5},{4,6},{5,7},{10,8},{11,9},{8,1... | collective-permute-start | bytes 296 | tf_op jit(solution)/shard_map/ppermute | solution.py:492
  22.0 2.2 %collective-permute-start = (s32[1,24]{1,0:T(1,128)}, s32[1,24]{1,0:T(1,128)S(1)}, u32[]{:S(2)}, u32[]{:S(2)}) collective-permute-start(s32[1,24]{1,0:T(1,128)} %param.10), channel_id=1, source_target_pairs={{1,0},{2,1},{3,2},{0,3},{5,4},{6,5},{7,6},{4,7},{9,8},{10,9},{11,1... | collective-permute-start | bytes 296 | tf_op jit(solution)/shard_map/ppermute | solution.py:492
  22.0 3.1 %collective-permute-start.2 = (s32[1,24]{1,0:T(1,128)}, s32[1,24]{1,0:T(1,128)S(1)}, u32[]{:S(2)}, u32[]{:S(2)}) collective-permute-start(s32[1,24]{1,0:T(1,128)} %param.10), channel_id=1, source_target_pairs={{3,0},{0,1},{1,2},{2,3},{7,4},{4,5},{5,6},{6,7},{11,8},{8,9},{9,10... | collective-permute-start | bytes 296 | tf_op jit(solution)/shard_map/ppermute | solution.py:492
  30.8 0.9 copy-start.6
  56.3 5.7 %copy-start = (bf16[512,128,128]{2,1,0:T(8,128)(2,1)}, bf16[512,128,128]{2,1,0:T(8,128)(2,1)S(1)}, u32[]{:S(2)}) copy-start(bf16[512,128,128]{2,1,0:T(8,128)(2,1)S(1)} %get-tuple-element.26.index_ref) | copy-start | bytes 50331652
  62.0 5.7 %copy-start.3 = (bf16[512,128,128]{2,1,0:T(8,128)(2,1)}, bf16[512,128,128]{2,1,0:T(8,128)(2,1)S(1)}, u32[]{:S(2)}) copy-start(bf16[512,128,128]{2,1,0:T(8,128)(2,1)S(1)} %get-tuple-element.27.turned_ref) | copy-start | bytes 50331652
  67.7 0.7 copy-start.8
  68.4 5.8 %copy-start.1 = (bf16[512,128,128]{2,1,0:T(8,128)(2,1)S(1)}, bf16[512,128,128]{2,1,0:T(8,128)(2,1)}, u32[]{:S(2)}) copy-start(bf16[512,128,128]{2,1,0:T(8,128)(2,1)} %copy-done) | copy-start | bytes 50331652
  74.2 5.8 %copy-start.4 = (bf16[512,128,128]{2,1,0:T(8,128)(2,1)S(1)}, bf16[512,128,128]{2,1,0:T(8,128)(2,1)}, u32[]{:S(2)}) copy-start(bf16[512,128,128]{2,1,0:T(8,128)(2,1)} %copy-done.3) | copy-start | bytes 50331652
  89.0 55.9 %collective-permute-start.9 = (bf16[1072,128]{1,0:T(8,128)(2,1)S(1)}, bf16[1072,128]{1,0:T(8,128)(2,1)S(1)}, u32[]{:S(2)}, u32[]{:S(2)}) collective-permute-start(bf16[1072,128]{1,0:T(8,128)(2,1)S(1)} %pairs.8), channel_id=1, source_target_pairs={{0,28},{4,0},{8,4},{12,8},{16,12},{20,16},{24,20},{28,24},{1,29},{... | collective-permute-start | bytes 823304 | tf_op jit(solution)/shard_map/ppermute | solution.py:520
  107.6 40.1 %collective-permute-start.7 = (bf16[1072,128]{1,0:T(8,128)(2,1)S(1)}, bf16[1072,128]{1,0:T(8,128)(2,1)S(1)}, u32[]{:S(2)}, u32[]{:S(2)}) collective-permute-start(bf16[1072,128]{1,0:T(8,128)(2,1)S(1)} %get-tuple-element.32), channel_id=1, source_target_pairs={{0,20},{4,24},{8,28},{12,0},{16,4},{20,8},{24,12},{28,16},{1,21},{... | collective-permute-start | bytes 823304 | tf_op jit(solution)/shard_map/ppermute | solution.py:520
  107.6 60.6 %collective-permute-start.8 = (bf16[1072,128]{1,0:T(8,128)(2,1)}, bf16[1072,128]{1,0:T(8,128)(2,1)S(1)}, u32[]{:S(2)}, u32[]{:S(2)}) collective-permute-start(bf16[1072,128]{1,0:T(8,128)(2,1)} %get-tuple-element.33), channel_id=1, source_target_pairs={{0,24},{4,28},{8,0},{12,4},{16,8},{20,12},{24,16},{28,20},{1,25},{... | collective-permute-start | bytes 823304 | tf_op jit(solution)/shard_map/ppermute | solution.py:520
  126.3 42.0 %collective-permute-start.5 = (bf16[1072,128]{1,0:T(8,128)(2,1)}, bf16[1072,128]{1,0:T(8,128)(2,1)S(1)}, u32[]{:S(2)}, u32[]{:S(2)}) collective-permute-start(bf16[1072,128]{1,0:T(8,128)(2,1)} %get-tuple-element.30), channel_id=1, source_target_pairs={{0,12},{4,16},{8,20},{12,24},{16,28},{20,0},{24,4},{28,8},{1,13},{... | collective-permute-start | bytes 823304 | tf_op jit(solution)/shard_map/ppermute | solution.py:520
  126.3 42.0 %collective-permute-start.6 = (bf16[1072,128]{1,0:T(8,128)(2,1)}, bf16[1072,128]{1,0:T(8,128)(2,1)}, u32[]{:S(2)}, u32[]{:S(2)}) collective-permute-start(bf16[1072,128]{1,0:T(8,128)(2,1)} %get-tuple-element.31), channel_id=1, source_target_pairs={{0,16},{4,20},{8,24},{12,28},{16,0},{20,4},{24,8},{28,12},{1,17},{... | collective-permute-start | bytes 823304 | tf_op jit(solution)/shard_map/ppermute | solution.py:520
  144.9 23.4 %collective-permute-start.3 = (bf16[1072,128]{1,0:T(8,128)(2,1)}, bf16[1072,128]{1,0:T(8,128)(2,1)}, u32[]{:S(2)}, u32[]{:S(2)}) collective-permute-start(bf16[1072,128]{1,0:T(8,128)(2,1)} %get-tuple-element.28), channel_id=1, source_target_pairs={{0,4},{4,8},{8,12},{12,16},{16,20},{20,24},{24,28},{28,0},{1,5},{5... | collective-permute-start | bytes 823304 | tf_op jit(solution)/shard_map/ppermute | solution.py:520
  147.7 20.6 %collective-permute-start.4 = (bf16[1072,128]{1,0:T(8,128)(2,1)}, bf16[1072,128]{1,0:T(8,128)(2,1)}, u32[]{:S(2)}, u32[]{:S(2)}) collective-permute-start(bf16[1072,128]{1,0:T(8,128)(2,1)} %get-tuple-element.29), channel_id=1, source_target_pairs={{0,8},{4,12},{8,16},{12,20},{16,24},{20,28},{24,0},{28,4},{1,9},{5... | collective-permute-start | bytes 823304 | tf_op jit(solution)/shard_map/ppermute | solution.py:520
  147.7 5.8 %copy-start.2 = (bf16[512,128,128]{2,1,0:T(8,128)(2,1)S(1)}, bf16[512,128,128]{2,1,0:T(8,128)(2,1)}, u32[]{:S(2)}) copy-start(bf16[512,128,128]{2,1,0:T(8,128)(2,1)} %copy-done) | copy-start | bytes 50331652
  153.4 5.8 %copy-start.5 = (bf16[512,128,128]{2,1,0:T(8,128)(2,1)S(1)}, bf16[512,128,128]{2,1,0:T(8,128)(2,1)}, u32[]{:S(2)}) copy-start(bf16[512,128,128]{2,1,0:T(8,128)(2,1)} %copy-done.3) | copy-start | bytes 50331652
  159.2 9.1 %copy-start.7 = (bf16[16,32,128]{2,1,0:T(8,128)(2,1)S(1)}, bf16[16,32,128]{2,1,0:T(8,128)(2,1)}, u32[]{:S(2)}) copy-start(bf16[16,32,128]{2,1,0:T(8,128)(2,1)} %queries_ref.1) | copy-start | bytes 393220
  159.2 9.1 %copy-start.9 = (f32[512,128]{1,0:T(8,128)S(1)}, f32[512,128]{1,0:T(8,128)}, u32[]{:S(2)}) copy-start(f32[512,128]{1,0:T(8,128)} %copy-done.8) | copy-start | bytes 786436
  159.2 9.1 %copy-start.10 = (f32[16,64]{1,0:T(8,128)S(1)}, f32[16,64]{1,0:T(8,128)}, u32[]{:S(2)}) copy-start(f32[16,64]{1,0:T(8,128)} %teacher_ref.1) | copy-start | bytes 12292

commit v4 on v3

--- a/solution.py
+++ b/solution.py
@@ -12,7 +12,7 @@
 epsilon = 1e-06
 LOG2E = 1.4426950408889634
 GROUP = 4
-UNITS = 8
+UNITS = 12
 LOADS = 8
 LOAD_STEP = 16
 NEG_STEP = 8
@@ -191,11 +191,12 @@
         return found
 
     def forward(step, carry):
-        expos, weights = [], []
+        expos, weights, rows = [], [], []
         for u in range(UNITS):
             _, q, base = entry(step * UNITS + u)
             for g in range(GROUP):
-                inverse = inverse_ref[pl.ds(rows_ref[q, base + g], 1), :]
+                rows.append(rows_ref[q, base + g])
+                inverse = inverse_ref[pl.ds(rows[-1], 1), :]
                 raw = raw_ref[u, :, g * wide : (g + 1) * wide]
                 expo = jnp.exp2(raw * (inverse * (LOG2E / inner_temp)))
                 expos.append(expo.astype(jnp.bfloat16))
@@ -203,12 +204,10 @@
         following = multiply(step + 1)
         backs = []
         for u in range(UNITS):
-            _, tiles = tiles_of(step * UNITS + u, index_ref)
-            for g in range(0, GROUP, 2):
-                k = u * GROUP + g
+            for k in range(u * GROUP, (u + 1) * GROUP, 2):
                 part = dot(
                     jnp.concatenate(weights[k : k + 2], axis=0),
-                    jnp.concatenate(tiles[g : g + 2], axis=1),
+                    jnp.concatenate([index_ref[row] for row in rows[k : k + 2]], axis=1),
                 )
                 backs += [part[:tokens, :dim], part[tokens:, dim:]]
         totals = []
@@ -334,7 +333,7 @@
 
 
 def neg_kernel(rows_ref, queries_ref, shard_ref, index_ref, turned_ref, inverse_ref, acc_ref, sums_ref,
-               sems, unit_ref, expo_ref, total_ref, left_ref, back_ref, *, tokens):
+               sems, unit_ref, expo_ref, total_ref, left_ref, back_ref, raw_ref, *, tokens):
     total = rows_ref.shape[0]
     chunk = expo_ref.shape[0]
     height, dim = queries_ref.shape
@@ -353,21 +352,24 @@
     same = jnp.where(same, 1.0, 0.0).astype(jnp.bfloat16)
 
     def block(number, carry):
+        def tiles_of(step):
+            first = number * chunk + jnp.minimum(step, chunk // NEG_STEP - 1) * NEG_STEP
+            return jnp.concatenate([index_ref[rows_ref[first + g]] for g in range(NEG_STEP)], axis=0)
+
         def forward(step, carry):
             first = step * NEG_STEP
-            tiles = jnp.concatenate(
-                [index_ref[rows_ref[number * chunk + first + g]] for g in range(NEG_STEP)], axis=0
-            )
-            raw = dot(tiles, unit_ref[...])
-            broad = tiles.astype(jnp.float32)
+            broad = tiles_of(step).astype(jnp.float32)
             inverse = lax.rsqrt(jnp.sum(broad * broad, axis=-1, keepdims=True) + epsilon)
-            expo = jnp.exp2(raw * (inverse * (LOG2E / inner_temp)))
+            expo = jnp.exp2(raw_ref[...] * (inverse * (LOG2E / inner_temp)))
+            following = dot(tiles_of(step + 1), unit_ref[...])
             for g in range(NEG_STEP):
                 part = slice(g * wide, (g + 1) * wide)
                 expo_ref[first + g] = (expo[part] * inverse[part]).astype(jnp.bfloat16)
                 total_ref[pl.ds(first + g, 1), :] = jnp.sum(expo[part], axis=0, keepdims=True)
+            raw_ref[...] = following
             return carry
 
+        raw_ref[...] = dot(tiles_of(0), unit_ref[...])
         lax.fori_loop(0, chunk // NEG_STEP, forward, 0)
         for c in range(height // lanes):
             part = slice(c * lanes, (c + 1) * lanes)
@@ -423,6 +425,7 @@
             pltpu.VMEM((chunk, height), jnp.float32),
             pltpu.VMEM((chunk, height), jnp.float32),
             pltpu.VMEM((dim, height), jnp.float32),
+            pltpu.VMEM((NEG_STEP * wide, height), jnp.float32),
         ],
         compiler_params=pltpu.CompilerParams(vmem_limit_bytes=VMEM_LIMIT),
         cost_estimate=pl.CostEstimate(
@@ -509,7 +512,6 @@
     messages = []
     order = list(range(1, owners)) + [0]
     groups = [order[first : first + SOURCES] for first in range(0, owners, SOURCES)]
-    groups = groups[:-1] + [groups[-1][:-1], groups[-1][-1:]]
     for steps in groups:
         sources = [lax.rem(me + step, owners) for step in steps]
         found = pairs(

time: 171 us -> 167 us (0.977); the launches traced: 172 us -> 166 us
  local copies, waits for them, and re-layouts: 38.9 us -> 26.7 us
  Pallas kernels: 106 us -> 94.1 us
  waiting for transfers between devices: 2.39 us -> 13.7 us
  starting transfers between devices: 11.8 us -> 19.1 us
    pallas_call x5 -> x4, Pallas kernels: 73.9 us -> 60.5 us  [pairs(): pl.pallas_call(functools.partial(pair_kernel, cands=cands, sources=len(so...]
    ppermute x7, waiting for transfers between devices: 0.02 us -> 12.5 us  [on_device(): lax.ppermute(message, 'corpus', [(i, (i + step) % owners) for i in range(...]
    unnamed x22 -> x14, local copies, waits for them, and re-layouts: 36.1 us -> 23.9 us
    ppermute x7, starting transfers between devices: 2.81 us -> 9.11 us  [on_device(): lax.ppermute(message, 'corpus', [(i, (i + step) % owners) for i in range(...]
    pallas_call x1, Pallas kernels: 24.5 us -> 26.6 us  [negatives(): pl.pallas_call(functools.partial(neg_kernel, tokens=tokens), in_specs=[pl...]
  transfers between devices with their start and end apart: 11 -> 11, of which waited for: 2 -> 4; matrix products, arithmetic and copies ran while one was open for 1% -> 1% of each run, Pallas kernels for 55% -> 47%
where the time goes in v4:
time: 167 us; the launch traced here: 166 us
  Pallas kernels  94.1 us (56%)
  local copies, waits for them, and re-layouts  26.7 us (16%)
  starting transfers between devices  19.1 us (11%)
  waiting for transfers between devices  13.7 us (8%)
  blocking collectives  9.28 us (6%)
  other arithmetic  2.45 us (1%)
    pallas_call x4, Pallas kernels, pairs(): pl.pallas_call(functools.partial(pair_kernel, cands=cands, sources=len(so...  60.5 us
    pallas_call x1, Pallas kernels, negatives(): pl.pallas_call(functools.partial(neg_kernel, tokens=tokens), in_specs=[pl...  26.6 us
    unnamed x14, local copies, waits for them, and re-layouts  23.9 us
    ppermute x7, waiting for transfers between devices, on_device(): lax.ppermute(message, 'corpus', [(i, (i + step) % owners) for i in range(...  12.5 us
    all_to_all x1, blocking collectives, told(): lax.all_to_all(copies, 'corpus', split_axis=0, concat_axis=0, tiled=True)  9.28 us
    ppermute x7, starting transfers between devices, on_device(): lax.ppermute(message, 'corpus', [(i, (i + step) % owners) for i in range(...  9.11 us
    all_to_all x1, starting transfers between devices, told(): lax.all_to_all(copies, 'corpus', split_axis=0, concat_axis=0, tiled=True)  7.01 us
    pallas_call x1, Pallas kernels, prep(): pl.pallas_call(functools.partial(prep_kernel, shard=shard, cands=cands),...  4.98 us
  transfers between devices with their start and end apart: 11, of which 4 were waited for; matrix products, arithmetic and copies ran while one was open for 1% of the time, Pallas kernels for 47%

profile of v4, /device:TPU:20, one launch (start us, length us, event | category | flops | bytes accessed | tf_op | source)
XLA Modules:
  0.0 166.1 jit_solution(338929375971046695)
XLA Ops:
  0.6 0.7 fusion
  1.4 0.8 pad_maximum_fusion
  2.1 9.3 %all_to_all.10 = f32[8,16,128]{2,1,0:T(8,128)S(1)} all-to-all(f32[8,16,128]{2,1,0:T(8,128)S(1)} %broadcast_in_dim.4), channel_id=1, replica_groups=mesh['corpus'=8,'blk'=4] {'corpus'}, dimensions={0} | all-to-all | bytes 131072 | tf_op jit(solution)/shard_map/all_to_all | solution.py:505
  11.4 2.1 %broadcast_in_dim.5 = bf16[8,16,32,128]{3,2,1,0:T(8,128)(2,1)} broadcast(bf16[16,32,128]{2,1,0:T(8,128)(2,1)} %queries_ref.1), dimensions={1,2,3} | broadcast | bytes 1179648 | tf_op jit(solution)/shard_map/broadcast_in_dim | solution.py:504
  13.5 7.0 %all-to-all-start.1 = ((bf16[8,16,32,128]{3,2,1,0:T(8,128)(2,1)}), bf16[8,16,32,128]{3,2,1,0:T(8,128)(2,1)S(1)}, u32[]{:S(2)}, u32[]{:S(2)}) async-start(bf16[8,16,32,128]{3,2,1,0:T(8,128)(2,1)} %broadcast_in_dim.5), calls=%async_computation.1 | async-start | bytes 2097152 | tf_op jit(solution)/shard_map/all_to_all | solution.py:505
  20.5 1.5 collective-permute-start.1
  22.0 1.4 collective-permute-start
  23.5 0.1 pad_add_fusion.1.source_ref
  23.6 0.1 pad_add_fusion.3.source_ref
  23.7 0.1 pad_add_fusion.4.source_ref
  23.8 0.4 collective-permute-done.1
  24.2 0.7 collective-permute-done
  24.9 0.7 pad_add_fusion
  25.6 0.1 reshape.22.rows_ref
  25.7 5.0 %prep.1 = (s32[128,128]{1,0:T(8,128)S(1)}, f32[2048,128]{1,0:T(8,128)S(1)}) custom-call(s32[1]{0:T(128)} %bitcast.me_ref, f32[128,128]{1,0:T(8,128)S(1)} %bitcast.17), custom_call_target="tpu_custom_call" | custom-call | flops 16384 | bytes 16384 | tf_op jit(solution)/shard_map/prep/pallas_call | solution.py:133
  30.7 0.9 copy-done.4
  31.5 26.6 %negatives.1 = (bf16[512,128,128]{2,1,0:T(8,128)(2,1)S(1)}, bf16[512,128,128]{2,1,0:T(8,128)(2,1)S(1)}, f32[512,128]{1,0:T(8,128)S(1)}, f32[512,128]{1,0:T(8,128)S(1)}, f32[8,512]{1,0:T(8,128)S(1)}) custom-call(s32[96]{0:T(128)S(1)} %reshape.22.rows_ref, bf16[512,128]{1,0:T(8,128)(2,1)S(1)} %bitcast.16, bf16[512,128,128]{2,1,0:T(8,128)(2,1)} %shard_ref.1), custom_call_target="tpu_custom_call" | custom-call | flops 3221225472 | bytes 3145728 | tf_op jit(solution)/shard_map/negatives/pallas_call | solution.py:406
  58.2 5.7 %copy-done = bf16[512,128,128]{2,1,0:T(8,128)(2,1)} copy-done((bf16[512,128,128]{2,1,0:T(8,128)(2,1)}, bf16[512,128,128]{2,1,0:T(8,128)(2,1)S(1)}, u32[]{:S(2)}) %copy-start) | copy-done | bytes 16777240
  63.9 5.7 %copy-done.2 = bf16[512,128,128]{2,1,0:T(8,128)(2,1)} copy-done((bf16[512,128,128]{2,1,0:T(8,128)(2,1)}, bf16[512,128,128]{2,1,0:T(8,128)(2,1)S(1)}, u32[]{:S(2)}) %copy-start.2) | copy-done | bytes 16777240
  69.6 5.8 %copy-done.1 = bf16[512,128,128]{2,1,0:T(8,128)(2,1)S(1)} copy-done((bf16[512,128,128]{2,1,0:T(8,128)(2,1)S(1)}, bf16[512,128,128]{2,1,0:T(8,128)(2,1)}, u32[]{:S(2)}) %copy-start.1) | copy-done | bytes 16777240
  75.4 5.8 %copy-done.3 = bf16[512,128,128]{2,1,0:T(8,128)(2,1)S(1)} copy-done((bf16[512,128,128]{2,1,0:T(8,128)(2,1)S(1)}, bf16[512,128,128]{2,1,0:T(8,128)(2,1)}, u32[]{:S(2)}) %copy-start.3) | copy-done | bytes 16777240
  81.2 13.5 %pairs.4 = (bf16[1072,128]{1,0:T(8,128)(2,1)S(1)}, bf16[1072,128]{1,0:T(8,128)(2,1)S(1)}) custom-call(s32[2]{0:T(128)S(1)} %pad_add_fusion.1.source_ref, s32[128,128]{1,0:T(8,128)S(1)} %get-tuple-element.25.rows_ref, f32[2048,128]{1,0:T(8,128)S(1)} %get-tuple-element.26.target_ref, bf16[8,16,32,128]{3,2,1,0:T(8,128)(2,1)S(1)} %all-to-all-done.1.queries_ref, ...), custom_call_target="tpu_custom_call" | custom-call | flops 1610612736 | bytes 16777216 | tf_op jit(solution)/shard_map/pairs/pallas_call | solution.py:299
  94.7 1.5 collective-permute-start.4
  96.2 14.6 %pairs.5 = (bf16[1072,128]{1,0:T(8,128)(2,1)S(1)}, bf16[1072,128]{1,0:T(8,128)(2,1)S(1)}) custom-call(s32[2]{0:T(128)S(1)} %pad_add_fusion.2.source_ref, s32[128,128]{1,0:T(8,128)S(1)} %get-tuple-element.25.rows_ref, f32[2048,128]{1,0:T(8,128)S(1)} %get-tuple-element.26.target_ref, bf16[8,16,32,128]{3,2,1,0:T(8,128)(2,1)S(1)} %all-to-all-done.1.queries_ref, ...), custom_call_target="tpu_custom_call" | custom-call | flops 1610612736 | bytes 16777216 | tf_op jit(solution)/shard_map/pairs/pallas_call | solution.py:299
  110.8 7.1 %collective-permute-start.6 = (bf16[1072,128]{1,0:T(8,128)(2,1)S(1)}, bf16[1072,128]{1,0:T(8,128)(2,1)S(1)}, u32[]{:S(2)}, u32[]{:S(2)}) collective-permute-start(bf16[1072,128]{1,0:T(8,128)(2,1)S(1)} %get-tuple-element.33), channel_id=1, source_target_pairs={{0,16},{4,20},{8,24},{12,28},{16,0},{20,4},{24,8},{28,12},{1,17},{... | collective-permute-start | bytes 823304 | tf_op jit(solution)/shard_map/ppermute | solution.py:522
  118.0 16.8 %pairs.6 = (bf16[1072,128]{1,0:T(8,128)(2,1)S(1)}, bf16[1072,128]{1,0:T(8,128)(2,1)S(1)}) custom-call(s32[2]{0:T(128)S(1)} %pad_add_fusion.3.source_ref, s32[128,128]{1,0:T(8,128)S(1)} %get-tuple-element.25.rows_ref, f32[2048,128]{1,0:T(8,128)S(1)} %get-tuple-element.26.target_ref, bf16[8,16,32,128]{3,2,1,0:T(8,128)(2,1)S(1)} %all-to-all-done.1.queries_ref, ...), custom_call_target="tpu_custom_call" | custom-call | flops 1610612736 | bytes 16777216 | tf_op jit(solution)/shard_map/pairs/pallas_call | solution.py:299
  134.8 0.2 collective-permute-start.7
  135.1 15.7 %pairs.7 = (bf16[1072,128]{1,0:T(8,128)(2,1)S(1)}, bf16[1072,128]{1,0:T(8,128)(2,1)S(1)}) custom-call(s32[2]{0:T(128)S(1)} %pad_add_fusion.4.source_ref, s32[128,128]{1,0:T(8,128)S(1)} %get-tuple-element.25.rows_ref, f32[2048,128]{1,0:T(8,128)S(1)} %get-tuple-element.26.target_ref, bf16[8,16,32,128]{3,2,1,0:T(8,128)(2,1)S(1)} %all-to-all-done.1.queries_ref, ...), custom_call_target="tpu_custom_call" | custom-call | flops 1610612736 | bytes 16777216 | tf_op jit(solution)/shard_map/pairs/pallas_call | solution.py:299
  150.9 6.4 %collective-permute-done.8.refs_5_ = bf16[1072,128]{1,0:T(8,128)(2,1)S(1)} collective-permute-done((bf16[1072,128]{1,0:T(8,128)(2,1)S(1)}, bf16[1072,128]{1,0:T(8,128)(2,1)S(1)}, u32[]{:S(2)}, u32[]{:S(2)}) %collective-permute-start.8) | collective-permute-done | bytes 274464 | tf_op jit(solution)/shard_map/ppermute | solution.py:522
  157.3 6.1 %collective-permute-done.9.refs_6_ = bf16[1072,128]{1,0:T(8,128)(2,1)S(1)} collective-permute-done((bf16[1072,128]{1,0:T(8,128)(2,1)S(1)}, bf16[1072,128]{1,0:T(8,128)(2,1)S(1)}, u32[]{:S(2)}, u32[]{:S(2)}) %collective-permute-start.9) | collective-permute-done | bytes 274464 | tf_op jit(solution)/shard_map/ppermute | solution.py:522
  163.5 2.0 %finish.1 = (f32[16,128]{1,0:T(8,128)S(1)}, f32[16,32,128]{2,1,0:T(8,128)}) custom-call(bf16[16,32,128]{2,1,0:T(8,128)(2,1)S(1)} %copy-done.5, f32[16,64]{1,0:T(8,128)S(1)} %copy-done.6, f32[512,128]{1,0:T(8,128)S(1)} %get-tuple-element.23.back_ref, f32[8,512]{1,0:T(8,128)S(1)} %get-tuple-element.24.sums_ref, ...), custom_call_target="tpu_custom_call" | custom-call | tf_op jit(solution)/shard_map/finish/pallas_call | solution.py:472
  165.5 0.6 slice_reduce_fusion
  (23 shorter events, 0.4 us)
Async XLA Ops:
  13.5 56.1 %all-to-all-start.1 = ((bf16[8,16,32,128]{3,2,1,0:T(8,128)(2,1)}), bf16[8,16,32,128]{3,2,1,0:T(8,128)(2,1)S(1)}, u32[]{:S(2)}, u32[]{:S(2)}) async-start(bf16[8,16,32,128]{3,2,1,0:T(8,128)(2,1)} %broadcast_in_dim.5), calls=%async_computation.1 | async-start | bytes 2097152 | tf_op jit(solution)/shard_map/all_to_all | solution.py:505
  20.5 3.3 %collective-permute-start.2 = (s32[1,24]{1,0:T(1,128)}, s32[1,24]{1,0:T(1,128)S(1)}, u32[]{:S(2)}, u32[]{:S(2)}) collective-permute-start(s32[1,24]{1,0:T(1,128)} %param.10), channel_id=1, source_target_pairs={{3,0},{0,1},{1,2},{2,3},{7,4},{4,5},{5,6},{6,7},{11,8},{8,9},{9,10... | collective-permute-start | bytes 296 | tf_op jit(solution)/shard_map/ppermute | solution.py:495
  20.5 3.7 %collective-permute-start.1 = (s32[1,24]{1,0:T(1,128)}, s32[1,24]{1,0:T(1,128)S(1)}, u32[]{:S(2)}, u32[]{:S(2)}) collective-permute-start(s32[1,24]{1,0:T(1,128)} %param.10), channel_id=1, source_target_pairs={{2,0},{3,1},{0,2},{1,3},{6,4},{7,5},{4,6},{5,7},{10,8},{11,9},{8,1... | collective-permute-start | bytes 296 | tf_op jit(solution)/shard_map/ppermute | solution.py:495
  22.0 2.9 %collective-permute-start = (s32[1,24]{1,0:T(1,128)}, s32[1,24]{1,0:T(1,128)S(1)}, u32[]{:S(2)}, u32[]{:S(2)}) collective-permute-start(s32[1,24]{1,0:T(1,128)} %param.10), channel_id=1, source_target_pairs={{1,0},{2,1},{3,2},{0,3},{5,4},{6,5},{7,6},{4,7},{9,8},{10,9},{11,1... | collective-permute-start | bytes 296 | tf_op jit(solution)/shard_map/ppermute | solution.py:495
  30.6 0.9 copy-start.4
  58.1 5.7 %copy-start = (bf16[512,128,128]{2,1,0:T(8,128)(2,1)}, bf16[512,128,128]{2,1,0:T(8,128)(2,1)S(1)}, u32[]{:S(2)}) copy-start(bf16[512,128,128]{2,1,0:T(8,128)(2,1)S(1)} %get-tuple-element.28.index_ref) | copy-start | bytes 50331652
  63.9 5.7 %copy-start.2 = (bf16[512,128,128]{2,1,0:T(8,128)(2,1)}, bf16[512,128,128]{2,1,0:T(8,128)(2,1)S(1)}, u32[]{:S(2)}) copy-start(bf16[512,128,128]{2,1,0:T(8,128)(2,1)S(1)} %get-tuple-element.29.turned_ref) | copy-start | bytes 50331652
  69.6 5.8 %copy-start.1 = (bf16[512,128,128]{2,1,0:T(8,128)(2,1)S(1)}, bf16[512,128,128]{2,1,0:T(8,128)(2,1)}, u32[]{:S(2)}) copy-start(bf16[512,128,128]{2,1,0:T(8,128)(2,1)} %copy-done) | copy-start | bytes 50331652
  75.4 5.8 %copy-start.3 = (bf16[512,128,128]{2,1,0:T(8,128)(2,1)S(1)}, bf16[512,128,128]{2,1,0:T(8,128)(2,1)}, u32[]{:S(2)}) copy-start(bf16[512,128,128]{2,1,0:T(8,128)(2,1)} %copy-done.2) | copy-start | bytes 50331652
  94.6 56.1 %collective-permute-start.3 = (bf16[1072,128]{1,0:T(8,128)(2,1)S(1)}, bf16[1072,128]{1,0:T(8,128)(2,1)S(1)}, u32[]{:S(2)}, u32[]{:S(2)}) collective-permute-start(bf16[1072,128]{1,0:T(8,128)(2,1)S(1)} %get-tuple-element.30), channel_id=1, source_target_pairs={{0,4},{4,8},{8,12},{12,16},{16,20},{20,24},{24,28},{28,0},{1,5},{5... | collective-permute-start | bytes 823304 | tf_op jit(solution)/shard_map/ppermute | solution.py:522
  94.7 56.2 %collective-permute-start.4 = (bf16[1072,128]{1,0:T(8,128)(2,1)S(1)}, bf16[1072,128]{1,0:T(8,128)(2,1)S(1)}, u32[]{:S(2)}, u32[]{:S(2)}) collective-permute-start(bf16[1072,128]{1,0:T(8,128)(2,1)S(1)} %get-tuple-element.31), channel_id=1, source_target_pairs={{0,8},{4,12},{8,16},{12,20},{16,24},{20,28},{24,0},{28,4},{1,9},{5... | collective-permute-start | bytes 823304 | tf_op jit(solution)/shard_map/ppermute | solution.py:522
  110.8 40.1 %collective-permute-start.5 = (bf16[1072,128]{1,0:T(8,128)(2,1)S(1)}, bf16[1072,128]{1,0:T(8,128)(2,1)S(1)}, u32[]{:S(2)}, u32[]{:S(2)}) collective-permute-start(bf16[1072,128]{1,0:T(8,128)(2,1)S(1)} %get-tuple-element.32), channel_id=1, source_target_pairs={{0,12},{4,16},{8,20},{12,24},{16,28},{20,0},{24,4},{28,8},{1,13},{... | collective-permute-start | bytes 823304 | tf_op jit(solution)/shard_map/ppermute | solution.py:522
  110.8 40.1 %collective-permute-start.6 = (bf16[1072,128]{1,0:T(8,128)(2,1)S(1)}, bf16[1072,128]{1,0:T(8,128)(2,1)S(1)}, u32[]{:S(2)}, u32[]{:S(2)}) collective-permute-start(bf16[1072,128]{1,0:T(8,128)(2,1)S(1)} %get-tuple-element.33), channel_id=1, source_target_pairs={{0,16},{4,20},{8,24},{12,28},{16,0},{20,4},{24,8},{28,12},{1,17},{... | collective-permute-start | bytes 823304 | tf_op jit(solution)/shard_map/ppermute | solution.py:522
  134.8 28.7 %copy-start.5 = (bf16[16,32,128]{2,1,0:T(8,128)(2,1)S(1)}, bf16[16,32,128]{2,1,0:T(8,128)(2,1)}, u32[]{:S(2)}) copy-start(bf16[16,32,128]{2,1,0:T(8,128)(2,1)} %queries_ref.1) | copy-start | bytes 393220
  134.8 28.7 %copy-start.6 = (f32[16,64]{1,0:T(8,128)S(1)}, f32[16,64]{1,0:T(8,128)}, u32[]{:S(2)}) copy-start(f32[16,64]{1,0:T(8,128)} %teacher_ref.1) | copy-start | bytes 12292
  134.8 16.1 %collective-permute-start.7 = (bf16[1072,128]{1,0:T(8,128)(2,1)S(1)}, bf16[1072,128]{1,0:T(8,128)(2,1)S(1)}, u32[]{:S(2)}, u32[]{:S(2)}) collective-permute-start(bf16[1072,128]{1,0:T(8,128)(2,1)S(1)} %get-tuple-element.34), channel_id=1, source_target_pairs={{0,20},{4,24},{8,28},{12,0},{16,4},{20,8},{24,12},{28,16},{1,21},{... | collective-permute-start | bytes 823304 | tf_op jit(solution)/shard_map/ppermute | solution.py:522
  150.8 6.6 %collective-permute-start.8 = (bf16[1072,128]{1,0:T(8,128)(2,1)S(1)}, bf16[1072,128]{1,0:T(8,128)(2,1)S(1)}, u32[]{:S(2)}, u32[]{:S(2)}) collective-permute-start(bf16[1072,128]{1,0:T(8,128)(2,1)S(1)} %get-tuple-element.35), channel_id=1, source_target_pairs={{0,24},{4,28},{8,0},{12,4},{16,8},{20,12},{24,16},{28,20},{1,25},{... | collective-permute-start | bytes 823304 | tf_op jit(solution)/shard_map/ppermute | solution.py:522
  150.8 12.6 %collective-permute-start.9 = (bf16[1072,128]{1,0:T(8,128)(2,1)S(1)}, bf16[1072,128]{1,0:T(8,128)(2,1)S(1)}, u32[]{:S(2)}, u32[]{:S(2)}) collective-permute-start(bf16[1072,128]{1,0:T(8,128)(2,1)S(1)} %get-tuple-element.36), channel_id=1, source_target_pairs={{0,28},{4,0},{8,4},{12,8},{16,12},{20,16},{24,20},{28,24},{1,29},{... | collective-permute-start | bytes 823304 | tf_op jit(solution)/shard_map/ppermute | solution.py:522

commit v5 on v4

--- a/solution.py
+++ b/solution.py
@@ -12,13 +12,13 @@
 epsilon = 1e-06
 LOG2E = 1.4426950408889634
 GROUP = 4
-UNITS = 12
+UNITS = 24
 LOADS = 8
 LOAD_STEP = 16
 NEG_STEP = 8
 NEG_CHUNK = 24
 SOURCES = 2
-VMEM_LIMIT = 12 * 1024 * 1024
+VMEM_LIMIT = 14 * 1024 * 1024
 LAST = (((1,), (1,)), ((), ()))
 
 
@@ -74,6 +74,28 @@
             return carry
 
         lax.fori_loop(0, chunk // LOAD_STEP, body, 0)
+
+
+def load(index):
+    count, tokens, dim = index.shape
+    return pl.pallas_call(
+        load_shard,
+        in_specs=[pl.BlockSpec(memory_space=pltpu.HBM)],
+        out_specs=[pl.BlockSpec(memory_space=pltpu.VMEM)] * 3,
+        out_shape=[
+            pltpu.VMEM((count, tokens, dim), jnp.bfloat16),
+            pltpu.VMEM((count, dim, tokens), jnp.bfloat16),
+            pltpu.VMEM((count, tokens), jnp.float32),
+        ],
+        scratch_shapes=[pltpu.SemaphoreType.DMA((LOADS,))],
+        compiler_params=pltpu.CompilerParams(vmem_limit_bytes=VMEM_LIMIT),
+        cost_estimate=pl.CostEstimate(
+            flops=2 * count * tokens * dim,
+            bytes_accessed=2 * count * tokens * dim,
+            transcendentals=count * tokens,
+        ),
+        name="load",
+    )(pltpu.with_memory_space_constraint(index, pltpu.HBM))
 
 
 def prep_kernel(me_ref, meta_ref, rows_ref, target_ref, value_ref, place_ref, result_ref, *, shard, cands):
@@ -332,38 +354,56 @@
     )(jnp.stack(sources), rows, targets, queries, inverse, index, turned)
 
 
-def neg_kernel(rows_ref, queries_ref, shard_ref, index_ref, turned_ref, inverse_ref, acc_ref, sums_ref,
-               sems, unit_ref, expo_ref, total_ref, left_ref, back_ref, raw_ref, *, tokens):
+def neg_kernel(rows_ref, queries_ref, shard_ref, acc_ref, sums_ref,
+               unit_ref, expo_ref, total_ref, left_ref, back_ref, raw_ref, tiles_ref, turned_ref, sems,
+               *, tokens):
     total = rows_ref.shape[0]
     chunk = expo_ref.shape[0]
     height, dim = queries_ref.shape
-    wide = index_ref.shape[1]
+    wide = shard_ref.shape[1]
     lanes = 128
     half = min(height, 256)
+    def fetch(number):
+        place = jnp.bitwise_and(number, 1)
+        for k in range(chunk):
+            pltpu.make_async_copy(
+                shard_ref.at[rows_ref[number * chunk + k]], tiles_ref.at[place, k], sems.at[place]
+            ).start()
+
+    fetch(jnp.int32(0))
     for c in range(height // lanes):
         part = slice(c * lanes, (c + 1) * lanes)
         unit_ref[:, part] = rounded_queries(queries_ref[part]).T
-    load_shard(shard_ref, index_ref, turned_ref, inverse_ref, sems)
     back_ref[...] = jnp.zeros_like(back_ref)
     sums_ref[...] = jnp.zeros_like(sums_ref)
+
     same = lax.broadcasted_iota(jnp.int32, (lanes, lanes), 0) // tokens == lax.broadcasted_iota(
         jnp.int32, (lanes, lanes), 1
     ) // tokens
     same = jnp.where(same, 1.0, 0.0).astype(jnp.bfloat16)
 
     def block(number, carry):
+        @pl.when(number + 1 < total // chunk)
+        def _():
+            fetch(number + 1)
+
+        place = jnp.bitwise_and(number, 1)
+        pltpu.make_async_copy(shard_ref.at[pl.ds(0, chunk)], tiles_ref.at[place], sems.at[place]).wait()
+
         def tiles_of(step):
-            first = number * chunk + jnp.minimum(step, chunk // NEG_STEP - 1) * NEG_STEP
-            return jnp.concatenate([index_ref[rows_ref[first + g]] for g in range(NEG_STEP)], axis=0)
+            first = jnp.minimum(step, chunk // NEG_STEP - 1) * NEG_STEP
+            return tiles_ref[place, pl.ds(first, NEG_STEP)].reshape(NEG_STEP * wide, dim)
 
         def forward(step, carry):
             first = step * NEG_STEP
-            broad = tiles_of(step).astype(jnp.float32)
+            tiles = tiles_of(step)
+            broad = tiles.astype(jnp.float32)
             inverse = lax.rsqrt(jnp.sum(broad * broad, axis=-1, keepdims=True) + epsilon)
             expo = jnp.exp2(raw_ref[...] * (inverse * (LOG2E / inner_temp)))
             following = dot(tiles_of(step + 1), unit_ref[...])
             for g in range(NEG_STEP):
                 part = slice(g * wide, (g + 1) * wide)
+                turned_ref[first + g] = tiles[part].T
                 expo_ref[first + g] = (expo[part] * inverse[part]).astype(jnp.bfloat16)
                 total_ref[pl.ds(first + g, 1), :] = jnp.sum(expo[part], axis=0, keepdims=True)
             raw_ref[...] = following
@@ -384,8 +424,7 @@
             def backward(step, acc):
                 for g in range(NEG_STEP):
                     k = step * NEG_STEP + g
-                    tile = turned_ref[rows_ref[number * chunk + k]]
-                    acc = acc + dot(tile, expo_ref[k, :, part]) * left_ref[pl.ds(k, 1), part]
+                    acc = acc + dot(turned_ref[k], expo_ref[k, :, part]) * left_ref[pl.ds(k, 1), part]
                 return acc
 
             back_ref[:, part] = lax.fori_loop(0, chunk // NEG_STEP, backward, back_ref[:, part])
@@ -410,24 +449,23 @@
             pl.BlockSpec(memory_space=pltpu.VMEM),
             pl.BlockSpec(memory_space=pltpu.HBM),
         ],
-        out_specs=[pl.BlockSpec(memory_space=pltpu.VMEM)] * 5,
+        out_specs=[pl.BlockSpec(memory_space=pltpu.VMEM)] * 2,
         out_shape=[
-            pltpu.VMEM(index.shape, jnp.bfloat16),
-            pltpu.VMEM((index.shape[0], dim, wide), jnp.bfloat16),
-            pltpu.VMEM((index.shape[0], wide), jnp.float32),
             jax.ShapeDtypeStruct((height, dim), jnp.float32),
             jax.ShapeDtypeStruct((8, height), jnp.float32),
         ],
         scratch_shapes=[
-            pltpu.SemaphoreType.DMA((LOADS,)),
             pltpu.VMEM((dim, height), jnp.bfloat16),
             pltpu.VMEM((chunk, wide, height), jnp.bfloat16),
             pltpu.VMEM((chunk, height), jnp.float32),
             pltpu.VMEM((chunk, height), jnp.float32),
             pltpu.VMEM((dim, height), jnp.float32),
             pltpu.VMEM((NEG_STEP * wide, height), jnp.float32),
-        ],
-        compiler_params=pltpu.CompilerParams(vmem_limit_bytes=VMEM_LIMIT),
+            pltpu.VMEM((2, chunk, wide, dim), jnp.bfloat16),
+            pltpu.VMEM((chunk, dim, wide), jnp.bfloat16),
+            pltpu.SemaphoreType.DMA((2,)),
+        ],
+        compiler_params=pltpu.CompilerParams(vmem_limit_bytes=2 * VMEM_LIMIT),
         cost_estimate=pl.CostEstimate(
             flops=4 * total * height * wide * dim,
             bytes_accessed=2 * total * wide * dim,
@@ -508,7 +546,9 @@
     all_queries = told(queries)
     rows, targets = prep(me.reshape(1), all_meta, shard, cands)
     rows, all_neg = lax.optimization_barrier((rows, all_neg))
-    index, turned, inverse, neg_acc, neg_sum = negatives(all_neg, queries, index)
+    neg_acc, neg_sum = negatives(all_neg, queries, index)
+    index, all_queries, rows, neg_acc = lax.optimization_barrier((index, all_queries, rows, neg_acc))
+    index, turned, inverse = load(index)
     messages = []
     order = list(range(1, owners)) + [0]
     groups = [order[first : first + SOURCES] for first in range(0, owners, SOURCES)]

time: 167 us -> 167 us (level)
  the two profiles are of different devices: /device:TPU:20 before, /device:TPU:15 now
where the time goes in v5:
time: 167 us; the launch traced here: 168 us
  Pallas kernels  85.1 us (51%)
  local copies, waits for them, and re-layouts  26.7 us (16%)
  starting transfers between devices  26.5 us (16%)
  waiting for transfers between devices  17.1 us (10%)
  blocking collectives  9.51 us (6%)
  other arithmetic  2.45 us (1%)
    pallas_call x4, Pallas kernels, pairs(): pl.pallas_call(functools.partial(pair_kernel, cands=cands, sources=len(so...  50.2 us
    unnamed x14, local copies, waits for them, and re-layouts  23.9 us
    pallas_call x1, Pallas kernels, negatives(): pl.pallas_call(functools.partial(neg_kernel, tokens=tokens), in_specs=[pl...  19.3 us
    ppermute x7, starting transfers between devices, on_device(): lax.ppermute(message, 'corpus', [(i, (i + step) % owners) for i in range(...  17.6 us
    ppermute x7, waiting for transfers between devices, on_device(): lax.ppermute(message, 'corpus', [(i, (i + step) % owners) for i in range(...  14 us
    all_to_all x1, blocking collectives, told(): lax.all_to_all(copies, 'corpus', split_axis=0, concat_axis=0, tiled=True)  9.51 us
    pallas_call x1, Pallas kernels, load(): pl.pallas_call(load_shard, in_specs=[pl.BlockSpec(memory_space=pltpu.HBM)...  8.67 us
    all_to_all x1, starting transfers between devices, told(): lax.all_to_all(copies, 'corpus', split_axis=0, concat_axis=0, tiled=True)  5.17 us
  transfers between devices with their start and end apart: 11, of which 4 were waited for; matrix products, arithmetic and copies ran while one was open for 1% of the time, Pallas kernels for 37%

profile of v5, /device:TPU:15, one launch (start us, length us, event | category | flops | bytes accessed | tf_op | source)
XLA Modules:
  0.0 168.2 jit_solution(9838844191352711033)
XLA Ops:
  0.6 0.7 fusion
  1.4 0.8 pad_maximum_fusion
  2.1 9.5 %all_to_all.10 = f32[8,16,128]{2,1,0:T(8,128)S(1)} all-to-all(f32[8,16,128]{2,1,0:T(8,128)S(1)} %broadcast_in_dim.5), channel_id=1, replica_groups=mesh['corpus'=8,'blk'=4] {'corpus'}, dimensions={0} | all-to-all | bytes 131072 | tf_op jit(solution)/shard_map/all_to_all | solution.py:543
  11.6 2.1 %broadcast_in_dim.4 = bf16[8,16,32,128]{3,2,1,0:T(8,128)(2,1)} broadcast(bf16[16,32,128]{2,1,0:T(8,128)(2,1)} %queries_ref.1), dimensions={1,2,3} | broadcast | bytes 1179648 | tf_op jit(solution)/shard_map/broadcast_in_dim | solution.py:542
  13.7 5.2 %all-to-all-start = ((bf16[8,16,32,128]{3,2,1,0:T(8,128)(2,1)}), bf16[8,16,32,128]{3,2,1,0:T(8,128)(2,1)S(1)}, u32[]{:S(2)}, u32[]{:S(2)}) async-start(bf16[8,16,32,128]{3,2,1,0:T(8,128)(2,1)} %broadcast_in_dim.4), calls=%async_computation | async-start | bytes 2097152 | tf_op jit(solution)/shard_map/all_to_all | solution.py:543
  18.9 2.5 %collective-permute-start.2 = (s32[1,24]{1,0:T(1,128)}, s32[1,24]{1,0:T(1,128)S(1)}, u32[]{:S(2)}, u32[]{:S(2)}) collective-permute-start(s32[1,24]{1,0:T(1,128)} %param.10), channel_id=1, source_target_pairs={{3,0},{0,1},{1,2},{2,3},{7,4},{4,5},{5,6},{6,7},{11,8},{8,9},{9,10... | collective-permute-start | bytes 296 | tf_op jit(solution)/shard_map/ppermute | solution.py:533
  21.4 1.2 collective-permute-start.1
  22.9 1.0 collective-permute-done.1
  23.9 2.1 %collective-permute-done = s32[1,24]{1,0:T(1,128)S(1)} collective-permute-done((s32[1,24]{1,0:T(1,128)}, s32[1,24]{1,0:T(1,128)S(1)}, u32[]{:S(2)}, u32[]{:S(2)}) %collective-permute-start) | collective-permute-done | bytes 128 | tf_op jit(solution)/shard_map/ppermute | solution.py:533
  26.0 0.7 pad_add_fusion
  26.7 0.1 reshape.22.rows_ref
  26.8 5.0 %prep.1 = (s32[128,128]{1,0:T(8,128)S(1)}, f32[2048,128]{1,0:T(8,128)S(1)}) custom-call(s32[1]{0:T(128)} %bitcast.me_ref, f32[128,128]{1,0:T(8,128)S(1)} %bitcast.17), custom_call_target="tpu_custom_call" | custom-call | flops 16384 | bytes 16384 | tf_op jit(solution)/shard_map/prep/pallas_call | solution.py:155
  31.8 0.9 copy-done.4
  32.7 19.3 %negatives.1 = (f32[512,128]{1,0:T(8,128)S(1)}, f32[8,512]{1,0:T(8,128)S(1)}) custom-call(s32[96]{0:T(128)S(1)} %reshape.22.rows_ref, bf16[512,128]{1,0:T(8,128)(2,1)S(1)} %bitcast.16, bf16[512,128,128]{2,1,0:T(8,128)(2,1)} %index_ref), custom_call_target="tpu_custom_call" | custom-call | flops 3221225472 | bytes 3145728 | tf_op jit(solution)/shard_map/negatives/pallas_call | solution.py:445
  51.9 8.7 %load.1 = (bf16[512,128,128]{2,1,0:T(8,128)(2,1)S(1)}, bf16[512,128,128]{2,1,0:T(8,128)(2,1)S(1)}, f32[512,128]{1,0:T(8,128)S(1)}) custom-call(bf16[512,128,128]{2,1,0:T(8,128)(2,1)} %index_ref), custom_call_target="tpu_custom_call" | custom-call | flops 16777216 | bytes 16777216 | tf_op jit(solution)/shard_map/load/pallas_call | solution.py:81
  60.6 5.7 %copy-done = bf16[512,128,128]{2,1,0:T(8,128)(2,1)} copy-done((bf16[512,128,128]{2,1,0:T(8,128)(2,1)}, bf16[512,128,128]{2,1,0:T(8,128)(2,1)S(1)}, u32[]{:S(2)}) %copy-start) | copy-done | bytes 16777240
  66.3 5.8 %copy-done.2 = bf16[512,128,128]{2,1,0:T(8,128)(2,1)} copy-done((bf16[512,128,128]{2,1,0:T(8,128)(2,1)}, bf16[512,128,128]{2,1,0:T(8,128)(2,1)S(1)}, u32[]{:S(2)}) %copy-start.2) | copy-done | bytes 16777240
  72.1 5.8 %copy-done.1 = bf16[512,128,128]{2,1,0:T(8,128)(2,1)S(1)} copy-done((bf16[512,128,128]{2,1,0:T(8,128)(2,1)S(1)}, bf16[512,128,128]{2,1,0:T(8,128)(2,1)}, u32[]{:S(2)}) %copy-start.1) | copy-done | bytes 16777240
  77.9 5.8 %copy-done.3 = bf16[512,128,128]{2,1,0:T(8,128)(2,1)S(1)} copy-done((bf16[512,128,128]{2,1,0:T(8,128)(2,1)S(1)}, bf16[512,128,128]{2,1,0:T(8,128)(2,1)}, u32[]{:S(2)}) %copy-start.3) | copy-done | bytes 16777240
  83.6 12.0 %pairs.4 = (bf16[1072,128]{1,0:T(8,128)(2,1)S(1)}, bf16[1072,128]{1,0:T(8,128)(2,1)S(1)}) custom-call(s32[2]{0:T(128)S(1)} %pad_add_fusion.1.source_ref, s32[128,128]{1,0:T(8,128)S(1)} %get-tuple-element.31.rows_ref, f32[2048,128]{1,0:T(8,128)S(1)} %get-tuple-element.32.target_ref, bf16[8,16,32,128]{3,2,1,0:T(8,128)(2,1)S(1)} %all-to-all-done.queries_ref, ...), custom_call_target="tpu_custom_call" | custom-call | flops 1610612736 | bytes 16777216 | tf_op jit(solution)/shard_map/pairs/pallas_call | solution.py:321
  95.7 5.4 %collective-permute-start.4 = (bf16[1072,128]{1,0:T(8,128)(2,1)S(1)}, bf16[1072,128]{1,0:T(8,128)(2,1)S(1)}, u32[]{:S(2)}, u32[]{:S(2)}) collective-permute-start(bf16[1072,128]{1,0:T(8,128)(2,1)S(1)} %get-tuple-element.39), channel_id=1, source_target_pairs={{0,8},{4,12},{8,16},{12,20},{16,24},{20,28},{24,0},{28,4},{1,9},{5... | collective-permute-start | bytes 823304 | tf_op jit(solution)/shard_map/ppermute | solution.py:562
  101.1 14.1 %pairs.5 = (bf16[1072,128]{1,0:T(8,128)(2,1)S(1)}, bf16[1072,128]{1,0:T(8,128)(2,1)S(1)}) custom-call(s32[2]{0:T(128)S(1)} %pad_add_fusion.2.source_ref, s32[128,128]{1,0:T(8,128)S(1)} %get-tuple-element.31.rows_ref, f32[2048,128]{1,0:T(8,128)S(1)} %get-tuple-element.32.target_ref, bf16[8,16,32,128]{3,2,1,0:T(8,128)(2,1)S(1)} %all-to-all-done.queries_ref, ...), custom_call_target="tpu_custom_call" | custom-call | flops 1610612736 | bytes 16777216 | tf_op jit(solution)/shard_map/pairs/pallas_call | solution.py:321
  115.2 0.2 collective-permute-start.5
  115.5 5.5 %collective-permute-start.6 = (bf16[1072,128]{1,0:T(8,128)(2,1)S(1)}, bf16[1072,128]{1,0:T(8,128)(2,1)S(1)}, u32[]{:S(2)}, u32[]{:S(2)}) collective-permute-start(bf16[1072,128]{1,0:T(8,128)(2,1)S(1)} %get-tuple-element.41), channel_id=1, source_target_pairs={{0,16},{4,20},{8,24},{12,28},{16,0},{20,4},{24,8},{28,12},{1,17},{... | collective-permute-start | bytes 823304 | tf_op jit(solution)/shard_map/ppermute | solution.py:562
  121.0 12.0 %pairs.6 = (bf16[1072,128]{1,0:T(8,128)(2,1)S(1)}, bf16[1072,128]{1,0:T(8,128)(2,1)S(1)}) custom-call(s32[2]{0:T(128)S(1)} %pad_add_fusion.3.source_ref, s32[128,128]{1,0:T(8,128)S(1)} %get-tuple-element.31.rows_ref, f32[2048,128]{1,0:T(8,128)S(1)} %get-tuple-element.32.target_ref, bf16[8,16,32,128]{3,2,1,0:T(8,128)(2,1)S(1)} %all-to-all-done.queries_ref, ...), custom_call_target="tpu_custom_call" | custom-call | flops 1610612736 | bytes 16777216 | tf_op jit(solution)/shard_map/pairs/pallas_call | solution.py:321
  133.1 12.0 %pairs.7 = (bf16[1072,128]{1,0:T(8,128)(2,1)S(1)}, bf16[1072,128]{1,0:T(8,128)(2,1)S(1)}) custom-call(s32[2]{0:T(128)S(1)} %pad_add_fusion.4.source_ref, s32[128,128]{1,0:T(8,128)S(1)} %get-tuple-element.31.rows_ref, f32[2048,128]{1,0:T(8,128)S(1)} %get-tuple-element.32.target_ref, bf16[8,16,32,128]{3,2,1,0:T(8,128)(2,1)S(1)} %all-to-all-done.queries_ref, ...), custom_call_target="tpu_custom_call" | custom-call | flops 1610612736 | bytes 16777216 | tf_op jit(solution)/shard_map/pairs/pallas_call | solution.py:321
  145.2 1.3 collective-permute-start.8
  146.5 5.1 %collective-permute-start.9 = (bf16[1072,128]{1,0:T(8,128)(2,1)S(1)}, bf16[1072,128]{1,0:T(8,128)(2,1)S(1)}, u32[]{:S(2)}, u32[]{:S(2)}) collective-permute-start(bf16[1072,128]{1,0:T(8,128)(2,1)S(1)} %get-tuple-element.44), channel_id=1, source_target_pairs={{0,28},{4,0},{8,4},{12,8},{16,12},{20,16},{24,20},{28,24},{1,29},{... | collective-permute-start | bytes 823304 | tf_op jit(solution)/shard_map/ppermute | solution.py:562
  151.6 4.0 %collective-permute-done.8.refs_5_ = bf16[1072,128]{1,0:T(8,128)(2,1)S(1)} collective-permute-done((bf16[1072,128]{1,0:T(8,128)(2,1)S(1)}, bf16[1072,128]{1,0:T(8,128)(2,1)S(1)}, u32[]{:S(2)}, u32[]{:S(2)}) %collective-permute-start.8) | collective-permute-done | bytes 274464 | tf_op jit(solution)/shard_map/ppermute | solution.py:562
  155.6 10.0 %collective-permute-done.9.refs_6_ = bf16[1072,128]{1,0:T(8,128)(2,1)S(1)} collective-permute-done((bf16[1072,128]{1,0:T(8,128)(2,1)S(1)}, bf16[1072,128]{1,0:T(8,128)(2,1)S(1)}, u32[]{:S(2)}, u32[]{:S(2)}) %collective-permute-start.9) | collective-permute-done | bytes 274464 | tf_op jit(solution)/shard_map/ppermute | solution.py:562
  165.6 2.0 %finish.1 = (f32[16,128]{1,0:T(8,128)S(1)}, f32[16,32,128]{2,1,0:T(8,128)}) custom-call(bf16[16,32,128]{2,1,0:T(8,128)(2,1)S(1)} %copy-done.5, f32[16,64]{1,0:T(8,128)S(1)} %copy-done.6, f32[512,128]{1,0:T(8,128)S(1)} %get-tuple-element.29.back_ref, f32[8,512]{1,0:T(8,128)S(1)} %get-tuple-element.30.sums_ref, ...), custom_call_target="tpu_custom_call" | custom-call | tf_op jit(solution)/shard_map/finish/pallas_call | solution.py:510
  167.6 0.6 slice_reduce_fusion
  (24 shorter events, 0.5 us)
Async XLA Ops:
  13.7 38.2 %all-to-all-start = ((bf16[8,16,32,128]{3,2,1,0:T(8,128)(2,1)}), bf16[8,16,32,128]{3,2,1,0:T(8,128)(2,1)S(1)}, u32[]{:S(2)}, u32[]{:S(2)}) async-start(bf16[8,16,32,128]{3,2,1,0:T(8,128)(2,1)} %broadcast_in_dim.4), calls=%async_computation | async-start | bytes 2097152 | tf_op jit(solution)/shard_map/all_to_all | solution.py:543
  18.9 4.0 %collective-permute-start.2 = (s32[1,24]{1,0:T(1,128)}, s32[1,24]{1,0:T(1,128)S(1)}, u32[]{:S(2)}, u32[]{:S(2)}) collective-permute-start(s32[1,24]{1,0:T(1,128)} %param.10), channel_id=1, source_target_pairs={{3,0},{0,1},{1,2},{2,3},{7,4},{4,5},{5,6},{6,7},{11,8},{8,9},{9,10... | collective-permute-start | bytes 296 | tf_op jit(solution)/shard_map/ppermute | solution.py:533
  21.4 2.5 %collective-permute-start.1 = (s32[1,24]{1,0:T(1,128)}, s32[1,24]{1,0:T(1,128)S(1)}, u32[]{:S(2)}, u32[]{:S(2)}) collective-permute-start(s32[1,24]{1,0:T(1,128)} %param.10), channel_id=1, source_target_pairs={{2,0},{3,1},{0,2},{1,3},{6,4},{7,5},{4,6},{5,7},{10,8},{11,9},{8,1... | collective-permute-start | bytes 296 | tf_op jit(solution)/shard_map/ppermute | solution.py:533
  22.6 3.4 %collective-permute-start = (s32[1,24]{1,0:T(1,128)}, s32[1,24]{1,0:T(1,128)S(1)}, u32[]{:S(2)}, u32[]{:S(2)}) collective-permute-start(s32[1,24]{1,0:T(1,128)} %param.10), channel_id=1, source_target_pairs={{1,0},{2,1},{3,2},{0,3},{5,4},{6,5},{7,6},{4,7},{9,8},{10,9},{11,1... | collective-permute-start | bytes 296 | tf_op jit(solution)/shard_map/ppermute | solution.py:533
  31.8 0.9 copy-start.4
  60.6 5.7 %copy-start = (bf16[512,128,128]{2,1,0:T(8,128)(2,1)}, bf16[512,128,128]{2,1,0:T(8,128)(2,1)S(1)}, u32[]{:S(2)}) copy-start(bf16[512,128,128]{2,1,0:T(8,128)(2,1)S(1)} %get-tuple-element.36.index_ref) | copy-start | bytes 50331652
  66.3 5.8 %copy-start.2 = (bf16[512,128,128]{2,1,0:T(8,128)(2,1)}, bf16[512,128,128]{2,1,0:T(8,128)(2,1)S(1)}, u32[]{:S(2)}) copy-start(bf16[512,128,128]{2,1,0:T(8,128)(2,1)S(1)} %get-tuple-element.37.turned_ref) | copy-start | bytes 50331652
  72.1 5.8 %copy-start.1 = (bf16[512,128,128]{2,1,0:T(8,128)(2,1)S(1)}, bf16[512,128,128]{2,1,0:T(8,128)(2,1)}, u32[]{:S(2)}) copy-start(bf16[512,128,128]{2,1,0:T(8,128)(2,1)} %copy-done) | copy-start | bytes 50331652
  77.9 5.8 %copy-start.3 = (bf16[512,128,128]{2,1,0:T(8,128)(2,1)S(1)}, bf16[512,128,128]{2,1,0:T(8,128)(2,1)}, u32[]{:S(2)}) copy-start(bf16[512,128,128]{2,1,0:T(8,128)(2,1)} %copy-done.2) | copy-start | bytes 50331652
  95.7 49.5 %collective-permute-start.3 = (bf16[1072,128]{1,0:T(8,128)(2,1)S(1)}, bf16[1072,128]{1,0:T(8,128)(2,1)S(1)}, u32[]{:S(2)}, u32[]{:S(2)}) collective-permute-start(bf16[1072,128]{1,0:T(8,128)(2,1)S(1)} %get-tuple-element.38), channel_id=1, source_target_pairs={{0,4},{4,8},{8,12},{12,16},{16,20},{20,24},{24,28},{28,0},{1,5},{5... | collective-permute-start | bytes 823304 | tf_op jit(solution)/shard_map/ppermute | solution.py:562
  95.7 50.7 %collective-permute-start.4 = (bf16[1072,128]{1,0:T(8,128)(2,1)S(1)}, bf16[1072,128]{1,0:T(8,128)(2,1)S(1)}, u32[]{:S(2)}, u32[]{:S(2)}) collective-permute-start(bf16[1072,128]{1,0:T(8,128)(2,1)S(1)} %get-tuple-element.39), channel_id=1, source_target_pairs={{0,8},{4,12},{8,16},{12,20},{16,24},{20,28},{24,0},{28,4},{1,9},{5... | collective-permute-start | bytes 823304 | tf_op jit(solution)/shard_map/ppermute | solution.py:562
  115.2 36.4 %collective-permute-start.5 = (bf16[1072,128]{1,0:T(8,128)(2,1)S(1)}, bf16[1072,128]{1,0:T(8,128)(2,1)S(1)}, u32[]{:S(2)}, u32[]{:S(2)}) collective-permute-start(bf16[1072,128]{1,0:T(8,128)(2,1)S(1)} %get-tuple-element.40), channel_id=1, source_target_pairs={{0,12},{4,16},{8,20},{12,24},{16,28},{20,0},{24,4},{28,8},{1,13},{... | collective-permute-start | bytes 823304 | tf_op jit(solution)/shard_map/ppermute | solution.py:562
  115.5 36.1 %collective-permute-start.6 = (bf16[1072,128]{1,0:T(8,128)(2,1)S(1)}, bf16[1072,128]{1,0:T(8,128)(2,1)S(1)}, u32[]{:S(2)}, u32[]{:S(2)}) collective-permute-start(bf16[1072,128]{1,0:T(8,128)(2,1)S(1)} %get-tuple-element.41), channel_id=1, source_target_pairs={{0,16},{4,20},{8,24},{12,28},{16,0},{20,4},{24,8},{28,12},{1,17},{... | collective-permute-start | bytes 823304 | tf_op jit(solution)/shard_map/ppermute | solution.py:562
  133.0 32.6 %copy-start.5 = (bf16[16,32,128]{2,1,0:T(8,128)(2,1)S(1)}, bf16[16,32,128]{2,1,0:T(8,128)(2,1)}, u32[]{:S(2)}) copy-start(bf16[16,32,128]{2,1,0:T(8,128)(2,1)} %queries_ref.1) | copy-start | bytes 393220
  133.0 32.6 %copy-start.6 = (f32[16,64]{1,0:T(8,128)S(1)}, f32[16,64]{1,0:T(8,128)}, u32[]{:S(2)}) copy-start(f32[16,64]{1,0:T(8,128)} %teacher_ref.1) | copy-start | bytes 12292
  133.1 18.5 %collective-permute-start.7 = (bf16[1072,128]{1,0:T(8,128)(2,1)S(1)}, bf16[1072,128]{1,0:T(8,128)(2,1)S(1)}, u32[]{:S(2)}, u32[]{:S(2)}) collective-permute-start(bf16[1072,128]{1,0:T(8,128)(2,1)S(1)} %get-tuple-element.42), channel_id=1, source_target_pairs={{0,20},{4,24},{8,28},{12,0},{16,4},{20,8},{24,12},{28,16},{1,21},{... | collective-permute-start | bytes 823304 | tf_op jit(solution)/shard_map/ppermute | solution.py:562
  145.2 10.4 %collective-permute-start.8 = (bf16[1072,128]{1,0:T(8,128)(2,1)S(1)}, bf16[1072,128]{1,0:T(8,128)(2,1)S(1)}, u32[]{:S(2)}, u32[]{:S(2)}) collective-permute-start(bf16[1072,128]{1,0:T(8,128)(2,1)S(1)} %get-tuple-element.43), channel_id=1, source_target_pairs={{0,24},{4,28},{8,0},{12,4},{16,8},{20,12},{24,16},{28,20},{1,25},{... | collective-permute-start | bytes 823304 | tf_op jit(solution)/shard_map/ppermute | solution.py:562
  146.5 19.1 %collective-permute-start.9 = (bf16[1072,128]{1,0:T(8,128)(2,1)S(1)}, bf16[1072,128]{1,0:T(8,128)(2,1)S(1)}, u32[]{:S(2)}, u32[]{:S(2)}) collective-permute-start(bf16[1072,128]{1,0:T(8,128)(2,1)S(1)} %get-tuple-element.44), channel_id=1, source_target_pairs={{0,28},{4,0},{8,4},{12,8},{16,12},{20,16},{24,20},{28,24},{1,29},{... | collective-permute-start | bytes 823304 | tf_op jit(solution)/shard_map/ppermute | solution.py:562

commit v6 on v5

--- a/solution.py
+++ b/solution.py
@@ -12,13 +12,13 @@
 epsilon = 1e-06
 LOG2E = 1.4426950408889634
 GROUP = 4
-UNITS = 24
+UNITS = 12
 LOADS = 8
 LOAD_STEP = 16
 NEG_STEP = 8
 NEG_CHUNK = 24
 SOURCES = 2
-VMEM_LIMIT = 14 * 1024 * 1024
+VMEM_LIMIT = 8 * 1024 * 1024
 LAST = (((1,), (1,)), ((), ()))
 
 
@@ -465,7 +465,7 @@
             pltpu.VMEM((chunk, dim, wide), jnp.bfloat16),
             pltpu.SemaphoreType.DMA((2,)),
         ],
-        compiler_params=pltpu.CompilerParams(vmem_limit_bytes=2 * VMEM_LIMIT),
+        compiler_params=pltpu.CompilerParams(vmem_limit_bytes=3 * VMEM_LIMIT),
         cost_estimate=pl.CostEstimate(
             flops=4 * total * height * wide * dim,
             bytes_accessed=2 * total * wide * dim,

time: 167 us -> 149 us (0.89)
  the two profiles are of different devices: /device:TPU:15 before, /device:TPU:4 now
where the time goes in v6:
time: 149 us; the launch traced here: 151 us
  Pallas kernels  101 us (68%)
  waiting for transfers between devices  21.2 us (14%)
  blocking collectives  11.4 us (8%)
  starting transfers between devices  10.1 us (7%)
  local copies, waits for them, and re-layouts  3.7 us (2%)
  other arithmetic  2.45 us (2%)
    pallas_call x4, Pallas kernels, pairs(): pl.pallas_call(functools.partial(pair_kernel, cands=cands, sources=len(so...  66.2 us
    ppermute x7, waiting for transfers between devices, on_device(): lax.ppermute(message, 'corpus', [(i, (i + step) % owners) for i in range(...  20.1 us
    pallas_call x1, Pallas kernels, negatives(): pl.pallas_call(functools.partial(neg_kernel, tokens=tokens), in_specs=[pl...  19.2 us
    all_to_all x1, blocking collectives, told(): lax.all_to_all(copies, 'corpus', split_axis=0, concat_axis=0, tiled=True)  11.4 us
    pallas_call x1, Pallas kernels, load(): pl.pallas_call(load_shard, in_specs=[pl.BlockSpec(memory_space=pltpu.HBM)...  8.67 us
    all_to_all x1, starting transfers between devices, told(): lax.all_to_all(copies, 'corpus', split_axis=0, concat_axis=0, tiled=True)  5.1 us
    pallas_call x1, Pallas kernels, prep(): pl.pallas_call(functools.partial(prep_kernel, shard=shard, cands=cands),...  4.98 us
  transfers between devices with their start and end apart: 11, of which 4 were waited for; matrix products, arithmetic and copies ran while one was open for 1% of the time, Pallas kernels for 49%

profile of v6, /device:TPU:4, one launch (start us, length us, event | category | flops | bytes accessed | tf_op | source)
XLA Modules:
  0.0 150.8 jit_solution(9778679813963603570)
XLA Ops:
  0.6 0.7 fusion
  1.4 0.8 pad_maximum_fusion
  2.1 11.4 %all_to_all.10 = f32[8,16,128]{2,1,0:T(8,128)S(1)} all-to-all(f32[8,16,128]{2,1,0:T(8,128)S(1)} %broadcast_in_dim.5), channel_id=1, replica_groups=mesh['corpus'=8,'blk'=4] {'corpus'}, dimensions={0} | all-to-all | bytes 131072 | tf_op jit(solution)/shard_map/all_to_all | solution.py:543
  13.5 2.1 %broadcast_in_dim.4 = bf16[8,16,32,128]{3,2,1,0:T(8,128)(2,1)} broadcast(bf16[16,32,128]{2,1,0:T(8,128)(2,1)} %queries_ref.1), dimensions={1,2,3} | broadcast | bytes 1179648 | tf_op jit(solution)/shard_map/broadcast_in_dim | solution.py:542
  15.6 5.1 %all-to-all-start = ((bf16[8,16,32,128]{3,2,1,0:T(8,128)(2,1)}), bf16[8,16,32,128]{3,2,1,0:T(8,128)(2,1)S(1)}, u32[]{:S(2)}, u32[]{:S(2)}) async-start(bf16[8,16,32,128]{3,2,1,0:T(8,128)(2,1)} %broadcast_in_dim.4), calls=%async_computation | async-start | bytes 2097152 | tf_op jit(solution)/shard_map/all_to_all | solution.py:543
  20.7 1.5 %collective-permute-start.1 = (s32[1,24]{1,0:T(1,128)}, s32[1,24]{1,0:T(1,128)S(1)}, u32[]{:S(2)}, u32[]{:S(2)}) collective-permute-start(s32[1,24]{1,0:T(1,128)} %param.10), channel_id=1, source_target_pairs={{2,0},{3,1},{0,2},{1,3},{6,4},{7,5},{4,6},{5,7},{10,8},{11,9},{8,1... | collective-permute-start | bytes 296 | tf_op jit(solution)/shard_map/ppermute | solution.py:533
  22.2 1.4 collective-permute-start
  23.7 0.1 pad_add_fusion.1.source_ref
  23.7 0.1 pad_add_fusion.2.source_ref
  23.8 0.1 pad_add_fusion.3.source_ref
  23.9 0.1 pad_add_fusion.4.source_ref
  24.0 0.4 collective-permute-done.1
  24.4 0.7 collective-permute-done
  25.1 0.7 pad_add_fusion
  25.8 0.1 reshape.22.rows_ref
  25.8 5.0 %prep.1 = (s32[128,128]{1,0:T(8,128)S(1)}, f32[2048,128]{1,0:T(8,128)S(1)}) custom-call(s32[1]{0:T(128)} %bitcast.me_ref, f32[128,128]{1,0:T(8,128)S(1)} %bitcast.17), custom_call_target="tpu_custom_call" | custom-call | flops 16384 | bytes 16384 | tf_op jit(solution)/shard_map/prep/pallas_call | solution.py:155
  30.8 0.9 copy-done
  31.7 19.2 %negatives.1 = (f32[512,128]{1,0:T(8,128)S(1)}, f32[8,512]{1,0:T(8,128)S(1)}) custom-call(s32[96]{0:T(128)S(1)} %reshape.22.rows_ref, bf16[512,128]{1,0:T(8,128)(2,1)S(1)} %bitcast.16, bf16[512,128,128]{2,1,0:T(8,128)(2,1)} %index_ref), custom_call_target="tpu_custom_call" | custom-call | flops 3221225472 | bytes 3145728 | tf_op jit(solution)/shard_map/negatives/pallas_call | solution.py:445
  51.0 8.7 %load.1 = (bf16[512,128,128]{2,1,0:T(8,128)(2,1)S(1)}, bf16[512,128,128]{2,1,0:T(8,128)(2,1)S(1)}, f32[512,128]{1,0:T(8,128)S(1)}) custom-call(bf16[512,128,128]{2,1,0:T(8,128)(2,1)} %index_ref), custom_call_target="tpu_custom_call" | custom-call | flops 16777216 | bytes 16777216 | tf_op jit(solution)/shard_map/load/pallas_call | solution.py:81
  59.7 17.1 %pairs.4 = (bf16[1072,128]{1,0:T(8,128)(2,1)S(1)}, bf16[1072,128]{1,0:T(8,128)(2,1)S(1)}) custom-call(s32[2]{0:T(128)S(1)} %pad_add_fusion.1.source_ref, s32[128,128]{1,0:T(8,128)S(1)} %get-tuple-element.31.rows_ref, f32[2048,128]{1,0:T(8,128)S(1)} %get-tuple-element.32.target_ref, bf16[8,16,32,128]{3,2,1,0:T(8,128)(2,1)S(1)} %all-to-all-done.queries_ref, ...), custom_call_target="tpu_custom_call" | custom-call | flops 1610612736 | bytes 16777216 | tf_op jit(solution)/shard_map/pairs/pallas_call | solution.py:321
  76.8 1.5 collective-permute-start.3
  78.3 17.1 %pairs.5 = (bf16[1072,128]{1,0:T(8,128)(2,1)S(1)}, bf16[1072,128]{1,0:T(8,128)(2,1)S(1)}) custom-call(s32[2]{0:T(128)S(1)} %pad_add_fusion.2.source_ref, s32[128,128]{1,0:T(8,128)S(1)} %get-tuple-element.31.rows_ref, f32[2048,128]{1,0:T(8,128)S(1)} %get-tuple-element.32.target_ref, bf16[8,16,32,128]{3,2,1,0:T(8,128)(2,1)S(1)} %all-to-all-done.queries_ref, ...), custom_call_target="tpu_custom_call" | custom-call | flops 1610612736 | bytes 16777216 | tf_op jit(solution)/shard_map/pairs/pallas_call | solution.py:321
  95.5 0.1 collective-permute-start.5
  95.6 0.1 collective-permute-start.6
  95.6 14.8 %pairs.6 = (bf16[1072,128]{1,0:T(8,128)(2,1)S(1)}, bf16[1072,128]{1,0:T(8,128)(2,1)S(1)}) custom-call(s32[2]{0:T(128)S(1)} %pad_add_fusion.3.source_ref, s32[128,128]{1,0:T(8,128)S(1)} %get-tuple-element.31.rows_ref, f32[2048,128]{1,0:T(8,128)S(1)} %get-tuple-element.32.target_ref, bf16[8,16,32,128]{3,2,1,0:T(8,128)(2,1)S(1)} %all-to-all-done.queries_ref, ...), custom_call_target="tpu_custom_call" | custom-call | flops 1610612736 | bytes 16777216 | tf_op jit(solution)/shard_map/pairs/pallas_call | solution.py:321
  110.5 0.3 collective-permute-start.7
  110.8 17.1 %pairs.7 = (bf16[1072,128]{1,0:T(8,128)(2,1)S(1)}, bf16[1072,128]{1,0:T(8,128)(2,1)S(1)}) custom-call(s32[2]{0:T(128)S(1)} %pad_add_fusion.4.source_ref, s32[128,128]{1,0:T(8,128)S(1)} %get-tuple-element.31.rows_ref, f32[2048,128]{1,0:T(8,128)S(1)} %get-tuple-element.32.target_ref, bf16[8,16,32,128]{3,2,1,0:T(8,128)(2,1)S(1)} %all-to-all-done.queries_ref, ...), custom_call_target="tpu_custom_call" | custom-call | flops 1610612736 | bytes 16777216 | tf_op jit(solution)/shard_map/pairs/pallas_call | solution.py:321
  127.9 0.1 collective-permute-start.8
  128.1 8.5 %collective-permute-done.8.refs_5_ = bf16[1072,128]{1,0:T(8,128)(2,1)S(1)} collective-permute-done((bf16[1072,128]{1,0:T(8,128)(2,1)S(1)}, bf16[1072,128]{1,0:T(8,128)(2,1)S(1)}, u32[]{:S(2)}, u32[]{:S(2)}) %collective-permute-start.8) | collective-permute-done | bytes 274464 | tf_op jit(solution)/shard_map/ppermute | solution.py:562
  136.6 11.5 %collective-permute-done.9.refs_6_ = bf16[1072,128]{1,0:T(8,128)(2,1)S(1)} collective-permute-done((bf16[1072,128]{1,0:T(8,128)(2,1)S(1)}, bf16[1072,128]{1,0:T(8,128)(2,1)S(1)}, u32[]{:S(2)}, u32[]{:S(2)}) %collective-permute-start.9) | collective-permute-done | bytes 274464 | tf_op jit(solution)/shard_map/ppermute | solution.py:562
  148.1 2.0 %finish.1 = (f32[16,128]{1,0:T(8,128)S(1)}, f32[16,32,128]{2,1,0:T(8,128)}) custom-call(bf16[16,32,128]{2,1,0:T(8,128)(2,1)S(1)} %copy-done.1, f32[16,64]{1,0:T(8,128)S(1)} %copy-done.2, f32[512,128]{1,0:T(8,128)S(1)} %get-tuple-element.29.back_ref, f32[8,512]{1,0:T(8,128)S(1)} %get-tuple-element.30.sums_ref, ...), custom_call_target="tpu_custom_call" | custom-call | tf_op jit(solution)/shard_map/finish/pallas_call | solution.py:510
  150.2 0.6 slice_reduce_fusion
  (16 shorter events, 0.1 us)
Async XLA Ops:
  15.6 35.4 %all-to-all-start = ((bf16[8,16,32,128]{3,2,1,0:T(8,128)(2,1)}), bf16[8,16,32,128]{3,2,1,0:T(8,128)(2,1)S(1)}, u32[]{:S(2)}, u32[]{:S(2)}) async-start(bf16[8,16,32,128]{3,2,1,0:T(8,128)(2,1)} %broadcast_in_dim.4), calls=%async_computation | async-start | bytes 2097152 | tf_op jit(solution)/shard_map/all_to_all | solution.py:543
  20.7 3.3 %collective-permute-start.2 = (s32[1,24]{1,0:T(1,128)}, s32[1,24]{1,0:T(1,128)S(1)}, u32[]{:S(2)}, u32[]{:S(2)}) collective-permute-start(s32[1,24]{1,0:T(1,128)} %param.10), channel_id=1, source_target_pairs={{3,0},{0,1},{1,2},{2,3},{7,4},{4,5},{5,6},{6,7},{11,8},{8,9},{9,10... | collective-permute-start | bytes 296 | tf_op jit(solution)/shard_map/ppermute | solution.py:533
  20.7 3.7 %collective-permute-start.1 = (s32[1,24]{1,0:T(1,128)}, s32[1,24]{1,0:T(1,128)S(1)}, u32[]{:S(2)}, u32[]{:S(2)}) collective-permute-start(s32[1,24]{1,0:T(1,128)} %param.10), channel_id=1, source_target_pairs={{2,0},{3,1},{0,2},{1,3},{6,4},{7,5},{4,6},{5,7},{10,8},{11,9},{8,1... | collective-permute-start | bytes 296 | tf_op jit(solution)/shard_map/ppermute | solution.py:533
  22.2 2.9 %collective-permute-start = (s32[1,24]{1,0:T(1,128)}, s32[1,24]{1,0:T(1,128)S(1)}, u32[]{:S(2)}, u32[]{:S(2)}) collective-permute-start(s32[1,24]{1,0:T(1,128)} %param.10), channel_id=1, source_target_pairs={{1,0},{2,1},{3,2},{0,3},{5,4},{6,5},{7,6},{4,7},{9,8},{10,9},{11,1... | collective-permute-start | bytes 296 | tf_op jit(solution)/shard_map/ppermute | solution.py:533
  30.8 0.9 copy-start
  76.8 51.1 %collective-permute-start.3 = (bf16[1072,128]{1,0:T(8,128)(2,1)S(1)}, bf16[1072,128]{1,0:T(8,128)(2,1)S(1)}, u32[]{:S(2)}, u32[]{:S(2)}) collective-permute-start(bf16[1072,128]{1,0:T(8,128)(2,1)S(1)} %get-tuple-element.38), channel_id=1, source_target_pairs={{0,4},{4,8},{8,12},{12,16},{16,20},{20,24},{24,28},{28,0},{1,5},{5... | collective-permute-start | bytes 823304 | tf_op jit(solution)/shard_map/ppermute | solution.py:562
  78.3 49.6 %collective-permute-start.4 = (bf16[1072,128]{1,0:T(8,128)(2,1)S(1)}, bf16[1072,128]{1,0:T(8,128)(2,1)S(1)}, u32[]{:S(2)}, u32[]{:S(2)}) collective-permute-start(bf16[1072,128]{1,0:T(8,128)(2,1)S(1)} %get-tuple-element.39), channel_id=1, source_target_pairs={{0,8},{4,12},{8,16},{12,20},{16,24},{20,28},{24,0},{28,4},{1,9},{5... | collective-permute-start | bytes 823304 | tf_op jit(solution)/shard_map/ppermute | solution.py:562
  95.5 32.6 %collective-permute-start.5 = (bf16[1072,128]{1,0:T(8,128)(2,1)S(1)}, bf16[1072,128]{1,0:T(8,128)(2,1)S(1)}, u32[]{:S(2)}, u32[]{:S(2)}) collective-permute-start(bf16[1072,128]{1,0:T(8,128)(2,1)S(1)} %get-tuple-element.40), channel_id=1, source_target_pairs={{0,12},{4,16},{8,20},{12,24},{16,28},{20,0},{24,4},{28,8},{1,13},{... | collective-permute-start | bytes 823304 | tf_op jit(solution)/shard_map/ppermute | solution.py:562
  95.6 32.5 %collective-permute-start.6 = (bf16[1072,128]{1,0:T(8,128)(2,1)S(1)}, bf16[1072,128]{1,0:T(8,128)(2,1)S(1)}, u32[]{:S(2)}, u32[]{:S(2)}) collective-permute-start(bf16[1072,128]{1,0:T(8,128)(2,1)S(1)} %get-tuple-element.41), channel_id=1, source_target_pairs={{0,16},{4,20},{8,24},{12,28},{16,0},{20,4},{24,8},{28,12},{1,17},{... | collective-permute-start | bytes 823304 | tf_op jit(solution)/shard_map/ppermute | solution.py:562
  110.5 37.7 %copy-start.1 = (bf16[16,32,128]{2,1,0:T(8,128)(2,1)S(1)}, bf16[16,32,128]{2,1,0:T(8,128)(2,1)}, u32[]{:S(2)}) copy-start(bf16[16,32,128]{2,1,0:T(8,128)(2,1)} %queries_ref.1) | copy-start | bytes 393220
  110.5 37.6 %copy-start.2 = (f32[16,64]{1,0:T(8,128)S(1)}, f32[16,64]{1,0:T(8,128)}, u32[]{:S(2)}) copy-start(f32[16,64]{1,0:T(8,128)} %teacher_ref.1) | copy-start | bytes 12292
  110.5 17.6 %collective-permute-start.7 = (bf16[1072,128]{1,0:T(8,128)(2,1)S(1)}, bf16[1072,128]{1,0:T(8,128)(2,1)S(1)}, u32[]{:S(2)}, u32[]{:S(2)}) collective-permute-start(bf16[1072,128]{1,0:T(8,128)(2,1)S(1)} %get-tuple-element.42), channel_id=1, source_target_pairs={{0,20},{4,24},{8,28},{12,0},{16,4},{20,8},{24,12},{28,16},{1,21},{... | collective-permute-start | bytes 823304 | tf_op jit(solution)/shard_map/ppermute | solution.py:562
  127.9 8.7 %collective-permute-start.8 = (bf16[1072,128]{1,0:T(8,128)(2,1)S(1)}, bf16[1072,128]{1,0:T(8,128)(2,1)S(1)}, u32[]{:S(2)}, u32[]{:S(2)}) collective-permute-start(bf16[1072,128]{1,0:T(8,128)(2,1)S(1)} %get-tuple-element.43), channel_id=1, source_target_pairs={{0,24},{4,28},{8,0},{12,4},{16,8},{20,12},{24,16},{28,20},{1,25},{... | collective-permute-start | bytes 823304 | tf_op jit(solution)/shard_map/ppermute | solution.py:562
  128.0 20.1 %collective-permute-start.9 = (bf16[1072,128]{1,0:T(8,128)(2,1)S(1)}, bf16[1072,128]{1,0:T(8,128)(2,1)S(1)}, u32[]{:S(2)}, u32[]{:S(2)}) collective-permute-start(bf16[1072,128]{1,0:T(8,128)(2,1)S(1)} %get-tuple-element.44), channel_id=1, source_target_pairs={{0,28},{4,0},{8,4},{12,8},{16,12},{20,16},{24,20},{28,24},{1,29},{... | collective-permute-start | bytes 823304 | tf_op jit(solution)/shard_map/ppermute | solution.py:562

commit v7 on v6

--- a/solution.py
+++ b/solution.py
@@ -18,6 +18,7 @@
 NEG_STEP = 8
 NEG_CHUNK = 24
 SOURCES = 2
+CODE = 64
 VMEM_LIMIT = 8 * 1024 * 1024
 LAST = (((1,), (1,)), ((), ()))
 
@@ -98,12 +99,21 @@
     )(pltpu.with_memory_space_constraint(index, pltpu.HBM))
 
 
-def prep_kernel(me_ref, meta_ref, rows_ref, target_ref, value_ref, place_ref, result_ref, *, shard, cands):
-    count = meta_ref.shape[0]
-    code = meta_ref[:, :cands]
+def prep_kernel(me_ref, told_ref, rows_ref, target_ref, value_ref, place_ref, result_ref, *, shard, cands):
+    sources, height = told_ref.shape[:2]
+    each = rows_ref.shape[0] // sources
+    count = rows_ref.shape[0]
+    base = height - 3 * each
+
+    def part(k):
+        rows = [told_ref[s, base + k * each : base + (k + 1) * each, :] for s in range(sources)]
+        return jnp.concatenate(rows, axis=0).astype(jnp.float32)
+
+    codes, upper, lower = part(0), part(1), part(2)
+    code = CODE * codes[:, :cands] + codes[:, cands:]
     owner = jnp.floor((code + 0.5) * (1.0 / shard))
     row = code - owner * shard
-    teacher = meta_ref[:, cands:]
+    teacher = upper[:, :cands] + upper[:, cands:] + lower[:, :cands]
     log_target = teacher - jnp.log(jnp.sum(jnp.exp(teacher), axis=-1, keepdims=True))
     target = jnp.exp(log_target)
     mine = (owner == me_ref[0].astype(jnp.float32)).astype(jnp.float32)
@@ -149,8 +159,7 @@
         )
 
 
-def prep(me, meta, shard, cands):
-    count = meta.shape[0]
+def prep(me, told, count, shard, cands):
     wide = 128
     return pl.pallas_call(
         functools.partial(prep_kernel, shard=shard, cands=cands),
@@ -171,7 +180,7 @@
         compiler_params=pltpu.CompilerParams(vmem_limit_bytes=VMEM_LIMIT),
         cost_estimate=pl.CostEstimate(flops=count * wide, bytes_accessed=count * wide, transcendentals=0),
         name="prep",
-    )(me, meta)
+    )(me, told)
 
 
 def pair_kernel(source_ref, rows_ref, target_ref, queries_ref, inverse_ref, index_ref, turned_ref, *refs, cands, sources):
@@ -197,7 +206,7 @@
         return slot, q, jnp.bitwise_and(slot, per_query - 1) * GROUP
 
     for q in range(count):
-        unit_ref[q] = rounded_queries(queries_ref[0, q])
+        unit_ref[q] = rounded_queries(queries_ref[0, q * tokens : (q + 1) * tokens, :])
     acc_ref[...] = jnp.zeros_like(acc_ref)
     ones = jnp.ones((8, wide), jnp.bfloat16)
 
@@ -311,8 +320,8 @@
                 out_ref[pl.ds(count * 2 * tokens + j * count, count), :] = part
 
 
-def pairs(sources, rows, targets, queries, inverse, index, turned, cands, room):
-    count, tokens, dim = queries.shape[1:]
+def pairs(sources, rows, targets, told, count, tokens, inverse, index, turned, cands, room):
+    dim = told.shape[2]
     wide = rows.shape[1]
     per_query = cands // GROUP
     slots = count * per_query
@@ -326,7 +335,7 @@
             in_specs=[
                 pl.BlockSpec((count, wide), lambda i, s: (s[i], 0), memory_space=pltpu.SMEM),
                 pl.BlockSpec((slots, wide), lambda i, s: (s[i], 0)),
-                pl.BlockSpec((1, count, tokens, dim), lambda i, s: (s[i], 0, 0, 0)),
+                pl.BlockSpec((1,) + told.shape[1:], lambda i, s: (s[i], 0, 0)),
                 pl.BlockSpec(memory_space=pltpu.VMEM),
                 pl.BlockSpec(memory_space=pltpu.VMEM),
                 pl.BlockSpec(memory_space=pltpu.VMEM),
@@ -351,7 +360,7 @@
             transcendentals=len(sources) * room * tokens * wide,
         ),
         name="pairs",
-    )(jnp.stack(sources), rows, targets, queries, inverse, index, turned)
+    )(jnp.stack(sources), rows, targets, told, inverse, index, turned)
 
 
 def neg_kernel(rows_ref, queries_ref, shard_ref, acc_ref, sums_ref,
@@ -535,19 +544,21 @@
     def gathered(value, axis, size):
         return [value] + [from_step(value, axis, size, step) for step in range(1, size)]
 
-    code = (cand_owner[..., 0] * shard + cand_row).astype(jnp.float32)
-    meta = jnp.concatenate([code, teacher], axis=1)
+    code = cand_owner[..., 0] * shard + cand_row
+    high = lax.reduce_precision(teacher, 8, 7)
+    mid = lax.reduce_precision(teacher - high, 8, 7)
+    low = lax.reduce_precision(teacher - high - mid, 8, 7)
+    meta = [code // CODE, code % CODE, high, mid, low, jnp.zeros_like(low)]
+    meta = [value.astype(jnp.bfloat16) for value in meta]
+    meta = [jnp.concatenate(meta[k : k + 2], axis=1) for k in range(0, 6, 2)]
+    message = jnp.concatenate([queries.reshape(count * tokens, dim)] + meta, axis=0)
     all_neg = jnp.concatenate(gathered(neg_row, "blk", group), axis=0).reshape(-1)
-    def told(value):
-        copies = jnp.broadcast_to(value[None], (owners,) + value.shape)
-        return lax.all_to_all(copies, "corpus", split_axis=0, concat_axis=0, tiled=True)
-
-    all_meta = told(meta).reshape(owners * count, -1)
-    all_queries = told(queries)
-    rows, targets = prep(me.reshape(1), all_meta, shard, cands)
-    rows, all_neg = lax.optimization_barrier((rows, all_neg))
+    told = jnp.broadcast_to(message[None], (owners,) + message.shape)
+    told = lax.all_to_all(told, "corpus", split_axis=0, concat_axis=0, tiled=True)
     neg_acc, neg_sum = negatives(all_neg, queries, index)
-    index, all_queries, rows, neg_acc = lax.optimization_barrier((index, all_queries, rows, neg_acc))
+    told, neg_acc = lax.optimization_barrier((told, neg_acc))
+    rows, targets = prep(me.reshape(1), told, owners * count, shard, cands)
+    index, told, rows = lax.optimization_barrier((index, told, rows))
     index, turned, inverse = load(index)
     messages = []
     order = list(range(1, owners)) + [0]
@@ -555,7 +566,7 @@
     for steps in groups:
         sources = [lax.rem(me + step, owners) for step in steps]
         found = pairs(
-            sources, rows, targets, all_queries, inverse, index, turned, cands, room
+            sources, rows, targets, told, count, tokens, inverse, index, turned, cands, room
         )
         for step, message in zip(steps, found):
             if step:

time: 149 us -> 138 us (0.926)
  the two profiles are of different devices: /device:TPU:4 before, /device:TPU:20 now
where the time goes in v7:
time: 138 us
  Pallas kernels  70.1 us (51%)
  starting transfers between devices  45.6 us (33%)
  waiting for transfers between devices  15.6 us (11%)
  other arithmetic  3.39 us (2%)
  local copies, waits for them, and re-layouts  2.81 us (2%)
    ppermute x7, starting transfers between devices, on_device(): lax.ppermute(message, 'corpus', [(i, (i + step) % owners) for i in range(...  36.5 us
    pallas_call x4, Pallas kernels, pairs(): pl.pallas_call(functools.partial(pair_kernel, cands=cands, sources=len(so...  35.2 us
    pallas_call x1, Pallas kernels, negatives(): pl.pallas_call(functools.partial(neg_kernel, tokens=tokens), in_specs=[pl...  19.3 us
    ppermute x7, waiting for transfers between devices, on_device(): lax.ppermute(message, 'corpus', [(i, (i + step) % owners) for i in range(...  14.5 us
    pallas_call x1, Pallas kernels, load(): pl.pallas_call(load_shard, in_specs=[pl.BlockSpec(memory_space=pltpu.HBM)...  8.67 us
    all_to_all x1, starting transfers between devices, on_device(): lax.all_to_all(told, 'corpus', split_axis=0, concat_axis=0, tiled=True)  6.11 us
    pallas_call x1, Pallas kernels, prep(): pl.pallas_call(functools.partial(prep_kernel, shard=shard, cands=cands),...  4.96 us
    ppermute x3, starting transfers between devices, from_step(): lax.ppermute(value, axis, [((i + step) % size, i) for i in range(size)])  2.96 us
  transfers between devices with their start and end apart: 11, of which 4 were waited for; matrix products, arithmetic and copies ran while one was open for 1% of the time, Pallas kernels for 34%

profile of v7, /device:TPU:20, one launch (start us, length us, event | category | flops | bytes accessed | tf_op | source)
XLA Modules:
  0.0 138.2 jit_solution(16231745838388359132)
XLA Ops:
  0.6 0.7 reduce-precision_convert_fusion.1
  1.3 0.7 fusion.4
  2.1 1.0 fusion.1
  3.1 1.2 broadcast_in_dim.2
  4.2 6.1 %all-to-all-start = ((bf16[8,560,128]{2,1,0:T(8,128)(2,1)}), bf16[8,560,128]{2,1,0:T(8,128)(2,1)S(1)}, u32[]{:S(2)}, u32[]{:S(2)}) async-start(bf16[8,560,128]{2,1,0:T(8,128)(2,1)} %broadcast_in_dim.2), calls=%async_computation | async-start | bytes 2293760 | tf_op jit(solution)/shard_map/all_to_all | solution.py:557
  10.4 1.5 %collective-permute-start.1 = (s32[1,24]{1,0:T(1,128)}, s32[1,24]{1,0:T(1,128)S(1)}, u32[]{:S(2)}, u32[]{:S(2)}) collective-permute-start(s32[1,24]{1,0:T(1,128)} %param.10), channel_id=1, source_target_pairs={{2,0},{3,1},{0,2},{1,3},{6,4},{7,5},{4,6},{5,7},{10,8},{11,9},{8,1... | collective-permute-start | bytes 296 | tf_op jit(solution)/shard_map/ppermute | solution.py:542
  11.9 1.4 %collective-permute-start = (s32[1,24]{1,0:T(1,128)}, s32[1,24]{1,0:T(1,128)S(1)}, u32[]{:S(2)}, u32[]{:S(2)}) collective-permute-start(s32[1,24]{1,0:T(1,128)} %param.10), channel_id=1, source_target_pairs={{1,0},{2,1},{3,2},{0,3},{5,4},{6,5},{7,6},{4,7},{9,8},{10,9},{11,1... | collective-permute-start | bytes 296 | tf_op jit(solution)/shard_map/ppermute | solution.py:542
  13.3 0.1 pad_add_fusion.1.source_ref
  13.5 0.1 pad_add_fusion.3.source_ref
  13.6 0.4 collective-permute-done.1
  14.1 0.7 collective-permute-done
  14.7 0.7 pad_add_fusion
  15.4 0.1 reshape.18.rows_ref
  15.5 0.9 copy-done
  16.4 19.3 %negatives.1 = (f32[512,128]{1,0:T(8,128)S(1)}, f32[8,512]{1,0:T(8,128)S(1)}) custom-call(s32[96]{0:T(128)S(1)} %reshape.18.rows_ref, bf16[512,128]{1,0:T(8,128)(2,1)S(1)} %bitcast.18, bf16[512,128,128]{2,1,0:T(8,128)(2,1)} %index_ref), custom_call_target="tpu_custom_call" | custom-call | flops 3221225472 | bytes 3145728 | tf_op jit(solution)/shard_map/negatives/pallas_call | solution.py:454
  35.7 5.0 %prep.1 = (s32[128,128]{1,0:T(8,128)S(1)}, f32[2048,128]{1,0:T(8,128)S(1)}) custom-call(s32[1]{0:T(128)} %bitcast.5.me_ref, bf16[8,560,128]{2,1,0:T(8,128)(2,1)S(1)} %all-to-all-done.told_ref.queries_ref), custom_call_target="tpu_custom_call" | custom-call | flops 16384 | bytes 16384 | tf_op jit(solution)/shard_map/prep/pallas_call | solution.py:164
  40.6 8.7 %load.1 = (bf16[512,128,128]{2,1,0:T(8,128)(2,1)S(1)}, bf16[512,128,128]{2,1,0:T(8,128)(2,1)S(1)}, f32[512,128]{1,0:T(8,128)S(1)}) custom-call(bf16[512,128,128]{2,1,0:T(8,128)(2,1)} %index_ref), custom_call_target="tpu_custom_call" | custom-call | flops 16777216 | bytes 16777216 | tf_op jit(solution)/shard_map/load/pallas_call | solution.py:82
  49.3 8.0 %pairs.4 = (bf16[1072,128]{1,0:T(8,128)(2,1)S(1)}, bf16[1072,128]{1,0:T(8,128)(2,1)S(1)}) custom-call(s32[2]{0:T(128)S(1)} %pad_add_fusion.1.source_ref, s32[128,128]{1,0:T(8,128)S(1)} %get-tuple-element.29.rows_ref, f32[2048,128]{1,0:T(8,128)S(1)} %get-tuple-element.30.target_ref, bf16[8,560,128]{2,1,0:T(8,128)(2,1)S(1)} %all-to-all-done.told_ref.queries_ref, ...), custom_call_target="tpu_custom_call" | custom-call | flops 1610612736 | bytes 16777216 | tf_op jit(solution)/shard_map/pairs/pallas_call | solution.py:330
  57.3 1.6 %collective-permute-start.3 = (bf16[1072,128]{1,0:T(8,128)(2,1)S(1)}, bf16[1072,128]{1,0:T(8,128)(2,1)S(1)}, u32[]{:S(2)}, u32[]{:S(2)}) collective-permute-start(bf16[1072,128]{1,0:T(8,128)(2,1)S(1)} %get-tuple-element.36), channel_id=1, source_target_pairs={{0,4},{4,8},{8,12},{12,16},{16,20},{20,24},{24,28},{28,0},{1,5},{5... | collective-permute-start | bytes 823304 | tf_op jit(solution)/shard_map/ppermute | solution.py:573
  58.9 4.7 %collective-permute-start.4 = (bf16[1072,128]{1,0:T(8,128)(2,1)S(1)}, bf16[1072,128]{1,0:T(8,128)(2,1)S(1)}, u32[]{:S(2)}, u32[]{:S(2)}) collective-permute-start(bf16[1072,128]{1,0:T(8,128)(2,1)S(1)} %get-tuple-element.37), channel_id=1, source_target_pairs={{0,8},{4,12},{8,16},{12,20},{16,24},{20,28},{24,0},{28,4},{1,9},{5... | collective-permute-start | bytes 823304 | tf_op jit(solution)/shard_map/ppermute | solution.py:573
  63.6 9.1 %pairs.5 = (bf16[1072,128]{1,0:T(8,128)(2,1)S(1)}, bf16[1072,128]{1,0:T(8,128)(2,1)S(1)}) custom-call(s32[2]{0:T(128)S(1)} %pad_add_fusion.2.source_ref, s32[128,128]{1,0:T(8,128)S(1)} %get-tuple-element.29.rows_ref, f32[2048,128]{1,0:T(8,128)S(1)} %get-tuple-element.30.target_ref, bf16[8,560,128]{2,1,0:T(8,128)(2,1)S(1)} %all-to-all-done.told_ref.queries_ref, ...), custom_call_target="tpu_custom_call" | custom-call | flops 1610612736 | bytes 16777216 | tf_op jit(solution)/shard_map/pairs/pallas_call | solution.py:330
  72.7 6.5 %collective-permute-start.5 = (bf16[1072,128]{1,0:T(8,128)(2,1)S(1)}, bf16[1072,128]{1,0:T(8,128)(2,1)S(1)}, u32[]{:S(2)}, u32[]{:S(2)}) collective-permute-start(bf16[1072,128]{1,0:T(8,128)(2,1)S(1)} %get-tuple-element.38), channel_id=1, source_target_pairs={{0,12},{4,16},{8,20},{12,24},{16,28},{20,0},{24,4},{28,8},{1,13},{... | collective-permute-start | bytes 823304 | tf_op jit(solution)/shard_map/ppermute | solution.py:573
  79.3 5.2 %collective-permute-start.6 = (bf16[1072,128]{1,0:T(8,128)(2,1)S(1)}, bf16[1072,128]{1,0:T(8,128)(2,1)S(1)}, u32[]{:S(2)}, u32[]{:S(2)}) collective-permute-start(bf16[1072,128]{1,0:T(8,128)(2,1)S(1)} %get-tuple-element.39), channel_id=1, source_target_pairs={{0,16},{4,20},{8,24},{12,28},{16,0},{20,4},{24,8},{28,12},{1,17},{... | collective-permute-start | bytes 823304 | tf_op jit(solution)/shard_map/ppermute | solution.py:573
  84.4 7.9 %pairs.6 = (bf16[1072,128]{1,0:T(8,128)(2,1)S(1)}, bf16[1072,128]{1,0:T(8,128)(2,1)S(1)}) custom-call(s32[2]{0:T(128)S(1)} %pad_add_fusion.3.source_ref, s32[128,128]{1,0:T(8,128)S(1)} %get-tuple-element.29.rows_ref, f32[2048,128]{1,0:T(8,128)S(1)} %get-tuple-element.30.target_ref, bf16[8,560,128]{2,1,0:T(8,128)(2,1)S(1)} %all-to-all-done.told_ref.queries_ref, ...), custom_call_target="tpu_custom_call" | custom-call | flops 1610612736 | bytes 16777216 | tf_op jit(solution)/shard_map/pairs/pallas_call | solution.py:330
  92.4 5.7 %collective-permute-start.7 = (bf16[1072,128]{1,0:T(8,128)(2,1)S(1)}, bf16[1072,128]{1,0:T(8,128)(2,1)S(1)}, u32[]{:S(2)}, u32[]{:S(2)}) collective-permute-start(bf16[1072,128]{1,0:T(8,128)(2,1)S(1)} %get-tuple-element.40), channel_id=1, source_target_pairs={{0,20},{4,24},{8,28},{12,0},{16,4},{20,8},{24,12},{28,16},{1,21},{... | collective-permute-start | bytes 823304 | tf_op jit(solution)/shard_map/ppermute | solution.py:573
  98.1 10.2 %pairs.7 = (bf16[1072,128]{1,0:T(8,128)(2,1)S(1)}, bf16[1072,128]{1,0:T(8,128)(2,1)S(1)}) custom-call(s32[2]{0:T(128)S(1)} %pad_add_fusion.4.source_ref, s32[128,128]{1,0:T(8,128)S(1)} %get-tuple-element.29.rows_ref, f32[2048,128]{1,0:T(8,128)S(1)} %get-tuple-element.30.target_ref, bf16[8,560,128]{2,1,0:T(8,128)(2,1)S(1)} %all-to-all-done.told_ref.queries_ref, ...), custom_call_target="tpu_custom_call" | custom-call | flops 1610612736 | bytes 16777216 | tf_op jit(solution)/shard_map/pairs/pallas_call | solution.py:330
  108.3 12.2 %collective-permute-start.8 = (bf16[1072,128]{1,0:T(8,128)(2,1)S(1)}, bf16[1072,128]{1,0:T(8,128)(2,1)S(1)}, u32[]{:S(2)}, u32[]{:S(2)}) collective-permute-start(bf16[1072,128]{1,0:T(8,128)(2,1)S(1)} %get-tuple-element.41), channel_id=1, source_target_pairs={{0,24},{4,28},{8,0},{12,4},{16,8},{20,12},{24,16},{28,20},{1,25},{... | collective-permute-start | bytes 823304 | tf_op jit(solution)/shard_map/ppermute | solution.py:573
  120.5 0.6 collective-permute-start.9
  121.1 6.0 %collective-permute-done.8.refs_5_ = bf16[1072,128]{1,0:T(8,128)(2,1)S(1)} collective-permute-done((bf16[1072,128]{1,0:T(8,128)(2,1)S(1)}, bf16[1072,128]{1,0:T(8,128)(2,1)S(1)}, u32[]{:S(2)}, u32[]{:S(2)}) %collective-permute-start.8) | collective-permute-done | bytes 274464 | tf_op jit(solution)/shard_map/ppermute | solution.py:573
  127.1 8.4 %collective-permute-done.9.refs_6_ = bf16[1072,128]{1,0:T(8,128)(2,1)S(1)} collective-permute-done((bf16[1072,128]{1,0:T(8,128)(2,1)S(1)}, bf16[1072,128]{1,0:T(8,128)(2,1)S(1)}, u32[]{:S(2)}, u32[]{:S(2)}) %collective-permute-start.9) | collective-permute-done | bytes 274464 | tf_op jit(solution)/shard_map/ppermute | solution.py:573
  135.6 2.0 %finish.1 = (f32[16,128]{1,0:T(8,128)S(1)}, f32[16,32,128]{2,1,0:T(8,128)}) custom-call(bf16[16,32,128]{2,1,0:T(8,128)(2,1)S(1)} %copy-done.1, f32[16,64]{1,0:T(8,128)S(1)} %copy-done.2, f32[512,128]{1,0:T(8,128)S(1)} %get-tuple-element.25.back_ref, f32[8,512]{1,0:T(8,128)S(1)} %get-tuple-element.26.sums_ref, ...), custom_call_target="tpu_custom_call" | custom-call | tf_op jit(solution)/shard_map/finish/pallas_call | solution.py:519
  137.6 0.6 slice_reduce_fusion
  (15 shorter events, 0.2 us)
Async XLA Ops:
  4.2 31.4 %all-to-all-start = ((bf16[8,560,128]{2,1,0:T(8,128)(2,1)}), bf16[8,560,128]{2,1,0:T(8,128)(2,1)S(1)}, u32[]{:S(2)}, u32[]{:S(2)}) async-start(bf16[8,560,128]{2,1,0:T(8,128)(2,1)} %broadcast_in_dim.2), calls=%async_computation | async-start | bytes 2293760 | tf_op jit(solution)/shard_map/all_to_all | solution.py:557
  10.4 3.3 %collective-permute-start.2 = (s32[1,24]{1,0:T(1,128)}, s32[1,24]{1,0:T(1,128)S(1)}, u32[]{:S(2)}, u32[]{:S(2)}) collective-permute-start(s32[1,24]{1,0:T(1,128)} %param.10), channel_id=1, source_target_pairs={{3,0},{0,1},{1,2},{2,3},{7,4},{4,5},{5,6},{6,7},{11,8},{8,9},{9,10... | collective-permute-start | bytes 296 | tf_op jit(solution)/shard_map/ppermute | solution.py:542
  10.4 3.7 %collective-permute-start.1 = (s32[1,24]{1,0:T(1,128)}, s32[1,24]{1,0:T(1,128)S(1)}, u32[]{:S(2)}, u32[]{:S(2)}) collective-permute-start(s32[1,24]{1,0:T(1,128)} %param.10), channel_id=1, source_target_pairs={{2,0},{3,1},{0,2},{1,3},{6,4},{7,5},{4,6},{5,7},{10,8},{11,9},{8,1... | collective-permute-start | bytes 296 | tf_op jit(solution)/shard_map/ppermute | solution.py:542
  11.9 2.9 %collective-permute-start = (s32[1,24]{1,0:T(1,128)}, s32[1,24]{1,0:T(1,128)S(1)}, u32[]{:S(2)}, u32[]{:S(2)}) collective-permute-start(s32[1,24]{1,0:T(1,128)} %param.10), channel_id=1, source_target_pairs={{1,0},{2,1},{3,2},{0,3},{5,4},{6,5},{7,6},{4,7},{9,8},{10,9},{11,1... | collective-permute-start | bytes 296 | tf_op jit(solution)/shard_map/ppermute | solution.py:542
  15.5 0.9 copy-start
  57.3 51.0 %collective-permute-start.3 = (bf16[1072,128]{1,0:T(8,128)(2,1)S(1)}, bf16[1072,128]{1,0:T(8,128)(2,1)S(1)}, u32[]{:S(2)}, u32[]{:S(2)}) collective-permute-start(bf16[1072,128]{1,0:T(8,128)(2,1)S(1)} %get-tuple-element.36), channel_id=1, source_target_pairs={{0,4},{4,8},{8,12},{12,16},{16,20},{20,24},{24,28},{28,0},{1,5},{5... | collective-permute-start | bytes 823304 | tf_op jit(solution)/shard_map/ppermute | solution.py:573
  58.9 61.6 %collective-permute-start.4 = (bf16[1072,128]{1,0:T(8,128)(2,1)S(1)}, bf16[1072,128]{1,0:T(8,128)(2,1)S(1)}, u32[]{:S(2)}, u32[]{:S(2)}) collective-permute-start(bf16[1072,128]{1,0:T(8,128)(2,1)S(1)} %get-tuple-element.37), channel_id=1, source_target_pairs={{0,8},{4,12},{8,16},{12,20},{16,24},{20,28},{24,0},{28,4},{1,9},{5... | collective-permute-start | bytes 823304 | tf_op jit(solution)/shard_map/ppermute | solution.py:573
  72.7 48.4 %collective-permute-start.5 = (bf16[1072,128]{1,0:T(8,128)(2,1)S(1)}, bf16[1072,128]{1,0:T(8,128)(2,1)S(1)}, u32[]{:S(2)}, u32[]{:S(2)}) collective-permute-start(bf16[1072,128]{1,0:T(8,128)(2,1)S(1)} %get-tuple-element.38), channel_id=1, source_target_pairs={{0,12},{4,16},{8,20},{12,24},{16,28},{20,0},{24,4},{28,8},{1,13},{... | collective-permute-start | bytes 823304 | tf_op jit(solution)/shard_map/ppermute | solution.py:573
  79.3 41.9 %collective-permute-start.6 = (bf16[1072,128]{1,0:T(8,128)(2,1)S(1)}, bf16[1072,128]{1,0:T(8,128)(2,1)S(1)}, u32[]{:S(2)}, u32[]{:S(2)}) collective-permute-start(bf16[1072,128]{1,0:T(8,128)(2,1)S(1)} %get-tuple-element.39), channel_id=1, source_target_pairs={{0,16},{4,20},{8,24},{12,28},{16,0},{20,4},{24,8},{28,12},{1,17},{... | collective-permute-start | bytes 823304 | tf_op jit(solution)/shard_map/ppermute | solution.py:573
  92.4 43.2 %copy-start.1 = (bf16[16,32,128]{2,1,0:T(8,128)(2,1)S(1)}, bf16[16,32,128]{2,1,0:T(8,128)(2,1)}, u32[]{:S(2)}) copy-start(bf16[16,32,128]{2,1,0:T(8,128)(2,1)} %queries_ref.1) | copy-start | bytes 393220
  92.4 43.2 %copy-start.2 = (f32[16,64]{1,0:T(8,128)S(1)}, f32[16,64]{1,0:T(8,128)}, u32[]{:S(2)}) copy-start(f32[16,64]{1,0:T(8,128)} %teacher_ref.1) | copy-start | bytes 12292
  92.4 28.7 %collective-permute-start.7 = (bf16[1072,128]{1,0:T(8,128)(2,1)S(1)}, bf16[1072,128]{1,0:T(8,128)(2,1)S(1)}, u32[]{:S(2)}, u32[]{:S(2)}) collective-permute-start(bf16[1072,128]{1,0:T(8,128)(2,1)S(1)} %get-tuple-element.40), channel_id=1, source_target_pairs={{0,20},{4,24},{8,28},{12,0},{16,4},{20,8},{24,12},{28,16},{1,21},{... | collective-permute-start | bytes 823304 | tf_op jit(solution)/shard_map/ppermute | solution.py:573
  108.3 18.8 %collective-permute-start.8 = (bf16[1072,128]{1,0:T(8,128)(2,1)S(1)}, bf16[1072,128]{1,0:T(8,128)(2,1)S(1)}, u32[]{:S(2)}, u32[]{:S(2)}) collective-permute-start(bf16[1072,128]{1,0:T(8,128)(2,1)S(1)} %get-tuple-element.41), channel_id=1, source_target_pairs={{0,24},{4,28},{8,0},{12,4},{16,8},{20,12},{24,16},{28,20},{1,25},{... | collective-permute-start | bytes 823304 | tf_op jit(solution)/shard_map/ppermute | solution.py:573
  120.5 15.1 %collective-permute-start.9 = (bf16[1072,128]{1,0:T(8,128)(2,1)S(1)}, bf16[1072,128]{1,0:T(8,128)(2,1)S(1)}, u32[]{:S(2)}, u32[]{:S(2)}) collective-permute-start(bf16[1072,128]{1,0:T(8,128)(2,1)S(1)} %get-tuple-element.42), channel_id=1, source_target_pairs={{0,28},{4,0},{8,4},{12,8},{16,12},{20,16},{24,20},{28,24},{1,29},{... | collective-permute-start | bytes 823304 | tf_op jit(solution)/shard_map/ppermute | solution.py:573

commit v8 on v7

--- a/solution.py
+++ b/solution.py
@@ -561,17 +561,17 @@
     index, told, rows = lax.optimization_barrier((index, told, rows))
     index, turned, inverse = load(index)
     messages = []
-    order = list(range(1, owners)) + [0]
+    order = list(reversed(range(owners)))
     groups = [order[first : first + SOURCES] for first in range(0, owners, SOURCES)]
     for steps in groups:
-        sources = [lax.rem(me + step, owners) for step in steps]
+        sources = [jnp.bitwise_xor(me, step) for step in steps]
         found = pairs(
             sources, rows, targets, told, count, tokens, inverse, index, turned, cands, room
         )
         for step, message in zip(steps, found):
             if step:
                 message = lax.ppermute(
-                    message, "corpus", [(i, (i + step) % owners) for i in range(owners)]
+                    message, "corpus", [(i, i ^ step) for i in range(owners)]
                 )
             messages.append(message)
     losses, query_grads = finish(queries, teacher, neg_acc, neg_sum, messages)

time: 138 us -> 134 us (0.971)
  Pallas kernels: 70.1 us -> 98.8 us
  starting transfers between devices: 45.6 us -> 18.1 us
  waiting for transfers between devices: 15.6 us -> 9.95 us
    pallas_call x4, Pallas kernels: 35.2 us -> 63.9 us  [pairs(): pl.pallas_call(functools.partial(pair_kernel, cands=cands, sources=len(so...]
    ppermute x7, starting transfers between devices: 36.5 us -> 9.05 us  [on_device(): lax.ppermute(message, 'corpus', [(i, i ^ step) for i in range(owners)])]
    ppermute x7, waiting for transfers between devices: 14.5 us -> 8.82 us  [on_device(): lax.ppermute(message, 'corpus', [(i, i ^ step) for i in range(owners)])]
  transfers between devices with their start and end apart: 11 -> 11, of which waited for: 4 -> 4; matrix products, arithmetic and copies ran while one was open for 1% -> 1% of each run, Pallas kernels for 34% -> 50%
where the time goes in v8:
time: 134 us
  Pallas kernels  98.8 us (74%)
  starting transfers between devices  18.1 us (14%)
  waiting for transfers between devices  9.95 us (7%)
  other arithmetic  3.39 us (3%)
  local copies, waits for them, and re-layouts  2.81 us (2%)
    pallas_call x4, Pallas kernels, pairs(): pl.pallas_call(functools.partial(pair_kernel, cands=cands, sources=len(so...  63.9 us
    pallas_call x1, Pallas kernels, negatives(): pl.pallas_call(functools.partial(neg_kernel, tokens=tokens), in_specs=[pl...  19.2 us
    ppermute x7, starting transfers between devices, on_device(): lax.ppermute(message, 'corpus', [(i, i ^ step) for i in range(owners)])  9.05 us
    ppermute x7, waiting for transfers between devices, on_device(): lax.ppermute(message, 'corpus', [(i, i ^ step) for i in range(owners)])  8.82 us
    pallas_call x1, Pallas kernels, load(): pl.pallas_call(load_shard, in_specs=[pl.BlockSpec(memory_space=pltpu.HBM)...  8.67 us
    all_to_all x1, starting transfers between devices, on_device(): lax.all_to_all(told, 'corpus', split_axis=0, concat_axis=0, tiled=True)  6.11 us
    pallas_call x1, Pallas kernels, prep(): pl.pallas_call(functools.partial(prep_kernel, shard=shard, cands=cands),...  4.96 us
    ppermute x3, starting transfers between devices, from_step(): lax.ppermute(value, axis, [((i + step) % size, i) for i in range(size)])  2.96 us
  transfers between devices with their start and end apart: 11, of which 4 were waited for; matrix products, arithmetic and copies ran while one was open for 1% of the time, Pallas kernels for 50%

profile of v8, /device:TPU:20, one launch (start us, length us, event | category | flops | bytes accessed | tf_op | source)
XLA Modules:
  0.0 133.8 jit_solution(5727623964287124432)
XLA Ops:
  0.6 0.7 reduce-precision_convert_fusion.1
  1.3 0.7 fusion.4
  2.1 1.0 fusion.1
  3.1 1.2 broadcast_in_dim.2
  4.2 6.1 %all-to-all-start = ((bf16[8,560,128]{2,1,0:T(8,128)(2,1)}), bf16[8,560,128]{2,1,0:T(8,128)(2,1)S(1)}, u32[]{:S(2)}, u32[]{:S(2)}) async-start(bf16[8,560,128]{2,1,0:T(8,128)(2,1)} %broadcast_in_dim.2), calls=%async_computation | async-start | bytes 2293760 | tf_op jit(solution)/shard_map/all_to_all | solution.py:557
  10.4 1.5 %collective-permute-start.1 = (s32[1,24]{1,0:T(1,128)}, s32[1,24]{1,0:T(1,128)S(1)}, u32[]{:S(2)}, u32[]{:S(2)}) collective-permute-start(s32[1,24]{1,0:T(1,128)} %param.10), channel_id=1, source_target_pairs={{2,0},{3,1},{0,2},{1,3},{6,4},{7,5},{4,6},{5,7},{10,8},{11,9},{8,1... | collective-permute-start | bytes 296 | tf_op jit(solution)/shard_map/ppermute | solution.py:542
  11.9 1.4 %collective-permute-start = (s32[1,24]{1,0:T(1,128)}, s32[1,24]{1,0:T(1,128)S(1)}, u32[]{:S(2)}, u32[]{:S(2)}) collective-permute-start(s32[1,24]{1,0:T(1,128)} %param.10), channel_id=1, source_target_pairs={{1,0},{2,1},{3,2},{0,3},{5,4},{6,5},{7,6},{4,7},{9,8},{10,9},{11,1... | collective-permute-start | bytes 296 | tf_op jit(solution)/shard_map/ppermute | solution.py:542
  13.3 0.1 pad_add_fusion.1.source_ref
  13.4 0.1 pad_add_fusion.2.source_ref
  13.5 0.1 pad_add_fusion.3.source_ref
  13.5 0.1 pad_add_fusion.4.source_ref
  13.6 0.4 collective-permute-done.1
  14.1 0.7 collective-permute-done
  14.7 0.7 pad_add_fusion
  15.4 0.1 reshape.18.rows_ref
  15.5 0.9 copy-done
  16.4 19.2 %negatives.1 = (f32[512,128]{1,0:T(8,128)S(1)}, f32[8,512]{1,0:T(8,128)S(1)}) custom-call(s32[96]{0:T(128)S(1)} %reshape.18.rows_ref, bf16[512,128]{1,0:T(8,128)(2,1)S(1)} %bitcast.17, bf16[512,128,128]{2,1,0:T(8,128)(2,1)} %index_ref), custom_call_target="tpu_custom_call" | custom-call | flops 3221225472 | bytes 3145728 | tf_op jit(solution)/shard_map/negatives/pallas_call | solution.py:454
  35.7 5.0 %prep.1 = (s32[128,128]{1,0:T(8,128)S(1)}, f32[2048,128]{1,0:T(8,128)S(1)}) custom-call(s32[1]{0:T(128)} %bitcast.5.me_ref, bf16[8,560,128]{2,1,0:T(8,128)(2,1)S(1)} %all-to-all-done.told_ref.queries_ref), custom_call_target="tpu_custom_call" | custom-call | flops 16384 | bytes 16384 | tf_op jit(solution)/shard_map/prep/pallas_call | solution.py:164
  40.6 8.7 %load.1 = (bf16[512,128,128]{2,1,0:T(8,128)(2,1)S(1)}, bf16[512,128,128]{2,1,0:T(8,128)(2,1)S(1)}, f32[512,128]{1,0:T(8,128)S(1)}) custom-call(bf16[512,128,128]{2,1,0:T(8,128)(2,1)} %index_ref), custom_call_target="tpu_custom_call" | custom-call | flops 16777216 | bytes 16777216 | tf_op jit(solution)/shard_map/load/pallas_call | solution.py:82
  49.3 16.0 %pairs.4 = (bf16[1072,128]{1,0:T(8,128)(2,1)S(1)}, bf16[1072,128]{1,0:T(8,128)(2,1)S(1)}) custom-call(s32[2]{0:T(128)S(1)} %pad_add_fusion.1.source_ref, s32[128,128]{1,0:T(8,128)S(1)} %get-tuple-element.29.rows_ref, f32[2048,128]{1,0:T(8,128)S(1)} %get-tuple-element.30.target_ref, bf16[8,560,128]{2,1,0:T(8,128)(2,1)S(1)} %all-to-all-done.told_ref.queries_ref, ...), custom_call_target="tpu_custom_call" | custom-call | flops 1610612736 | bytes 16777216 | tf_op jit(solution)/shard_map/pairs/pallas_call | solution.py:330
  65.4 3.2 %collective-permute-start.4 = (bf16[1072,128]{1,0:T(8,128)(2,1)S(1)}, bf16[1072,128]{1,0:T(8,128)(2,1)S(1)}, u32[]{:S(2)}, u32[]{:S(2)}) collective-permute-start(bf16[1072,128]{1,0:T(8,128)(2,1)S(1)} %get-tuple-element.37), channel_id=1, source_target_pairs={{0,24},{4,28},{8,16},{12,20},{16,8},{20,12},{24,0},{28,4},{1,25},{... | collective-permute-start | bytes 823304 | tf_op jit(solution)/shard_map/ppermute | solution.py:573
  68.5 14.8 %pairs.5 = (bf16[1072,128]{1,0:T(8,128)(2,1)S(1)}, bf16[1072,128]{1,0:T(8,128)(2,1)S(1)}) custom-call(s32[2]{0:T(128)S(1)} %pad_add_fusion.2.source_ref, s32[128,128]{1,0:T(8,128)S(1)} %get-tuple-element.29.rows_ref, f32[2048,128]{1,0:T(8,128)S(1)} %get-tuple-element.30.target_ref, bf16[8,560,128]{2,1,0:T(8,128)(2,1)S(1)} %all-to-all-done.told_ref.queries_ref, ...), custom_call_target="tpu_custom_call" | custom-call | flops 1610612736 | bytes 16777216 | tf_op jit(solution)/shard_map/pairs/pallas_call | solution.py:330
  83.4 0.1 collective-permute-start.5
  83.4 5.0 %collective-permute-start.6 = (bf16[1072,128]{1,0:T(8,128)(2,1)S(1)}, bf16[1072,128]{1,0:T(8,128)(2,1)S(1)}, u32[]{:S(2)}, u32[]{:S(2)}) collective-permute-start(bf16[1072,128]{1,0:T(8,128)(2,1)S(1)} %get-tuple-element.39), channel_id=1, source_target_pairs={{0,16},{4,20},{8,24},{12,28},{16,0},{20,4},{24,8},{28,12},{1,17},{... | collective-permute-start | bytes 823304 | tf_op jit(solution)/shard_map/ppermute | solution.py:573
  88.4 16.0 %pairs.6 = (bf16[1072,128]{1,0:T(8,128)(2,1)S(1)}, bf16[1072,128]{1,0:T(8,128)(2,1)S(1)}) custom-call(s32[2]{0:T(128)S(1)} %pad_add_fusion.3.source_ref, s32[128,128]{1,0:T(8,128)S(1)} %get-tuple-element.29.rows_ref, f32[2048,128]{1,0:T(8,128)S(1)} %get-tuple-element.30.target_ref, bf16[8,560,128]{2,1,0:T(8,128)(2,1)S(1)} %all-to-all-done.told_ref.queries_ref, ...), custom_call_target="tpu_custom_call" | custom-call | flops 1610612736 | bytes 16777216 | tf_op jit(solution)/shard_map/pairs/pallas_call | solution.py:330
  104.4 0.1 collective-permute-start.7
  104.5 17.1 %pairs.7 = (bf16[1072,128]{1,0:T(8,128)(2,1)S(1)}, bf16[1072,128]{1,0:T(8,128)(2,1)S(1)}) custom-call(s32[2]{0:T(128)S(1)} %pad_add_fusion.4.source_ref, s32[128,128]{1,0:T(8,128)S(1)} %get-tuple-element.29.rows_ref, f32[2048,128]{1,0:T(8,128)S(1)} %get-tuple-element.30.target_ref, bf16[8,560,128]{2,1,0:T(8,128)(2,1)S(1)} %all-to-all-done.told_ref.queries_ref, ...), custom_call_target="tpu_custom_call" | custom-call | flops 1610612736 | bytes 16777216 | tf_op jit(solution)/shard_map/pairs/pallas_call | solution.py:330
  121.8 0.6 collective-permute-start.9
  122.4 8.7 %collective-permute-done.8.refs_5_ = bf16[1072,128]{1,0:T(8,128)(2,1)S(1)} collective-permute-done((bf16[1072,128]{1,0:T(8,128)(2,1)S(1)}, bf16[1072,128]{1,0:T(8,128)(2,1)S(1)}, u32[]{:S(2)}, u32[]{:S(2)}) %collective-permute-start.8) | collective-permute-done | bytes 274464 | tf_op jit(solution)/shard_map/ppermute | solution.py:573
  131.1 0.1 collective-permute-done.9.refs_6_
  131.2 2.0 %finish.1 = (f32[16,128]{1,0:T(8,128)S(1)}, f32[16,32,128]{2,1,0:T(8,128)}) custom-call(bf16[16,32,128]{2,1,0:T(8,128)(2,1)S(1)} %copy-done.1, f32[16,64]{1,0:T(8,128)S(1)} %copy-done.2, f32[512,128]{1,0:T(8,128)S(1)} %get-tuple-element.25.back_ref, f32[8,512]{1,0:T(8,128)S(1)} %get-tuple-element.26.sums_ref, ...), custom_call_target="tpu_custom_call" | custom-call | tf_op jit(solution)/shard_map/finish/pallas_call | solution.py:519
  133.2 0.6 slice_reduce_fusion
  (15 shorter events, 0.2 us)
Async XLA Ops:
  4.2 31.4 %all-to-all-start = ((bf16[8,560,128]{2,1,0:T(8,128)(2,1)}), bf16[8,560,128]{2,1,0:T(8,128)(2,1)S(1)}, u32[]{:S(2)}, u32[]{:S(2)}) async-start(bf16[8,560,128]{2,1,0:T(8,128)(2,1)} %broadcast_in_dim.2), calls=%async_computation | async-start | bytes 2293760 | tf_op jit(solution)/shard_map/all_to_all | solution.py:557
  10.4 3.3 %collective-permute-start.2 = (s32[1,24]{1,0:T(1,128)}, s32[1,24]{1,0:T(1,128)S(1)}, u32[]{:S(2)}, u32[]{:S(2)}) collective-permute-start(s32[1,24]{1,0:T(1,128)} %param.10), channel_id=1, source_target_pairs={{3,0},{0,1},{1,2},{2,3},{7,4},{4,5},{5,6},{6,7},{11,8},{8,9},{9,10... | collective-permute-start | bytes 296 | tf_op jit(solution)/shard_map/ppermute | solution.py:542
  10.4 3.7 %collective-permute-start.1 = (s32[1,24]{1,0:T(1,128)}, s32[1,24]{1,0:T(1,128)S(1)}, u32[]{:S(2)}, u32[]{:S(2)}) collective-permute-start(s32[1,24]{1,0:T(1,128)} %param.10), channel_id=1, source_target_pairs={{2,0},{3,1},{0,2},{1,3},{6,4},{7,5},{4,6},{5,7},{10,8},{11,9},{8,1... | collective-permute-start | bytes 296 | tf_op jit(solution)/shard_map/ppermute | solution.py:542
  11.9 2.9 %collective-permute-start = (s32[1,24]{1,0:T(1,128)}, s32[1,24]{1,0:T(1,128)S(1)}, u32[]{:S(2)}, u32[]{:S(2)}) collective-permute-start(s32[1,24]{1,0:T(1,128)} %param.10), channel_id=1, source_target_pairs={{1,0},{2,1},{3,2},{0,3},{5,4},{6,5},{7,6},{4,7},{9,8},{10,9},{11,1... | collective-permute-start | bytes 296 | tf_op jit(solution)/shard_map/ppermute | solution.py:542
  15.5 0.9 copy-start
  65.3 56.4 %collective-permute-start.3 = (bf16[1072,128]{1,0:T(8,128)(2,1)S(1)}, bf16[1072,128]{1,0:T(8,128)(2,1)S(1)}, u32[]{:S(2)}, u32[]{:S(2)}) collective-permute-start(bf16[1072,128]{1,0:T(8,128)(2,1)S(1)} %get-tuple-element.36), channel_id=1, source_target_pairs={{0,28},{4,24},{8,20},{12,16},{16,12},{20,8},{24,4},{28,0},{1,29},{... | collective-permute-start | bytes 823304 | tf_op jit(solution)/shard_map/ppermute | solution.py:573
  65.4 56.4 %collective-permute-start.4 = (bf16[1072,128]{1,0:T(8,128)(2,1)S(1)}, bf16[1072,128]{1,0:T(8,128)(2,1)S(1)}, u32[]{:S(2)}, u32[]{:S(2)}) collective-permute-start(bf16[1072,128]{1,0:T(8,128)(2,1)S(1)} %get-tuple-element.37), channel_id=1, source_target_pairs={{0,24},{4,28},{8,16},{12,20},{16,8},{20,12},{24,0},{28,4},{1,25},{... | collective-permute-start | bytes 823304 | tf_op jit(solution)/shard_map/ppermute | solution.py:573
  83.4 39.0 %collective-permute-start.5 = (bf16[1072,128]{1,0:T(8,128)(2,1)S(1)}, bf16[1072,128]{1,0:T(8,128)(2,1)S(1)}, u32[]{:S(2)}, u32[]{:S(2)}) collective-permute-start(bf16[1072,128]{1,0:T(8,128)(2,1)S(1)} %get-tuple-element.38), channel_id=1, source_target_pairs={{0,20},{4,16},{8,28},{12,24},{16,4},{20,0},{24,12},{28,8},{1,21},{... | collective-permute-start | bytes 823304 | tf_op jit(solution)/shard_map/ppermute | solution.py:573
  83.4 38.9 %collective-permute-start.6 = (bf16[1072,128]{1,0:T(8,128)(2,1)S(1)}, bf16[1072,128]{1,0:T(8,128)(2,1)S(1)}, u32[]{:S(2)}, u32[]{:S(2)}) collective-permute-start(bf16[1072,128]{1,0:T(8,128)(2,1)S(1)} %get-tuple-element.39), channel_id=1, source_target_pairs={{0,16},{4,20},{8,24},{12,28},{16,0},{20,4},{24,8},{28,12},{1,17},{... | collective-permute-start | bytes 823304 | tf_op jit(solution)/shard_map/ppermute | solution.py:573
  104.4 26.8 %copy-start.1 = (bf16[16,32,128]{2,1,0:T(8,128)(2,1)S(1)}, bf16[16,32,128]{2,1,0:T(8,128)(2,1)}, u32[]{:S(2)}) copy-start(bf16[16,32,128]{2,1,0:T(8,128)(2,1)} %queries_ref.1) | copy-start | bytes 393220
  104.4 26.8 %copy-start.2 = (f32[16,64]{1,0:T(8,128)S(1)}, f32[16,64]{1,0:T(8,128)}, u32[]{:S(2)}) copy-start(f32[16,64]{1,0:T(8,128)} %teacher_ref.1) | copy-start | bytes 12292
  104.4 18.0 %collective-permute-start.7 = (bf16[1072,128]{1,0:T(8,128)(2,1)S(1)}, bf16[1072,128]{1,0:T(8,128)(2,1)S(1)}, u32[]{:S(2)}, u32[]{:S(2)}) collective-permute-start(bf16[1072,128]{1,0:T(8,128)(2,1)S(1)} %get-tuple-element.40), channel_id=1, source_target_pairs={{0,12},{4,8},{8,4},{12,0},{16,28},{20,24},{24,20},{28,16},{1,13},{... | collective-permute-start | bytes 823304 | tf_op jit(solution)/shard_map/ppermute | solution.py:573
  121.7 9.4 %collective-permute-start.8 = (bf16[1072,128]{1,0:T(8,128)(2,1)S(1)}, bf16[1072,128]{1,0:T(8,128)(2,1)S(1)}, u32[]{:S(2)}, u32[]{:S(2)}) collective-permute-start(bf16[1072,128]{1,0:T(8,128)(2,1)S(1)} %get-tuple-element.41), channel_id=1, source_target_pairs={{0,8},{4,12},{8,0},{12,4},{16,24},{20,28},{24,16},{28,20},{1,9},{5... | collective-permute-start | bytes 823304 | tf_op jit(solution)/shard_map/ppermute | solution.py:573
  121.8 9.4 %collective-permute-start.9 = (bf16[1072,128]{1,0:T(8,128)(2,1)S(1)}, bf16[1072,128]{1,0:T(8,128)(2,1)S(1)}, u32[]{:S(2)}, u32[]{:S(2)}) collective-permute-start(bf16[1072,128]{1,0:T(8,128)(2,1)S(1)} %get-tuple-element.42), channel_id=1, source_target_pairs={{0,4},{4,0},{8,12},{12,8},{16,20},{20,16},{24,28},{28,24},{1,5},{5... | collective-permute-start | bytes 823304 | tf_op jit(solution)/shard_map/ppermute | solution.py:573
